TPU v7x, 512 devices: a whole 4x8x8 slice. The times are simulated.
512 devices in a mesh: dp: 32 (over x, y), seq: 16 (over z, core).
Axes of the slice: x: 4, y: 8, z: 8, core: 2. Of those that a mesh axis runs over, the one named last changes fastest.
Arguments:
- encoder_timesteps: bfloat16 [8192, 16, 1536], P(('dp', 'seq')), may hold values from -10 to 10
- tile_parent_sequence: int32 [8192], P(('dp', 'seq')), may hold values from 0 to 15, as said below
- tile_recording_label: int32 [8192], P(('dp', 'seq')), may hold values from 0 to 3
- tile_valid_timesteps: int32 [8192], P(('dp', 'seq')), may hold values from 1 to 16, as said below
- standardize_scaling: float32 [1536], replicated, may hold values from 0.5 to 1.5
- triple_projector: bfloat16 [1536, 2304], P('dp'), may hold values from -0.15625 to 0.15625
- final_projector: bfloat16 [768, 1536], P('dp'), may hold values from -0.21875 to 0.21875
- lowered_maps: bfloat16 [2, 1536, 64], P(None, 'dp'), may hold values from -0.15625 to 0.15625
- raising_maps: bfloat16 [2, 64, 768], P(None, None, 'dp'), may hold values from -0.75 to 0.75
- focus_softness: float32 [8], replicated, may hold values from 2 to 12
- result_adjoint: bfloat16 [8192, 16, 1536], P(('dp', 'seq')), may hold values from -0.015625 to 0.015625
Outputs:
- block_out: bfloat16 [8192, 16, 1536], P(('dp', 'seq'))
- down_gradient: float32 [2, 1536, 64], P(None, 'dp')
- up_gradient: float32 [2, 64, 768], P(None, None, 'dp')
Inputs may be any that keep to these rules, and one draw needn't show every extreme that they name: `tile_parent_sequence`: at most 2 panels of one device go to one owner, and in every dp group one owner receives exactly 2 panels from every device of the group. `tile_valid_timesteps`: A clip is the set of panels of one dp group with the same tile_parent_sequence and tile_recording_label; every panel of a clip holds 16 frames except the clip's last panel in order of panel index.
All inputs are finite; a program needn't handle non-finite values.
Results may differ from a plain program's by a relative error of at most 0.028.
Values may be sent and summed in bfloat16 or wider, within the bound.
No kernel may reach another device: no remote copies, remote signals or barrier semaphores. Data moves between devices by JAX's collectives and lax.ppermute only.
A program may use at most 128 MiB of HBM per device.

v0:
```python
import jax
import jax.numpy as jnp
from jax import lax
from jax.sharding import PartitionSpec as P

EPS_NORM = 1e-05
EPS_HEAD = 1e-06


def layer_norm(encoder_timesteps, standardize_scaling):
    values = encoder_timesteps.astype(jnp.float32)
    centred = values - jnp.mean(values, axis=-1, keepdims=True)
    scaled = centred * lax.rsqrt(jnp.mean(centred * centred, axis=-1, keepdims=True) + EPS_NORM)
    return (scaled * standardize_scaling).astype(jnp.bfloat16)


def slot_matrix(tile_parent_sequence, slots_each, owner_count):
    panels_here = tile_parent_sequence.shape[0]
    owner_hits = (
        tile_parent_sequence[:, None] == jnp.arange(owner_count, dtype=jnp.int32)[None, :]
    ).astype(jnp.int32)
    earlier = (
        jnp.arange(panels_here, dtype=jnp.int32)[:, None]
        > jnp.arange(panels_here, dtype=jnp.int32)[None, :]
    ).astype(jnp.int32)
    before = jnp.dot(earlier, owner_hits)
    slot_rank = jnp.sum(before * owner_hits, axis=1)
    slot_place = tile_parent_sequence * slots_each + slot_rank
    return (
        slot_place[None, :] == jnp.arange(owner_count * slots_each, dtype=jnp.int32)[:, None]
    ).astype(jnp.bfloat16)


def apply_focus(
    asker_vectors, lookup_vectors, payload_vectors, timestep_labels, timestep_valid, focus_softness
):
    row_count = asker_vectors.shape[0]
    focus_number = focus_softness.shape[0]

    def divide_foci(array):
        return jnp.swapaxes(array.reshape(row_count, focus_number, -1), 0, 1)

    diagonal = jnp.arange(row_count)[:, None] == jnp.arange(row_count)[None, :]
    allowed = (timestep_labels[:, None] == timestep_labels[None, :]) & (
        timestep_valid[None, :] > 0.5
    ) | diagonal

    def single_focus(focus_elements):
        focus_askers, focus_lookups, focus_payloads, logit_softness = focus_elements
        broad_askers = focus_askers.astype(jnp.float32)
        key_wide = focus_lookups.astype(jnp.float32)
        normed_askers = broad_askers * lax.rsqrt(
            jnp.mean(broad_askers * broad_askers, axis=-1, keepdims=True) + EPS_HEAD
        )
        normed_lookups = key_wide * lax.rsqrt(
            jnp.mean(key_wide * key_wide, axis=-1, keepdims=True) + EPS_HEAD
        )
        focus_logits = lax.dot_general(
            normed_askers, normed_lookups, (((1,), (1,)), ((), ())), precision=lax.Precision.HIGHEST
        ) * (logit_softness / broad_askers.shape[-1])
        unnormed = jnp.where(allowed, jnp.exp(focus_logits), 0.0)
        weights = (unnormed / jnp.sum(unnormed, axis=-1, keepdims=True)).astype(jnp.bfloat16)
        return jnp.dot(weights, focus_payloads, preferred_element_type=jnp.float32)

    mixed_result = lax.map(
        single_focus,
        (
            divide_foci(asker_vectors),
            divide_foci(lookup_vectors),
            divide_foci(payload_vectors),
            focus_softness,
        ),
    )
    return jnp.swapaxes(mixed_result, 0, 1).reshape(row_count, -1)


def project(normalized_rows, triple_projector, down_full, full_up_matrix):
    base_proj = jnp.dot(
        normalized_rows,
        lax.all_gather(triple_projector, "dp", axis=0, tiled=True),
        preferred_element_type=jnp.float32,
    )
    rank_product = jnp.einsum(
        "eg,igp->iep", normalized_rows, down_full, preferred_element_type=jnp.float32
    ).astype(jnp.bfloat16)
    adapter_index = jnp.einsum(
        "dyj,djo->dyo", rank_product, full_up_matrix, preferred_element_type=jnp.float32
    )
    head_width = triple_projector.shape[1] // 3
    asker_vectors = (base_proj[:, :head_width] + adapter_index[0]).astype(jnp.bfloat16)
    lookup_vectors = base_proj[:, head_width : 2 * head_width].astype(jnp.bfloat16)
    payload_vectors = (base_proj[:, 2 * head_width :] + adapter_index[1]).astype(jnp.bfloat16)
    return (asker_vectors, lookup_vectors, payload_vectors, rank_product)


def to_owners(data, panel_info, select, owner_count, slots_each):
    packed = jnp.einsum("sp,pfw->sfw", select, data, preferred_element_type=jnp.float32).astype(
        data.dtype
    )
    packed_info = jnp.dot(select, panel_info, preferred_element_type=jnp.float32).astype(
        jnp.bfloat16
    )
    packed = packed.reshape((owner_count, slots_each) + packed.shape[1:])
    packed_info = packed_info.reshape(owner_count, slots_each, panel_info.shape[1])
    received, received_info = (
        lax.all_to_all(packed, "seq", split_axis=0, concat_axis=0, tiled=True),
        lax.all_to_all(packed_info, "seq", split_axis=0, concat_axis=0, tiled=True),
    )
    slot_total = owner_count * slots_each
    return (
        received.reshape((slot_total,) + data.shape[1:]),
        received_info.reshape(slot_total, panel_info.shape[1]),
    )


def send_grads(data, select, owner_count, slots_each):
    packed = jnp.einsum("sp,pfw->sfw", select, data, preferred_element_type=jnp.float32).astype(
        data.dtype
    )
    packed = packed.reshape((owner_count, slots_each) + data.shape[1:])
    received = lax.all_to_all(packed, "seq", split_axis=0, concat_axis=0, tiled=True)
    return received.reshape((owner_count * slots_each,) + data.shape[1:])


def to_sources(data, select, owner_count, slots_each):
    parts = data.reshape((owner_count, slots_each) + data.shape[1:])
    received = lax.all_to_all(parts, "seq", split_axis=0, concat_axis=0, tiled=True)
    received = received.reshape(data.shape)
    return jnp.einsum("sp,sfw->pfw", select, received, preferred_element_type=jnp.float32).astype(
        data.dtype
    )


def owner_rows(received_info, panel_len):
    timestep_labels = jnp.repeat(received_info[:, 0].astype(jnp.float32), panel_len)
    live_count = received_info[:, 1].astype(jnp.float32)
    positions = jnp.arange(panel_len, dtype=jnp.int32).astype(jnp.float32)
    timestep_valid = (positions[None, :] < live_count[:, None]).astype(jnp.float32).reshape(-1)
    return (timestep_labels, timestep_valid)


def adapter_gradients(
    normalized_rows, rank_product, query_gradient, value_gradient, full_up_matrix
):
    gradient_pairs = jnp.stack([query_gradient, value_gradient])
    up_gradient = jnp.einsum(
        "nfr,nfw->nrw", rank_product, gradient_pairs, preferred_element_type=jnp.float32
    )
    inner_gradient = jnp.einsum(
        "ydh,yih->ydi", gradient_pairs, full_up_matrix, preferred_element_type=jnp.float32
    ).astype(jnp.bfloat16)
    down_gradient = jnp.einsum(
        "fd,nfr->ndr", normalized_rows, inner_gradient, preferred_element_type=jnp.float32
    )
    return (down_gradient, up_gradient)


def on_device(
    encoder_timesteps,
    tile_parent_sequence,
    tile_recording_label,
    tile_valid_timesteps,
    standardize_scaling,
    triple_projector,
    final_projector,
    lowered_maps,
    raising_maps,
    focus_softness,
    result_adjoint,
):
    panels_here, panel_len, model_width = encoder_timesteps.shape
    owner_count = lax.axis_size("seq")
    slots_each = (panels_here + owner_count - 1) // owner_count + 1
    out_full, down_full, full_up_matrix = (
        lax.all_gather(final_projector, "dp", axis=0, tiled=True),
        lax.all_gather(lowered_maps, "dp", axis=1, tiled=True),
        lax.all_gather(raising_maps, "dp", axis=2, tiled=True),
    )
    select = slot_matrix(tile_parent_sequence, slots_each, owner_count)
    positions = jnp.arange(panel_len, dtype=jnp.int32)
    live_column = (
        (positions[None, :] < tile_valid_timesteps[:, None]).astype(jnp.bfloat16).reshape(-1, 1)
    )
    panel_info = jnp.stack([tile_recording_label, tile_valid_timesteps], axis=-1).astype(
        jnp.bfloat16
    )
    normalized_rows = layer_norm(encoder_timesteps, standardize_scaling).reshape(-1, model_width)
    asker_vectors, lookup_vectors, payload_vectors, rank_product = project(
        normalized_rows, triple_projector, down_full, full_up_matrix
    )
    head_width = asker_vectors.shape[1]
    joined = jnp.concatenate([asker_vectors, lookup_vectors, payload_vectors], axis=1).reshape(
        panels_here, panel_len, 3 * head_width
    )
    received, received_info = to_owners(joined, panel_info, select, owner_count, slots_each)
    owner_flat = received.reshape(-1, 3 * head_width)
    query_owner = owner_flat[:, :head_width]
    lookup_holder = owner_flat[:, head_width : 2 * head_width]
    value_owner = owner_flat[:, 2 * head_width :]
    timestep_labels, timestep_valid = owner_rows(received_info, panel_len)

    def run(asker_lowered, payload_lowered):
        return apply_focus(
            asker_lowered,
            lookup_holder,
            payload_lowered,
            timestep_labels,
            timestep_valid,
            focus_softness,
        )

    mixed_result, pullback = jax.vjp(run, query_owner, value_owner)
    context_back = to_sources(
        mixed_result.astype(jnp.bfloat16).reshape(-1, panel_len, head_width),
        select,
        owner_count,
        slots_each,
    )
    attn_out = jnp.dot(
        context_back.reshape(-1, head_width), out_full, preferred_element_type=jnp.float32
    )
    block_out = (
        encoder_timesteps.reshape(-1, model_width).astype(jnp.float32)
        + live_column.astype(jnp.float32) * attn_out
    ).astype(jnp.bfloat16)
    masked = result_adjoint.reshape(-1, model_width) * live_column
    d_context = jnp.einsum(
        "fd,wd->fw", masked, out_full, preferred_element_type=jnp.float32
    ).astype(jnp.bfloat16)
    received_grad = send_grads(
        d_context.reshape(panels_here, panel_len, head_width), select, owner_count, slots_each
    )
    query_gradient, value_gradient = pullback(
        received_grad.reshape(-1, head_width).astype(jnp.float32)
    )
    joined_grad = jnp.concatenate([query_gradient, value_gradient], axis=1).reshape(
        -1, panel_len, 2 * head_width
    )
    returned = to_sources(joined_grad, select, owner_count, slots_each).reshape(-1, 2 * head_width)
    down_gradient, up_gradient = adapter_gradients(
        normalized_rows,
        rank_product,
        returned[:, :head_width],
        returned[:, head_width:],
        full_up_matrix,
    )
    shard_down, shard_up = (
        lax.psum_scatter(
            down_gradient.astype(jnp.bfloat16), "dp", scatter_dimension=1, tiled=True
        ).astype(jnp.float32),
        lax.psum_scatter(
            up_gradient.astype(jnp.bfloat16), "dp", scatter_dimension=2, tiled=True
        ).astype(jnp.float32),
    )
    shard_down, shard_up = (
        lax.psum(shard_down.astype(jnp.bfloat16), "seq").astype(jnp.float32),
        lax.psum(shard_up.astype(jnp.bfloat16), "seq").astype(jnp.float32),
    )
    return (block_out.reshape(panels_here, panel_len, model_width), shard_down, shard_up)


def solution(mesh):
    in_specs = (
        P(("dp", "seq"), None, None),
        P(("dp", "seq")),
        P(("dp", "seq")),
        P(("dp", "seq")),
        P(),
        P("dp", None),
        P("dp", None),
        P(None, "dp", None),
        P(None, None, "dp"),
        P(),
        P(("dp", "seq"), None, None),
    )
    out_specs = (P(("dp", "seq"), None, None), P(None, "dp", None), P(None, None, "dp"))
    return jax.shard_map(
        on_device, mesh=mesh, in_specs=in_specs, out_specs=out_specs, check_vma=False
    )
```

profile of v0, /device:TPU:1, one launch (start us, length us, event | category | flops | bytes accessed | tf_op | source)
XLA Modules:
  0.0 702.1 jit_solution(10176296515647716277)
XLA Ops:
  11.8 11.8 %all-to-all-start.1 = ((bf16[16,2,2]{1,2,0:T(2,128)(2,1)}), bf16[16,2,2]{1,2,0:T(2,128)(2,1)S(1)}, u32[]{:S(2)}, u32[]{:S(2)}) async-start(bf16[16,2,2]{1,2,0:T(2,128)(2,1)} %copy.55), calls=%async_computation.1 | async-start | bytes 16384 | tf_op jit(solution)/shard_map/all_to_all | solution.py:107
  24.4 38.7 %all_gather.14 = bf16[2,64,768]{1,2,0:T(8,128)(2,1)S(1)} all-gather(bf16[2,64,24]{1,2,0:T(8,128)(2,1)} %param.23), channel_id=1, replica_groups=mesh['dp'=32,'seq'=16] {'dp'}, dimensions={2}, use_global_device_ids=true | all-gather | bytes 202752 | tf_op jit(solution)/shard_map/all_gather | solution.py:177
  63.1 37.9 %all_gather.13 = bf16[2,1536,64]{2,1,0:T(8,128)(2,1)S(1)} all-gather(bf16[2,48,64]{2,1,0:T(8,128)(2,1)} %param.22), channel_id=1, replica_groups=mesh['dp'=32,'seq'=16] {'dp'}, dimensions={1}, use_global_device_ids=true | all-gather | bytes 405504 | tf_op jit(solution)/shard_map/all_gather | solution.py:176
  108.9 26.2 %all-to-all-start.3 = ((bf16[16,2,16,768]{3,2,1,0:T(8,128)(2,1)}), bf16[16,2,16,768]{3,2,1,0:T(8,128)(2,1)}, u32[]{:S(2)}, u32[]{:S(2)}) async-start(bf16[16,2,16,768]{3,2,1,0:T(8,128)(2,1)} %bitcast.234), calls=%async_computation.3 | async-start | bytes 1572864 | tf_op jit(solution)/shard_map/all_to_all | solution.py:121
  135.2 63.1 %all-gather.3.cloned.1.call-done = bf16[1536,2304]{1,0:T(8,128)(2,1)} async-done(((bf16[48,2304]{1,0:T(8,128)(2,1)}), bf16[1536,2304]{1,0:T(8,128)(2,1)}) %all-gather.3.cloned.1.call-update) | async-done | bytes 7077904 | tf_op jit(solution)/shard_map/all_gather | solution.py:80
  198.2 5.0 fusion.91
  207.3 8.4 %all-to-all-start = ((bf16[16,2,16,2304]{3,2,1,0:T(8,128)(2,1)}), bf16[16,2,16,2304]{3,2,1,0:T(8,128)(2,1)S(1)}, u32[]{:S(2)}, u32[]{:S(2)}) async-start(bf16[16,2,16,2304]{3,2,1,0:T(8,128)(2,1)} %bitcast.224), calls=%async_computation | async-start | bytes 4718592 | tf_op jit(solution)/shard_map/all_to_all | solution.py:106
  219.3 50.8 %all-to-all-done = bf16[16,2,16,2304]{3,2,1,0:T(8,128)(2,1)S(1)} async-done(((bf16[16,2,16,2304]{3,2,1,0:T(8,128)(2,1)}), bf16[16,2,16,2304]{3,2,1,0:T(8,128)(2,1)S(1)}, u32[]{:S(2)}, u32[]{:S(2)}) %all-to-all-start) | async-done | bytes 2359328 | tf_op jit(solution)/shard_map/all_to_all | solution.py:106
  274.9 77.5 %while.49 = (s32[]{:T(128)}, bf16[8,512,96]{1,2,0:T(8,128)(2,1)}, f32[8,512,96]{1,2,0:T(8,128)}, f32[8,512,1]{1,2,0:T(1,128)S(1)}, f32[8,512,1]{1,2,0:T(1,128)S(...) while((s32[]{:T(128)}, bf16[8,512,96]{1,2,0:T(8,128)(2,1)}, ...), condition=%wide.region_7.8_spmd.clone, body=%wide.region_3.7_spmd.clone.sunk | while | flops 359729664 | bytes 9430757 | solution.py:65
  352.6 76.4 %while.50 = (s32[]{:T(128)}, bf16[8,512,96]{1,2,0:T(8,128)(2,1)S(1)}, bf16[8,512,96]{1,2,0:T(8,128)(2,1)S(1)}, f32[8,512,96]{2,0,1:T(8,128)}, bf16[8,512,96]{2,1...) while((s32[]{:T(128)}, ...), condition=%wide.region_11.12_spmd.clone, body=%wide.region_8.11_spmd.clone.sunk | while | flops 406667776 | bytes 5948117 | solution.py:65
  356.6 3.2 fusion.131
  366.2 3.2 fusion.131
  375.7 3.2 fusion.131
  385.3 3.2 fusion.131
  394.8 3.2 fusion.131
  404.4 3.2 fusion.131
  413.9 3.2 fusion.131
  433.6 5.3 all-to-all-start.4
  442.4 35.0 %all-to-all-done.4 = bf16[16,2,16,1536]{3,2,1,0:T(8,128)(2,1)S(1)} async-done(((bf16[16,2,16,1536]{3,2,1,0:T(8,128)(2,1)}), bf16[16,2,16,1536]{3,2,1,0:T(8,128)(2,1)S(1)}, u32[]{:S(2)}, u32[]{:S(2)}) %all-to-all-start.4) | async-done | bytes 1572896 | tf_op jit(solution)/shard_map/all_to_all | solution.py:127
  477.3 4.3 all-to-all-start.2
  493.8 10.4 %all-to-all-done.2 = bf16[16,2,16,768]{3,2,1,0:T(8,128)(2,1)S(1)} async-done(((bf16[16,2,16,768]{3,2,1,0:T(8,128)(2,1)}), bf16[16,2,16,768]{3,2,1,0:T(8,128)(2,1)S(1)}, u32[]{:S(2)}, u32[]{:S(2)}) %all-to-all-start.2) | async-done | bytes 786464 | tf_op jit(solution)/shard_map/all_to_all | solution.py:127
  504.8 3.3 fusion.61
  508.1 136.2 %all-reduce.6.cloned.1.call-done = (bf16[2,1536,64]{2,0,1:T(2,128)(2,1)}, bf16[2,64,768]{1,2,0:T(8,128)(2,1)}) async-done(((bf16[2,1536,64]{2,0,1:T(2,128)(2,1)}, bf16[2,64,768]{1,2,0:T(8,128)(2,1)}), (bf16[2,1536,64]{2,0,1:T(2,128)(2,1)}, bf16[2,64,768]{1,2,0:T(8,128)(2,1)})) %all-reduce.6.cloned.1.call-update) | async-done | bytes 589840
  645.8 48.5 %all-reduce.3 = (bf16[2,48,64]{2,0,1:T(2,128)(2,1)S(1)}, bf16[2,64,24]{1,2,0:T(8,128)(2,1)S(1)}) all-reduce(bf16[2,48,64]{2,0,1:T(2,128)(2,1)S(1)} %constant_dynamic-slice_fusion.8, bf16[2,64,24]{1,2,0:T(8,128)(2,1)S(1)} %constant_dynamic-slice_fusion.7), channel_id=1, replica_groups=mesh['dp'=32,'seq'=16] {'seq'}, use_global_device_ids=true, to_apply=%region_13.14 | all-reduce | flops 9216 | bytes 36864 | tf_op jit(solution)/shard_map/psum | solution.py:256
  (312 shorter events, 178.6 us)
Async XLA Ops:
  7.2 93.9 %copy-start = (bf16[16,16,1536]{2,1,0:T(8,128)(2,1)S(1)}, bf16[16,16,1536]{2,1,0:T(8,128)(2,1)}, u32[]{:S(2)}) copy-start(bf16[16,16,1536]{2,1,0:T(8,128)(2,1)} %param.15) | copy-start | bytes 2359300
  7.2 94.4 %copy-start.10 = (f32[1536]{0:T(1024)S(1)}, f32[1536]{0:T(1024)}, u32[]{:S(2)}) copy-start(f32[1536]{0:T(1024)} %param.19) | copy-start | bytes 18436
  7.2 97.2 %all-gather.5.cloned.1.call-start = ((), (), s32[]{:S(2)}) async-start(), calls=%async_computation.6 | async-start | bytes 2433024 | tf_op jit(solution)/shard_map/all_gather | solution.py:175
  7.9 190.3 %all-gather.3.cloned.1.call-start = ((), (), s32[]{:S(2)}) async-start(), calls=%async_computation.5 | async-start | bytes 7299072 | tf_op jit(solution)/shard_map/all_gather | solution.py:80
  11.8 97.2 %all-to-all-start.1 = ((bf16[16,2,2]{1,2,0:T(2,128)(2,1)}), bf16[16,2,2]{1,2,0:T(2,128)(2,1)S(1)}, u32[]{:S(2)}, u32[]{:S(2)}) async-start(bf16[16,2,2]{1,2,0:T(2,128)(2,1)} %copy.55), calls=%async_computation.1 | async-start | bytes 16384 | tf_op jit(solution)/shard_map/all_to_all | solution.py:107
  63.1 39.3 %copy-start.3 = (bf16[2,64,768]{1,2,0:T(8,128)(2,1)}, bf16[2,64,768]{1,2,0:T(8,128)(2,1)S(1)}, u32[]{:S(2)}) copy-start(bf16[2,64,768]{1,2,0:T(8,128)(2,1)S(1)} %all_gather.14) | copy-start | bytes 589828
  101.9 96.3 %copy-start.1 = (bf16[16,16,1536]{2,1,0:T(8,128)(2,1)}, bf16[16,16,1536]{2,1,0:T(8,128)(2,1)S(1)}, u32[]{:S(2)}) copy-start(bf16[16,16,1536]{2,1,0:T(8,128)(2,1)S(1)} %multiply_convert_fusion) | copy-start | bytes 2359300
  101.9 1.4 copy-start.7
  102.4 0.6 copy-start.8
  108.9 98.3 %all-to-all-start.3 = ((bf16[16,2,16,768]{3,2,1,0:T(8,128)(2,1)}), bf16[16,2,16,768]{3,2,1,0:T(8,128)(2,1)}, u32[]{:S(2)}, u32[]{:S(2)}) async-start(bf16[16,2,16,768]{3,2,1,0:T(8,128)(2,1)} %bitcast.234), calls=%async_computation.3 | async-start | bytes 1572864 | tf_op jit(solution)/shard_map/all_to_all | solution.py:121
  207.3 62.8 %all-to-all-start = ((bf16[16,2,16,2304]{3,2,1,0:T(8,128)(2,1)}), bf16[16,2,16,2304]{3,2,1,0:T(8,128)(2,1)S(1)}, u32[]{:S(2)}, u32[]{:S(2)}) async-start(bf16[16,2,16,2304]{3,2,1,0:T(8,128)(2,1)} %bitcast.224), calls=%async_computation | async-start | bytes 4718592 | tf_op jit(solution)/shard_map/all_to_all | solution.py:106
  271.5 2.8 copy-start.6
  273.0 1.6 copy-start.5
  273.0 1.9 copy-start.9
  433.6 43.7 %all-to-all-start.4 = ((bf16[16,2,16,1536]{3,2,1,0:T(8,128)(2,1)}), bf16[16,2,16,1536]{3,2,1,0:T(8,128)(2,1)S(1)}, u32[]{:S(2)}, u32[]{:S(2)}) async-start(bf16[16,2,16,1536]{3,2,1,0:T(8,128)(2,1)} %pad_maximum_fusion), calls=%async_computation.4 | async-start | bytes 3145728 | tf_op jit(solution)/shard_map/all_to_all | solution.py:127
  477.3 26.9 %all-to-all-start.2 = ((bf16[16,2,16,768]{3,2,1,0:T(8,128)(2,1)}), bf16[16,2,16,768]{3,2,1,0:T(8,128)(2,1)S(1)}, u32[]{:S(2)}, u32[]{:S(2)}) async-start(bf16[16,2,16,768]{3,2,1,0:T(8,128)(2,1)} %convert_element_type.217), calls=%async_computation.2 | async-start | bytes 1572864 | tf_op jit(solution)/shard_map/all_to_all | solution.py:127
  481.6 162.7 %all-reduce.6.cloned.1.call-start = ((), (), s32[]{:S(2)}) async-start(), calls=%async_computation.7 | async-start | bytes 2359296
  483.6 1.1 copy-start.2
  483.6 1.2 copy-start.4
Sparse Core Ops, SparseCore 0:
  11.2 86.2 all-gather.4
  100.6 97.5 all-gather.2
  491.4 152.8 all-reduce.5
where the time goes:
time: 706 us; the launch traced here: 702 us
  waiting for transfers between devices  297 us (42%)
  blocking collectives  125 us (18%)
  matrix products  101 us (14%)
  starting transfers between devices  56.4 us (8%)
  local copies, waits for them, and re-layouts  55.7 us (8%)
  other arithmetic  50.4 us (7%)
  between operations  15.5 us (2%)
    unnamed x4, waiting for transfers between devices  138 us
    all_gather x1, waiting for transfers between devices, project(): lax.all_gather(triple_projector, 'dp', axis=0, tiled=True)  63.1 us
    all_to_all x1, waiting for transfers between devices, to_owners(): lax.all_to_all(packed, 'seq', split_axis=0, concat_axis=0, tiled=True)  50.8 us
    psum x1, blocking collectives, on_device(): lax.psum(shard_down.astype(jnp.bfloat16), 'seq').astype(jnp.float32)  48.5 us
    all_to_all x2, waiting for transfers between devices, to_sources(): lax.all_to_all(parts, 'seq', split_axis=0, concat_axis=0, tiled=True)  45.4 us
    dynamic_update_slice x48, other arithmetic, apply_focus(): lax.map(single_focus, (divide_foci(asker_vectors), divide_foci(lookup_vec...  41.4 us
    dot_general x16, matrix products, single_focus(): lax.dot_general(normed_askers, normed_lookups, (((1,), (1,)), ((), ())),...  41.2 us
    dot_general x24, matrix products, single_focus(): return jnp.dot(weights, focus_payloads, preferred_element_type=jnp.float32)  40.2 us
  transfers between devices with their start and end apart: 8, of which 5 were waited for; matrix products, arithmetic and copies ran while one was open for 6% of the time, Pallas kernels for 0%

commit v1 on v0

v1 whole, which is shorter than its diff:
```python
import math

import jax
import jax.numpy as jnp
from jax import lax
from jax.experimental import pallas as pl
from jax.experimental.pallas import tpu as pltpu
from jax.sharding import PartitionSpec as P

EPS_NORM = 1e-05
EPS_HEAD = 1e-06
WIDE = 1536
PANELS = 16
LEN = 16
ROWS = PANELS * LEN
OWNERS = 16
SLOTS = 2
PACKED = OWNERS * SLOTS * LEN
HEAD = 96
FOCI = 4
HALF = FOCI * HEAD
RANK = 64
SHARDS = 32
BLOCK = WIDE // SHARDS
UPS = 2 * HALF // SHARDS
GRAD = 80
QKVL = 3 * HALF + 2 * RANK
F32 = jnp.float32
BF16 = jnp.bfloat16
SMEM = pltpu.MemorySpace.SMEM
VMEM = pltpu.MemorySpace.VMEM


def dot(a, b):
    return lax.dot_general(a, b, (((1,), (0,)), ((), ())), preferred_element_type=F32)


def dot_nt(a, b):
    return lax.dot_general(a, b, (((1,), (1,)), ((), ())), preferred_element_type=F32)


def slot_places(owner_ref):
    owners = [owner_ref[p] for p in range(PANELS)]
    places = []
    for p in range(PANELS):
        rank = jnp.int32(0)
        for q in range(p):
            rank = rank + jnp.where(owners[q] == owners[p], 1, 0)
        places.append(owners[p] * SLOTS + rank)
    return places


def spread(scalars, shape, axis):
    index = lax.broadcasted_iota(jnp.int32, shape, axis)
    panel = index // LEN
    values = jnp.zeros(shape, jnp.int32)
    for p in range(PANELS):
        values = jnp.where(panel == p, scalars[p], values)
    return values, index % LEN


def pack_kernel(owner_ref, live_ref, x_ref, adjoint_ref, gain_ref, normed_ref, masked_ref):
    place, step = spread(slot_places(owner_ref), (1, ROWS), 1)
    target = place * LEN + step
    slots = lax.broadcasted_iota(jnp.int32, (PACKED, ROWS), 0)
    select = jnp.where(slots == target, 1.0, 0.0).astype(BF16)
    values = x_ref[...].astype(F32)
    centred = values - jnp.mean(values, axis=-1, keepdims=True)
    scaled = centred * lax.rsqrt(jnp.mean(centred * centred, axis=-1, keepdims=True) + EPS_NORM)
    normed = (scaled * gain_ref[...]).astype(BF16)
    normed_ref[...] = dot(select, normed).astype(BF16).reshape(normed_ref.shape)
    lives, step = spread([live_ref[p] for p in range(PANELS)], (ROWS, 1), 0)
    masked = jnp.where(step < lives, adjoint_ref[...].astype(F32), 0.0).astype(BF16)
    masked_ref[...] = dot(select, masked).astype(BF16).reshape(masked_ref.shape)


def pack(owners, lives, x, adjoint, gain):
    packed = jax.ShapeDtypeStruct((OWNERS, SLOTS * LEN, WIDE), BF16)
    return pl.pallas_call(
        pack_kernel,
        out_shape=(packed, packed),
        in_specs=[pl.BlockSpec(memory_space=SMEM)] * 2 + [pl.BlockSpec(memory_space=VMEM)] * 3,
        out_specs=(pl.BlockSpec(memory_space=VMEM),) * 2,
        compiler_params=pltpu.CompilerParams(vmem_limit_bytes=40 << 20),
        cost_estimate=pl.CostEstimate(
            flops=4 * PACKED * ROWS * WIDE, bytes_accessed=6 * PACKED * WIDE, transcendentals=0
        ),
        name="pack",
    )(owners, lives, x, adjoint, gain)


def pad_rows(values, rows=128):
    return jnp.concatenate([values, jnp.zeros((rows - values.shape[0], values.shape[1]), values.dtype)], axis=0)


def focus_kernel(
    core_ref,
    soft_ref,
    normed_ref,
    masked_ref,
    tag_ref,
    code_ref,
    weight_ref,
    out_a_ref,
    out_b_ref,
    raise_ref,
    context_ref,
    grads_ref,
    base_s,
    query_s,
    key_s,
    value_s,
    cot_s,
    context_s,
    dquery_s,
    dvalue_s,
    down_s,
    up_s,
):
    owner = pl.program_id(0)
    core = core_ref[0]

    @pl.when(owner == 0)
    def _():
        down_s[...] = jnp.zeros_like(down_s)
        up_s[...] = jnp.zeros_like(up_s)

    @pl.loop(0, QKVL // 256)
    def _(n):
        columns = pl.ds(pl.multiple_of(n * 256, 256), 256)
        base_s[:, columns] = dot(normed_ref[...], weight_ref[:, columns])

    low = base_s[:, 3 * HALF :].astype(BF16)
    raising = raise_ref[...].astype(F32).T
    row = lax.broadcasted_iota(jnp.int32, raising.shape, 0)
    raise_q = jnp.where(row < RANK, raising, 0.0).astype(BF16)
    raise_v = jnp.where(row < RANK, 0.0, raising).astype(BF16)
    query = (base_s[:, :HALF] + dot(low, raise_q)).astype(BF16)
    query_s[...] = query.astype(F32).T
    key_s[...] = base_s[:, HALF : 2 * HALF].astype(BF16).astype(F32).T
    value = (base_s[:, 2 * HALF : 3 * HALF] + dot(low, raise_v)).astype(BF16)
    value_s[...] = value.astype(F32).T
    cot = dot_nt(out_a_ref[...], masked_ref[:, : WIDE // 2]) + dot_nt(
        out_b_ref[...], masked_ref[:, WIDE // 2 :]
    )
    cot_s[...] = cot.astype(BF16).astype(F32)

    rows_j = lax.broadcasted_iota(jnp.int32, (PACKED, PACKED), 0)
    rows_i = lax.broadcasted_iota(jnp.int32, (PACKED, PACKED), 1)
    allowed = (tag_ref[0:1, :] == code_ref[...]) | (rows_j == rows_i)
    ones_rows = jnp.where(lax.broadcasted_iota(jnp.int32, (32, PACKED), 0) < 2, 1.0, 0.0)
    sub = lax.broadcasted_iota(jnp.int32, (32, PACKED), 0)

    for h in range(FOCI):
        head = slice(h * HEAD, (h + 1) * HEAD)
        temper = soft_ref[core * FOCI + h] * (1.0 / HEAD)
        q = query_s[head, :]
        rq = lax.rsqrt(jnp.sum(q * q, axis=0, keepdims=True) * (1.0 / HEAD) + EPS_HEAD)
        qn = q * rq
        k = key_s[head, :]
        kn = k * lax.rsqrt(jnp.sum(k * k, axis=0, keepdims=True) * (1.0 / HEAD) + EPS_HEAD)
        kn = pad_rows(kn)
        qs = pad_rows(qn * (temper * math.log2(math.e))).astype(BF16)
        v = jnp.concatenate([value_s[head, :], ones_rows], axis=0)
        scores = dot(kn.T.astype(BF16), qs)
        unnormed = jnp.exp2(jnp.where(allowed, scores, -1e30)).astype(BF16)
        mixed = dot(v.astype(BF16), unnormed)
        inverse = 1.0 / mixed[HEAD : HEAD + 1, :]
        context = mixed[:HEAD, :] * inverse
        context_s[head, :] = context
        dc = (cot_s[head, :] * inverse).astype(BF16)
        shift = jnp.sum(dc.astype(F32) * context, axis=0, keepdims=True)
        shift_top = shift.astype(BF16).astype(F32)
        extra = jnp.where(sub == 0, -shift_top, jnp.where(sub == 1, shift_top - shift, 0.0))
        dc = jnp.concatenate([dc, extra.astype(BF16)], axis=0)
        inner = dot(v.T.astype(BF16), dc)
        dscores = (unnormed.astype(F32) * inner).astype(BF16)
        dqn = dot(kn.astype(BF16), dscores)[:HEAD, :] * temper
        dq = rq * (dqn - qn * (jnp.sum(qn * dqn, axis=0, keepdims=True) * (1.0 / HEAD)))
        dquery_s[head, :] = dq.astype(BF16)
        dv = dot_nt(unnormed, dc)
        dvalue_s[head, :] = dv.T[:HEAD, :].astype(BF16)

    context_ref[...] = context_s[...].T.astype(BF16).reshape(context_ref.shape)
    dquery = dquery_s[...]
    dvalue = dvalue_s[...]
    lane = lax.broadcasted_iota(jnp.int32, (HALF, 2 * RANK), 1)
    up_s[...] += jnp.where(lane < RANK, dot(dquery, low), dot(dvalue, low))
    inner_t = (dot(raise_q, dquery) + dot(raise_v, dvalue)).astype(BF16)
    down_s[...] += dot(inner_t, normed_ref[...])

    @pl.when(owner == 1)
    def _():
        grads_ref[...] = jnp.zeros_like(grads_ref)
        grads_ref[:, :BLOCK, :] = down_s[...].T.astype(BF16).reshape(SHARDS, BLOCK, 2 * RANK)
        for t in range(SHARDS // 2):
            part = pad_rows(up_s[t * UPS : (t + 1) * UPS, :], GRAD - BLOCK).astype(BF16)
            grads_ref[core * (SHARDS // 2) + t, BLOCK:, :] = part


def focus(core, soft, normed, masked, tags, codes, weights, out_a, out_b, raising):
    once = pl.Buffered(1)
    grid = pltpu.PrefetchScalarGridSpec(
        num_scalar_prefetch=1,
        grid=(2,),
        in_specs=[
            pl.BlockSpec(memory_space=SMEM),
            pl.BlockSpec((None, PACKED, WIDE), lambda o, c: (o, 0, 0)),
            pl.BlockSpec((None, PACKED, WIDE), lambda o, c: (o, 0, 0)),
            pl.BlockSpec((None, 8, PACKED), lambda o, c: (o, 0, 0)),
            pl.BlockSpec((None, PACKED, 1), lambda o, c: (o, 0, 0)),
            pl.BlockSpec((WIDE, QKVL), lambda o, c: (0, 0), pipeline_mode=once),
            pl.BlockSpec((HALF, WIDE // 2), lambda o, c: (c[0], 0), pipeline_mode=once),
            pl.BlockSpec((HALF, WIDE // 2), lambda o, c: (c[0], 0), pipeline_mode=once),
            pl.BlockSpec((HALF, 2 * RANK), lambda o, c: (c[0], 0), pipeline_mode=once),
        ],
        out_specs=[
            pl.BlockSpec((OWNERS, None, SLOTS * LEN, HALF), lambda o, c: (0, o, 0, 0)),
            pl.BlockSpec((SHARDS, GRAD, 2 * RANK), lambda o, c: (0, 0, 0)),
        ],
        scratch_shapes=[
            pltpu.VMEM((PACKED, QKVL), F32),
            pltpu.VMEM((HALF, PACKED), F32),
            pltpu.VMEM((HALF, PACKED), F32),
            pltpu.VMEM((HALF, PACKED), F32),
            pltpu.VMEM((HALF, PACKED), F32),
            pltpu.VMEM((HALF, PACKED), F32),
            pltpu.VMEM((HALF, PACKED), BF16),
            pltpu.VMEM((HALF, PACKED), BF16),
            pltpu.VMEM((2 * RANK, WIDE), F32),
            pltpu.VMEM((HALF, 2 * RANK), F32),
        ],
    )
    return pl.pallas_call(
        focus_kernel,
        grid_spec=grid,
        out_shape=(
            jax.ShapeDtypeStruct((OWNERS, 2, SLOTS * LEN, HALF), BF16),
            jax.ShapeDtypeStruct((SHARDS, GRAD, 2 * RANK), BF16),
        ),
        compiler_params=pltpu.CompilerParams(
            vmem_limit_bytes=56 << 20, dimension_semantics=("arbitrary",)
        ),
        cost_estimate=pl.CostEstimate(
            flops=12 << 30, bytes_accessed=16 << 20, transcendentals=2 * FOCI * PACKED * PACKED
        ),
        name="focus",
    )(core, soft, normed, masked, tags, codes, weights, out_a, out_b, raising)


def finish_kernel(owner_ref, live_ref, context_ref, x_ref, out_a_ref, out_b_ref, block_ref):
    place, step = spread(slot_places(owner_ref), (ROWS, 1), 0)
    target = place * LEN + step
    slots = lax.broadcasted_iota(jnp.int32, (ROWS, PACKED), 1)
    select = jnp.where(slots == target, 1.0, 0.0).astype(BF16)
    lives, _ = spread([live_ref[p] for p in range(PANELS)], (ROWS, 1), 0)
    halves = []
    for half in range(2):
        parts = []
        for o in range(OWNERS):
            source = o // 2 * 2 + half
            first = 0 if source == o else SLOTS * LEN
            parts.append(context_ref[source, first : first + SLOTS * LEN, :])
        halves.append(dot(select, jnp.concatenate(parts, axis=0)).astype(BF16))
    for side, ref in enumerate((out_a_ref, out_b_ref)):
        columns = slice(side * WIDE // 2, (side + 1) * WIDE // 2)
        attended = dot(halves[0], ref[:HALF, :]) + dot(halves[1], ref[HALF:, :])
        added = jnp.where(step < lives, attended, 0.0)
        block_ref[:, columns] = (x_ref[:, columns].astype(F32) + added).astype(BF16)


def finish(owners, lives, context, x, out_a, out_b):
    return pl.pallas_call(
        finish_kernel,
        out_shape=jax.ShapeDtypeStruct((ROWS, WIDE), BF16),
        in_specs=[pl.BlockSpec(memory_space=SMEM)] * 2 + [pl.BlockSpec(memory_space=VMEM)] * 4,
        out_specs=pl.BlockSpec(memory_space=VMEM),
        compiler_params=pltpu.CompilerParams(vmem_limit_bytes=40 << 20),
        cost_estimate=pl.CostEstimate(
            flops=2 * ROWS * 2 * HALF * (WIDE + PACKED), bytes_accessed=6 << 20, transcendentals=0
        ),
        name="finish",
    )(owners, lives, context, x, out_a, out_b)


def add_shards_kernel(part_ref, total_ref):
    total = part_ref[0].astype(F32)
    for t in range(1, SHARDS):
        total = total + part_ref[t].astype(F32)
    total = total.astype(BF16)
    for o in range(OWNERS):
        total_ref[o] = total


def add_shards(parts):
    return pl.pallas_call(
        add_shards_kernel,
        out_shape=jax.ShapeDtypeStruct((OWNERS, GRAD, 2 * RANK), BF16),
        in_specs=[pl.BlockSpec(memory_space=VMEM)],
        out_specs=pl.BlockSpec(memory_space=VMEM),
        name="add_shards",
    )(parts)


def add_owners_kernel(part_ref, down_ref, up_ref):
    total = part_ref[0].astype(F32)
    for o in range(1, OWNERS):
        total = total + part_ref[o].astype(F32)
    up = pad_rows(total[BLOCK : BLOCK + UPS, :]).T
    for n in range(2):
        down_ref[n] = total[:BLOCK, n * RANK : (n + 1) * RANK]
        up_ref[n] = up[n * RANK : (n + 1) * RANK, :UPS]


def add_owners(parts):
    return pl.pallas_call(
        add_owners_kernel,
        out_shape=(
            jax.ShapeDtypeStruct((2, BLOCK, RANK), F32),
            jax.ShapeDtypeStruct((2, RANK, UPS), F32),
        ),
        in_specs=[pl.BlockSpec(memory_space=VMEM)],
        out_specs=(pl.BlockSpec(memory_space=VMEM),) * 2,
        name="add_owners",
    )(parts)


def exchange(data, axis):
    return lax.all_to_all(data, axis, split_axis=0, concat_axis=0, tiled=True)


def swap_cores(data):
    pairs = [(s, s ^ 1) for s in range(OWNERS)]
    return lax.ppermute(data, "seq", pairs)


def panel_facts(owners, tags, lives):
    same = owners[:, None] == owners[None, :]
    order = jnp.arange(PANELS, dtype=jnp.int32)
    rank = jnp.sum((same & (order[:, None] > order[None, :])).astype(jnp.int32), axis=1)
    place = owners * SLOTS + rank
    hits = place[None, :] == jnp.arange(OWNERS * SLOTS, dtype=jnp.int32)[:, None]
    facts = [jnp.sum(jnp.where(hits, fact[None, :], 0), axis=1) for fact in (tags, lives)]
    sent = jnp.stack(facts, axis=-1).astype(BF16).reshape(OWNERS // 2, 2, SLOTS * 2)
    both = jnp.stack([sent, sent[:, ::-1]], axis=2).reshape(OWNERS, 2, SLOTS, 2)
    received = exchange(both, "seq").astype(F32)
    received = jnp.swapaxes(received, 0, 1).reshape(2, OWNERS * SLOTS, 1, 2)
    steps = jnp.arange(LEN, dtype=jnp.int32).astype(F32)[None, None, :]
    tag = jnp.broadcast_to(received[..., 0], (2, OWNERS * SLOTS, LEN))
    code = jnp.where(steps < received[..., 1], tag, -1.0)
    rows = jnp.broadcast_to(tag.reshape(2, 1, PACKED), (2, 8, PACKED))
    return rows, code.reshape(2, PACKED, 1)


def on_device(
    encoder_timesteps,
    tile_parent_sequence,
    tile_recording_label,
    tile_valid_timesteps,
    standardize_scaling,
    triple_projector,
    final_projector,
    lowered_maps,
    raising_maps,
    focus_softness,
    result_adjoint,
):
    core = lax.axis_index("seq") % 2
    starts = [n * 2 * HALF for n in range(3)]
    triple = [
        jnp.where(
            core == 0,
            triple_projector[:, first : first + HALF],
            triple_projector[:, first + HALF : first + 2 * HALF],
        )
        for first in starts
    ]
    lowered = jnp.concatenate([lowered_maps[0], lowered_maps[1]], axis=1)
    outward = jnp.concatenate([final_projector[:, : WIDE // 2], final_projector[:, WIDE // 2 :]], axis=0)
    raising = raising_maps.reshape(2 * RANK, UPS).T
    raising = jnp.concatenate([raising, jnp.zeros_like(raising)], axis=0)
    shard = jnp.concatenate([*triple, lowered, outward, raising], axis=1)
    whole = lax.all_gather(shard, "dp", axis=0, tiled=True)

    x = encoder_timesteps.reshape(ROWS, WIDE)
    normed, masked = pack(
        tile_parent_sequence,
        tile_valid_timesteps,
        x,
        result_adjoint.reshape(ROWS, WIDE),
        standardize_scaling.reshape(1, WIDE),
    )
    tag_rows, codes = panel_facts(tile_parent_sequence, tile_recording_label, tile_valid_timesteps)
    normed = exchange(normed, "seq")
    masked = exchange(masked, "seq")
    normed = jnp.stack([normed, swap_cores(normed)]).reshape(2, PACKED, WIDE)
    masked = jnp.stack([masked, swap_cores(masked)]).reshape(2, PACKED, WIDE)

    wide = whole.reshape(SHARDS, BLOCK, -1)
    outs = wide[:, :, QKVL : QKVL + WIDE // 2]
    out_a = outs[:, :UPS].reshape(2 * HALF, WIDE // 2)
    out_b = outs[:, UPS:].reshape(2 * HALF, WIDE // 2)
    raise_all = wide[:, :UPS, QKVL + WIDE // 2 :].reshape(2 * HALF, 2 * RANK)
    context, grads = focus(
        core.reshape(1),
        focus_softness,
        normed,
        masked,
        tag_rows,
        codes,
        whole,
        out_a,
        out_b,
        raise_all,
    )
    context = exchange(context.reshape(OWNERS, 2 * SLOTS * LEN, HALF), "seq")
    grads = exchange(add_shards(exchange(grads, "dp")), "seq")
    shard_down, shard_up = add_owners(grads)
    block_out = finish(tile_parent_sequence, tile_valid_timesteps, context, x, out_a, out_b)
    return block_out.reshape(encoder_timesteps.shape), shard_down, shard_up


def solution(mesh):
    in_specs = (
        P(("dp", "seq"), None, None),
        P(("dp", "seq")),
        P(("dp", "seq")),
        P(("dp", "seq")),
        P(),
        P("dp", None),
        P("dp", None),
        P(None, "dp", None),
        P(None, None, "dp"),
        P(),
        P(("dp", "seq"), None, None),
    )
    out_specs = (P(("dp", "seq"), None, None), P(None, "dp", None), P(None, None, "dp"))
    return jax.shard_map(
        on_device, mesh=mesh, in_specs=in_specs, out_specs=out_specs, check_vma=False
    )
```

time: 706 us -> 251 us (0.36)
  waiting for transfers between devices: 297 us -> 72.3 us
  matrix products: 101 us -> 0 us
  blocking collectives: 125 us -> 77.9 us
  other arithmetic: 50.4 us -> 10.2 us
  local copies, waits for them, and re-layouts: 55.7 us -> 20.4 us
  starting transfers between devices: 56.4 us -> 23.2 us
  Pallas kernels: 0 us -> 31.6 us
    unnamed x4 -> x1, waiting for transfers between devices: 138 us -> 0.02 us
    dot_general x53 -> x0, matrix products: 101 us -> none  [the longest x16 41.2 us: single_focus(): lax.dot_general(normed_askers, normed_lookups, (((1,), (1,)), ((), ())),...]
    all_to_all x0 -> x2, blocking collectives: none -> 77.9 us  [exchange(): return lax.all_to_all(data, axis, split_axis=0, concat_axis=0, tiled=True)]
    all_gather x2 -> x0, blocking collectives: 76.6 us -> none  [the longest x1 38.7 us: on_device(): lax.all_gather(raising_maps, 'dp', axis=2, tiled=True)]
    all_gather x2 -> x1, waiting for transfers between devices: 63.1 us -> 0.01 us  [on_device(): whole = lax.all_gather(shard, 'dp', axis=0, tiled=True)]
    psum x1 -> x0, blocking collectives: 48.5 us -> none  [on_device(): lax.psum(shard_down.astype(jnp.bfloat16), 'seq').astype(jnp.float32)]
    dynamic_update_slice x48 -> x0, other arithmetic: 41.4 us -> none  [apply_focus(): lax.map(single_focus, (divide_foci(asker_vectors), divide_foci(lookup_vec...]
    all_to_all x5 -> x4, starting transfers between devices: 56 us -> 19.4 us  [exchange(): return lax.all_to_all(data, axis, split_axis=0, concat_axis=0, tiled=True)]
  transfers between devices with their start and end apart: 8 -> 7, of which waited for: 5 -> 4; matrix products, arithmetic and copies ran while one was open for 6% -> 6% of each run, Pallas kernels for 0% -> 3%
where the time goes in v1:
time: 251 us; the launch traced here: 250 us
  blocking collectives  77.9 us (31%)
  waiting for transfers between devices  72.3 us (29%)
  Pallas kernels  31.6 us (13%)
  starting transfers between devices  23.2 us (9%)
  local copies, waits for them, and re-layouts  20.4 us (8%)
  between operations  14.2 us (6%)
  other arithmetic  10.2 us (4%)
    all_to_all x2, blocking collectives, exchange(): return lax.all_to_all(data, axis, split_axis=0, concat_axis=0, tiled=True)  77.9 us
    all_to_all x4, waiting for transfers between devices, exchange(): return lax.all_to_all(data, axis, split_axis=0, concat_axis=0, tiled=True)  72.3 us
    pallas_call x1, Pallas kernels, focus(): pl.pallas_call(focus_kernel, grid_spec=grid, out_shape=(jax.ShapeDtypeStr...  21.9 us
    all_to_all x4, starting transfers between devices, exchange(): return lax.all_to_all(data, axis, split_axis=0, concat_axis=0, tiled=True)  19.4 us
    unnamed x24, local copies, waits for them, and re-layouts  7.68 us
  transfers between devices with their start and end apart: 7, of which 4 were waited for; matrix products, arithmetic and copies ran while one was open for 6% of the time, Pallas kernels for 3%

profile of v1, /device:TPU:1, one launch (start us, length us, event | category | flops | bytes accessed | tf_op | source)
XLA Modules:
  0.0 249.8 jit_solution(4550176295849782536)
XLA Ops:
  12.0 1.1 copy-done.2
  15.5 3.2 %pack.1 = (bf16[16,32,1536]{2,1,0:T(8,128)(2,1)S(1)}, bf16[16,32,1536]{2,1,0:T(8,128)(2,1)}) custom-call(s32[16]{0:T(128)S(1)} %copy-done.6, s32[16]{0:T(128)S(1)} %copy-done.4, bf16[256,1536]{1,0:T(8,128)(2,1)S(1)} %bitcast.36, bf16[256,1536]{1,0:T(8,128)(2,1)S(1)} %bitcast.38, f32[1,1536]{1,0:T(1,128)S(1)} %reshape.160.gain_ref), custom_call_target="tpu_custom_call" | custom-call | flops 805306368 | bytes 4718592 | tf_op jit(solution)/shard_map/pack/pallas_call | solution.py:79
  18.7 51.4 %all_to_all.30 = bf16[16,32,1536]{2,1,0:T(8,128)(2,1)S(1)} all-to-all(bf16[16,32,1536]{2,1,0:T(8,128)(2,1)S(1)} %get-tuple-element.9), channel_id=1, replica_groups=mesh['dp'=32,'seq'=16] {'seq'}, dimensions={0} | all-to-all | bytes 3145728 | tf_op jit(solution)/shard_map/all_to_all | solution.py:329
  70.1 3.8 %all-to-all-start.1 = ((bf16[16,32,1536]{2,1,0:T(8,128)(2,1)}), bf16[16,32,1536]{2,1,0:T(8,128)(2,1)S(1)}, u32[]{:S(2)}, u32[]{:S(2)}) async-start(bf16[16,32,1536]{2,1,0:T(8,128)(2,1)} %get-tuple-element.10), calls=%async_computation.1 | async-start | bytes 3145728 | tf_op jit(solution)/shard_map/all_to_all | solution.py:329
  74.1 1.9 collective-permute-start
  76.2 35.5 %all-to-all-done.1 = bf16[16,32,1536]{2,1,0:T(8,128)(2,1)S(1)} async-done(((bf16[16,32,1536]{2,1,0:T(8,128)(2,1)}), bf16[16,32,1536]{2,1,0:T(8,128)(2,1)S(1)}, u32[]{:S(2)}, u32[]{:S(2)}) %all-to-all-start.1) | async-done | bytes 1572896 | tf_op jit(solution)/shard_map/all_to_all | solution.py:329
  111.6 1.9 collective-permute-start.1
  115.2 4.5 %all-to-all-start.2 = ((bf16[16,2,2,2]{2,3,1,0:T(2,128)(2,1)}), bf16[16,2,2,2]{2,3,1,0:T(2,128)(2,1)S(1)}, u32[]{:S(2)}, u32[]{:S(2)}) async-start(bf16[16,2,2,2]{2,3,1,0:T(2,128)(2,1)} %copy.40), calls=%async_computation.2 | async-start | bytes 32768 | tf_op jit(solution)/shard_map/all_to_all | solution.py:329
  119.8 7.2 %all-to-all-done.2 = bf16[16,2,2,2]{2,3,1,0:T(2,128)(2,1)S(1)} async-done(((bf16[16,2,2,2]{2,3,1,0:T(2,128)(2,1)}), bf16[16,2,2,2]{2,3,1,0:T(2,128)(2,1)S(1)}, u32[]{:S(2)}, u32[]{:S(2)}) %all-to-all-start.2) | async-done | bytes 288 | tf_op jit(solution)/shard_map/all_to_all | solution.py:329
  129.6 2.1 compare_select_fusion.code_ref
  131.7 3.4 %pad_maximum_fusion.normed_ref = bf16[2,512,1536]{2,1,0:T(8,128)(2,1)} fusion(bf16[1,512,1536]{2,1,0:T(8,128)(2,1)} %bitcast.4, bf16[1,512,1536]{2,1,0:T(8,128)(2,1)S(1)} %bitcast.40), kind=kLoop, calls=%fused_computation | loop fusion | flops 1572864 | bytes 6291456 | tf_op jit(solution)/shard_map/stack | solution.py:396
  135.1 3.4 %pad_maximum_fusion.1.masked_ref = bf16[2,512,1536]{2,1,0:T(8,128)(2,1)} fusion(bf16[1,512,1536]{2,1,0:T(8,128)(2,1)} %bitcast.6, bf16[1,512,1536]{2,1,0:T(8,128)(2,1)S(1)} %bitcast.39), kind=kLoop, calls=%fused_computation.1 | loop fusion | flops 1572864 | bytes 6291456 | tf_op jit(solution)/shard_map/stack | solution.py:397
  138.6 3.2 %fusion.1 = (bf16[32,24,768]{2,1,0:T(8,128)(2,1)}, bf16[32,24,768]{2,1,0:T(8,128)(2,1)}) fusion(bf16[32,48,2176]{2,1,0:T(8,128)(2,1)} %bitcast.41), kind=kLoop, calls=%fused_computation.22 | loop fusion | bytes 4718592 | tf_op jit(solution)/shard_map/slice | solution.py:402
  141.7 1.6 slice.67
  144.0 21.9 %focus.1 = (bf16[16,2,32,384]{3,2,1,0:T(8,128)(2,1)}, bf16[32,80,128]{2,1,0:T(8,128)(2,1)}) custom-call(s32[1]{0:T(128)} %bitcast.core_ref, f32[8]{0:T(128)} %soft_ref.1, bf16[2,512,1536]{2,1,0:T(8,128)(2,1)} %pad_maximum_fusion.normed_ref, bf16[2,512,1536]{2,1,0:T(8,128)(2,1)} %pad_maximum_fusion.1.masked_ref, f32[2,8,512]{2,1,0:T(8,128)} %broadcast_in_dim.54.tag_ref, ...), custom_call_target="tpu_custom_call" | custom-call | flops 12884901888 | bytes 16777216 | tf_op jit(solution)/shard_map/focus/pallas_call | solution.py:234
  165.9 26.5 %all_to_all.31.part_ref = bf16[32,80,128]{2,1,0:T(8,128)(2,1)} all-to-all(bf16[32,80,128]{2,1,0:T(8,128)(2,1)} %get-tuple-element.12), channel_id=1, replica_groups=mesh['dp'=32,'seq'=16] {'dp'}, dimensions={0} | all-to-all | bytes 1310720 | tf_op jit(solution)/shard_map/all_to_all | solution.py:329
  192.4 7.6 %all-to-all-start.3 = ((bf16[16,64,384]{2,1,0:T(8,128)(2,1)}), bf16[16,64,384]{2,1,0:T(8,128)(2,1)S(1)}, u32[]{:S(2)}, u32[]{:S(2)}) async-start(bf16[16,64,384]{2,1,0:T(8,128)(2,1)} %bitcast.44), calls=%async_computation.3 | async-start | bytes 1572864 | tf_op jit(solution)/shard_map/all_to_all | solution.py:329
  200.1 1.9 add_shards.1
  202.0 20.8 %all-to-all-done.3.context_ref = bf16[16,64,384]{2,1,0:T(8,128)(2,1)S(1)} async-done(((bf16[16,64,384]{2,1,0:T(8,128)(2,1)}), bf16[16,64,384]{2,1,0:T(8,128)(2,1)S(1)}, u32[]{:S(2)}, u32[]{:S(2)}) %all-to-all-start.3) | async-done | bytes 786464 | tf_op jit(solution)/shard_map/all_to_all | solution.py:329
  222.8 3.4 %all-to-all-start.5 = ((bf16[16,80,128]{2,1,0:T(8,128)(2,1)}), bf16[16,80,128]{2,1,0:T(8,128)(2,1)S(1)}, u32[]{:S(2)}, u32[]{:S(2)}) async-start(bf16[16,80,128]{2,1,0:T(8,128)(2,1)} %add_shards.1), calls=%async_computation.5 | async-start | bytes 655360 | tf_op jit(solution)/shard_map/all_to_all | solution.py:329
  227.4 2.9 %finish.1 = bf16[256,1536]{1,0:T(8,128)(2,1)} custom-call(s32[16]{0:T(128)S(1)} %copy-done.7, s32[16]{0:T(128)S(1)} %copy-done.5, bf16[16,64,384]{2,1,0:T(8,128)(2,1)S(1)} %all-to-all-done.3.context_ref, bf16[256,1536]{1,0:T(8,128)(2,1)S(1)} %bitcast.37, bf16[768,768]{1,0:T(8,128)(2,1)S(1)} %bitcast.35, bf16[768,768]{1,0:T(8,128)(2,1)S(1)} %bitcast.33), custom_call_target="tpu_custom_call" | custom-call | flops 805306368 | bytes 6291456 | tf_op jit(solution)/shard_map/finish/pallas_call | solution.py:273
  230.3 8.7 %all-to-all-done.5.part_ref = bf16[16,80,128]{2,1,0:T(8,128)(2,1)S(1)} async-done(((bf16[16,80,128]{2,1,0:T(8,128)(2,1)}), bf16[16,80,128]{2,1,0:T(8,128)(2,1)S(1)}, u32[]{:S(2)}, u32[]{:S(2)}) %all-to-all-start.5) | async-done | bytes 327712 | tf_op jit(solution)/shard_map/all_to_all | solution.py:329
  239.8 1.7 add_owners.1
  241.5 1.5 copy.45
  (64 shorter events, 14.2 us)
Async XLA Ops:
  7.2 131.4 %all-gather.2.cloned.1.call-start = ((), (), s32[]{:S(2)}) async-start(), calls=%async_computation.6 | async-start | bytes 6893568 | tf_op jit(solution)/shard_map/all_gather | solution.py:383
  12.0 1.1 copy-start.2
  13.1 0.7 copy-start.4
  13.8 0.7 copy-start.6
  14.4 1.1 copy-start.8
  70.1 3.8 %copy-start.7 = (s32[16]{0:T(128)S(1)}, s32[16]{0:T(128)}, u32[]{:S(2)}) copy-start(s32[16]{0:T(128)} %owner_ref.3) | copy-start | bytes 196
  70.1 5.9 %copy-start.5 = (s32[16]{0:T(128)S(1)}, s32[16]{0:T(128)}, u32[]{:S(2)}) copy-start(s32[16]{0:T(128)} %live_ref.3) | copy-start | bytes 196
  70.1 5.9 %copy-start.10 = (s32[16]{0:T(128)S(1)}, s32[16]{0:T(128)}, u32[]{:S(2)}) copy-start(s32[16]{0:T(128)} %param.13) | copy-start | bytes 196
  70.1 41.5 %all-to-all-start.1 = ((bf16[16,32,1536]{2,1,0:T(8,128)(2,1)}), bf16[16,32,1536]{2,1,0:T(8,128)(2,1)S(1)}, u32[]{:S(2)}, u32[]{:S(2)}) async-start(bf16[16,32,1536]{2,1,0:T(8,128)(2,1)} %get-tuple-element.10), calls=%async_computation.1 | async-start | bytes 3145728 | tf_op jit(solution)/shard_map/all_to_all | solution.py:329
  74.1 57.6 %collective-permute-start = (bf16[16,32,1536]{2,1,0:T(8,128)(2,1)S(1)}, bf16[16,32,1536]{2,1,0:T(8,128)(2,1)}, u32[]{:S(2)}, u32[]{:S(2)}) collective-permute-start(bf16[16,32,1536]{2,1,0:T(8,128)(2,1)S(1)} %all_to_all.30), channel_id=1, source_target_pairs={{0,1},{1,0},{2,3},{3,2},{4,5},{5,4},{6,7},{7,6},{8,9},{9,8},{10,11... | collective-permute-start | bytes 4718600 | tf_op jit(solution)/shard_map/ppermute | solution.py:334
  111.6 23.5 %collective-permute-start.1 = (bf16[16,32,1536]{2,1,0:T(8,128)(2,1)S(1)}, bf16[16,32,1536]{2,1,0:T(8,128)(2,1)}, u32[]{:S(2)}, u32[]{:S(2)}) collective-permute-start(bf16[16,32,1536]{2,1,0:T(8,128)(2,1)S(1)} %all-to-all-done.1), channel_id=1, source_target_pairs={{0,1},{1,0},{2,3},{3,2},{4,5},{5,4},{6,7},{7,6},{8,9},{9,8},{10,11... | collective-permute-start | bytes 4718600 | tf_op jit(solution)/shard_map/ppermute | solution.py:334
  115.2 11.8 %all-to-all-start.2 = ((bf16[16,2,2,2]{2,3,1,0:T(2,128)(2,1)}), bf16[16,2,2,2]{2,3,1,0:T(2,128)(2,1)S(1)}, u32[]{:S(2)}, u32[]{:S(2)}) async-start(bf16[16,2,2,2]{2,3,1,0:T(2,128)(2,1)} %copy.40), calls=%async_computation.2 | async-start | bytes 32768 | tf_op jit(solution)/shard_map/all_to_all | solution.py:329
  192.4 33.8 %copy-start = (bf16[32,24,768]{2,1,0:T(8,128)(2,1)S(1)}, bf16[32,24,768]{2,1,0:T(8,128)(2,1)}, u32[]{:S(2)}) copy-start(bf16[32,24,768]{2,1,0:T(8,128)(2,1)} %get-tuple-element.29) | copy-start | bytes 3538948
  192.4 33.8 %copy-start.1 = (bf16[32,24,768]{2,1,0:T(8,128)(2,1)S(1)}, bf16[32,24,768]{2,1,0:T(8,128)(2,1)}, u32[]{:S(2)}) copy-start(bf16[32,24,768]{2,1,0:T(8,128)(2,1)} %get-tuple-element.30) | copy-start | bytes 3538948
  192.4 30.4 %all-to-all-start.3 = ((bf16[16,64,384]{2,1,0:T(8,128)(2,1)}), bf16[16,64,384]{2,1,0:T(8,128)(2,1)S(1)}, u32[]{:S(2)}, u32[]{:S(2)}) async-start(bf16[16,64,384]{2,1,0:T(8,128)(2,1)} %bitcast.44), calls=%async_computation.3 | async-start | bytes 1572864 | tf_op jit(solution)/shard_map/all_to_all | solution.py:329
  222.8 16.2 %all-to-all-start.5 = ((bf16[16,80,128]{2,1,0:T(8,128)(2,1)}), bf16[16,80,128]{2,1,0:T(8,128)(2,1)S(1)}, u32[]{:S(2)}, u32[]{:S(2)}) async-start(bf16[16,80,128]{2,1,0:T(8,128)(2,1)} %add_shards.1), calls=%async_computation.5 | async-start | bytes 655360 | tf_op jit(solution)/shard_map/all_to_all | solution.py:329
  226.3 1.1 copy-start.3
  239.0 0.7 copy-start.9
Sparse Core Ops, SparseCore 0:
  11.4 100.3 all-gather.1

commit v2 on v1

v2 whole, which is shorter than its diff:
```python
import math

import jax
import jax.numpy as jnp
from jax import lax
from jax.experimental import pallas as pl
from jax.experimental.pallas import tpu as pltpu
from jax.sharding import PartitionSpec as P

EPS_NORM = 1e-05
EPS_HEAD = 1e-06
WIDE = 1536
PANELS = 16
LEN = 16
ROWS = PANELS * LEN
OWNERS = 16
SLOTS = 2
PACKED = OWNERS * SLOTS * LEN
HEAD = 96
FOCI = 4
HALF = FOCI * HEAD
RANK = 64
SHARDS = 32
BLOCK = WIDE // SHARDS
UPS = 2 * HALF // SHARDS
GRAD = 2 * UPS
HIDDEN = 2 * HALF
QKVL = 3 * HALF + 2 * RANK
F32 = jnp.float32
BF16 = jnp.bfloat16
SMEM = pltpu.MemorySpace.SMEM
VMEM = pltpu.MemorySpace.VMEM


def dot(a, b):
    return lax.dot_general(a, b, (((1,), (0,)), ((), ())), preferred_element_type=F32)


def dot_nt(a, b):
    return lax.dot_general(a, b, (((1,), (1,)), ((), ())), preferred_element_type=F32)


def slot_places(owner_ref):
    owners = [owner_ref[p] for p in range(PANELS)]
    places = []
    for p in range(PANELS):
        rank = jnp.int32(0)
        for q in range(p):
            rank = rank + jnp.where(owners[q] == owners[p], 1, 0)
        places.append(owners[p] * SLOTS + rank)
    return places


def spread(scalars, shape, axis):
    index = lax.broadcasted_iota(jnp.int32, shape, axis)
    panel = index // LEN
    values = jnp.zeros(shape, jnp.int32)
    for p in range(PANELS):
        values = jnp.where(panel == p, scalars[p], values)
    return values, index % LEN


def pack_kernel(owner_ref, live_ref, x_ref, adjoint_ref, gain_ref, normed_ref, masked_ref):
    place, step = spread(slot_places(owner_ref), (1, ROWS), 1)
    target = place * LEN + step
    slots = lax.broadcasted_iota(jnp.int32, (PACKED, ROWS), 0)
    select = jnp.where(slots == target, 1.0, 0.0).astype(BF16)
    values = x_ref[...].astype(F32)
    centred = values - jnp.mean(values, axis=-1, keepdims=True)
    scaled = centred * lax.rsqrt(jnp.mean(centred * centred, axis=-1, keepdims=True) + EPS_NORM)
    normed = (scaled * gain_ref[...]).astype(BF16)
    normed_ref[...] = dot(select, normed).astype(BF16).reshape(normed_ref.shape)
    lives, step = spread([live_ref[p] for p in range(PANELS)], (ROWS, 1), 0)
    masked = jnp.where(step < lives, adjoint_ref[...].astype(F32), 0.0).astype(BF16)
    masked_ref[...] = dot(select, masked).astype(BF16).reshape(masked_ref.shape)


def pack(owners, lives, x, adjoint, gain):
    packed = jax.ShapeDtypeStruct((OWNERS, SLOTS * LEN, WIDE), BF16)
    return pl.pallas_call(
        pack_kernel,
        out_shape=(packed, packed),
        in_specs=[pl.BlockSpec(memory_space=SMEM)] * 2 + [pl.BlockSpec(memory_space=VMEM)] * 3,
        out_specs=(pl.BlockSpec(memory_space=VMEM),) * 2,
        compiler_params=pltpu.CompilerParams(vmem_limit_bytes=40 << 20),
        cost_estimate=pl.CostEstimate(
            flops=4 * PACKED * ROWS * WIDE, bytes_accessed=6 * PACKED * WIDE, transcendentals=0
        ),
        name="pack",
    )(owners, lives, x, adjoint, gain)


def pad_rows(values, rows=128):
    return jnp.concatenate([values, jnp.zeros((rows - values.shape[0], values.shape[1]), values.dtype)], axis=0)


def owner_copies(sources, landing, sems):
    return [pltpu.make_async_copy(source, landing.at[o], sems.at[o]) for o, source in enumerate(sources)]


def raising_of(raise_s):
    tall = raise_s[...].astype(F32).reshape(SHARDS // 2, BLOCK, 2 * RANK)[:, :UPS]
    raising = tall.reshape(HALF, 2 * RANK).T
    row = lax.broadcasted_iota(jnp.int32, raising.shape, 0)
    raise_q = jnp.where(row < RANK, raising, 0.0).astype(BF16)
    raise_v = jnp.where(row < RANK, 0.0, raising).astype(BF16)
    return raise_q, raise_v


def unit(values):
    scale = lax.rsqrt(jnp.sum(values * values, axis=0, keepdims=True) * (1.0 / HEAD) + EPS_HEAD)
    return values * scale, scale


def forward_kernel(
    core_ref,
    soft_ref,
    tag_ref,
    code_ref,
    mine_ref,
    other_ref,
    whole_ref,
    context_ref,
    weights_ref,
    qkv_ref,
    low_ref,
    mixed_ref,
    inverse_ref,
    normed_s,
    weight_s,
    raise_s,
    base_s,
    row_sems,
    weight_sems,
    raise_sem,
):
    owner = pl.program_id(0)
    core = core_ref[0]
    rows = owner_copies((mine_ref, other_ref), normed_s, row_sems)
    tiles = [
        pltpu.make_async_copy(
            whole_ref.at[:, pl.ds(HIDDEN + n * 256, 256)],
            weight_s.at[:, pl.ds(n * 256, 256)],
            weight_sems.at[n],
        )
        for n in range(QKVL // 256)
    ]
    half = pl.ds(pl.multiple_of(core * (WIDE // 2), WIDE // 2), WIDE // 2)
    raises = pltpu.make_async_copy(
        whole_ref.at[half, pl.ds(HIDDEN + QKVL, 2 * RANK)], raise_s, raise_sem
    )

    @pl.when(owner == 0)
    def _():
        rows[0].start()
        for tile in tiles:
            tile.start()
        raises.start()
        rows[1].start()
        rows[0].wait()

    @pl.when(owner == 1)
    def _():
        rows[1].wait()

    for n, tile in enumerate(tiles):

        @pl.when(owner == 0)
        def _():
            tile.wait()

        columns = slice(n * 256, (n + 1) * 256)
        base_s[:, columns] = dot(normed_s[owner], weight_s[:, columns])

    @pl.when(owner == 0)
    def _():
        raises.wait()

    low = base_s[:, 3 * HALF :].astype(BF16)
    low_ref[...] = low
    raise_q, raise_v = raising_of(raise_s)
    query = (base_s[:, :HALF] + dot(low, raise_q)).astype(BF16).astype(F32).T
    key = base_s[:, HALF : 2 * HALF].astype(BF16).astype(F32).T
    value = (base_s[:, 2 * HALF : 3 * HALF] + dot(low, raise_v)).astype(BF16).astype(F32).T
    qkv_ref[:HALF, :] = query.astype(BF16)
    qkv_ref[HALF : 2 * HALF, :] = key.astype(BF16)
    qkv_ref[2 * HALF :, :] = value.astype(BF16)

    rows_j = lax.broadcasted_iota(jnp.int32, (PACKED, PACKED), 0)
    rows_i = lax.broadcasted_iota(jnp.int32, (PACKED, PACKED), 1)
    allowed = (tag_ref[0:1, :] == code_ref[...]) | (rows_j == rows_i)
    ones_rows = jnp.where(lax.broadcasted_iota(jnp.int32, (32, PACKED), 0) < 2, 1.0, 0.0)

    for h in range(FOCI):
        head = slice(h * HEAD, (h + 1) * HEAD)
        temper = soft_ref[core * FOCI + h] * (1.0 / HEAD)
        qn, _ = unit(query[head, :])
        kn, _ = unit(key[head, :])
        qs = pad_rows(qn * (temper * math.log2(math.e))).astype(BF16)
        v = jnp.concatenate([value[head, :], ones_rows], axis=0)
        scores = dot(pad_rows(kn).T.astype(BF16), qs)
        unnormed = jnp.exp2(jnp.where(allowed, scores, -1e30)).astype(BF16)
        weights_ref[h] = unnormed
        mixed = dot(v.astype(BF16), unnormed)
        inverse = 1.0 / mixed[HEAD : HEAD + 1, :]
        inverse_ref[h : h + 1, :] = inverse
        mixed_ref[head, :] = mixed[:HEAD, :] * inverse

    context_ref[...] = mixed_ref[...].T.astype(BF16).reshape(context_ref.shape)


def forward(core, soft, tags, codes, mine, other, whole):
    anywhere = pl.BlockSpec(memory_space=pl.ANY)
    grid = pltpu.PrefetchScalarGridSpec(
        num_scalar_prefetch=1,
        grid=(2,),
        in_specs=[
            pl.BlockSpec(memory_space=SMEM),
            pl.BlockSpec((None, 8, PACKED), lambda o, c: (o, 0, 0)),
            pl.BlockSpec((None, PACKED, 1), lambda o, c: (o, 0, 0)),
            anywhere,
            anywhere,
            anywhere,
        ],
        out_specs=[
            pl.BlockSpec((OWNERS, None, SLOTS * LEN, HALF), lambda o, c: (0, o, 0, 0)),
            pl.BlockSpec((None, FOCI, PACKED, PACKED), lambda o, c: (o, 0, 0, 0)),
            pl.BlockSpec((None, 3 * HALF, PACKED), lambda o, c: (o, 0, 0)),
            pl.BlockSpec((None, PACKED, 2 * RANK), lambda o, c: (o, 0, 0)),
            pl.BlockSpec((None, HALF, PACKED), lambda o, c: (o, 0, 0)),
            pl.BlockSpec((None, 8, PACKED), lambda o, c: (o, 0, 0)),
        ],
        scratch_shapes=[
            pltpu.VMEM((2, PACKED, WIDE), BF16),
            pltpu.VMEM((WIDE, QKVL), BF16),
            pltpu.VMEM((WIDE // 2, 2 * RANK), BF16),
            pltpu.VMEM((PACKED, QKVL), F32),
            pltpu.SemaphoreType.DMA((2,)),
            pltpu.SemaphoreType.DMA((QKVL // 256,)),
            pltpu.SemaphoreType.DMA,
        ],
    )
    return pl.pallas_call(
        forward_kernel,
        grid_spec=grid,
        out_shape=(
            jax.ShapeDtypeStruct((OWNERS, 2, SLOTS * LEN, HALF), BF16),
            jax.ShapeDtypeStruct((2, FOCI, PACKED, PACKED), BF16),
            jax.ShapeDtypeStruct((2, 3 * HALF, PACKED), BF16),
            jax.ShapeDtypeStruct((2, PACKED, 2 * RANK), BF16),
            jax.ShapeDtypeStruct((2, HALF, PACKED), F32),
            jax.ShapeDtypeStruct((2, 8, PACKED), F32),
        ),
        compiler_params=pltpu.CompilerParams(
            vmem_limit_bytes=48 << 20, dimension_semantics=("arbitrary",)
        ),
        cost_estimate=pl.CostEstimate(
            flops=6 << 30, bytes_accessed=16 << 20, transcendentals=2 * FOCI * PACKED * PACKED
        ),
        name="forward",
    )(core, soft, tags, codes, mine, other, whole)


def backward_kernel(
    core_ref,
    soft_ref,
    weights_ref,
    qkv_ref,
    low_ref,
    mixed_ref,
    inverse_ref,
    mine_ref,
    other_ref,
    masked_mine_ref,
    masked_other_ref,
    whole_ref,
    keep_ref,
    send_ref,
    up_ref,
    normed_s,
    masked_s,
    out_s,
    raise_s,
    cot_s,
    dquery_s,
    dvalue_s,
    down_s,
    up_s,
    row_sems,
    masked_sems,
    out_sem,
    raise_sem,
):
    owner = pl.program_id(0)
    core = core_ref[0]
    rows = owner_copies((mine_ref, other_ref), normed_s, row_sems)
    masks = owner_copies((masked_mine_ref, masked_other_ref), masked_s, masked_sems)
    half = pl.ds(pl.multiple_of(core * (WIDE // 2), WIDE // 2), WIDE // 2)
    outs = pltpu.make_async_copy(whole_ref.at[half, pl.ds(0, HIDDEN)], out_s, out_sem)
    raises = pltpu.make_async_copy(
        whole_ref.at[half, pl.ds(HIDDEN + QKVL, 2 * RANK)], raise_s, raise_sem
    )

    @pl.when(owner == 0)
    def _():
        outs.start()
        masks[0].start()
        rows[0].start()
        raises.start()
        masks[1].start()
        rows[1].start()
        down_s[...] = jnp.zeros_like(down_s)
        up_s[...] = jnp.zeros_like(up_s)
        outs.wait()
        masks[0].wait()

    @pl.when(owner == 1)
    def _():
        masks[1].wait()

    sides = []
    for side in range(2):
        columns = slice(side * WIDE // 2, (side + 1) * WIDE // 2)
        both = dot_nt(out_s[...], masked_s[owner, :, columns])
        both = both.reshape(SHARDS // 2, BLOCK, PACKED)
        sides.append(both[:, side * UPS : (side + 1) * UPS])
    cot_s[...] = (sides[0] + sides[1]).reshape(HALF, PACKED).astype(BF16).astype(F32)

    ones_rows = jnp.where(lax.broadcasted_iota(jnp.int32, (32, PACKED), 0) < 2, 1.0, 0.0)
    sub = lax.broadcasted_iota(jnp.int32, (32, PACKED), 0)

    for h in range(FOCI):
        head = slice(h * HEAD, (h + 1) * HEAD)
        temper = soft_ref[core * FOCI + h] * (1.0 / HEAD)
        qn, rq = unit(qkv_ref[head, :].astype(F32))
        kn, _ = unit(qkv_ref[HALF + h * HEAD : HALF + (h + 1) * HEAD, :].astype(F32))
        value = qkv_ref[2 * HALF + h * HEAD : 2 * HALF + (h + 1) * HEAD, :].astype(F32)
        v = jnp.concatenate([value, ones_rows], axis=0)
        unnormed = weights_ref[h]
        dc = (cot_s[head, :] * inverse_ref[h : h + 1, :]).astype(BF16)
        shift = jnp.sum(dc.astype(F32) * mixed_ref[head, :], axis=0, keepdims=True)
        shift_top = shift.astype(BF16).astype(F32)
        extra = jnp.where(sub == 0, -shift_top, jnp.where(sub == 1, shift_top - shift, 0.0))
        dc = jnp.concatenate([dc, extra.astype(BF16)], axis=0)
        inner = dot(v.T.astype(BF16), dc)
        dscores = (unnormed.astype(F32) * inner).astype(BF16)
        dqn = dot(pad_rows(kn).astype(BF16), dscores)[:HEAD, :] * temper
        dq = rq * (dqn - qn * (jnp.sum(qn * dqn, axis=0, keepdims=True) * (1.0 / HEAD)))
        dquery_s[head, :] = dq.astype(BF16)
        dv = dot_nt(unnormed, dc)
        dvalue_s[head, :] = dv.T[:HEAD, :].astype(BF16)

    @pl.when(owner == 0)
    def _():
        raises.wait()
        rows[0].wait()

    @pl.when(owner == 1)
    def _():
        rows[1].wait()

    low = low_ref[...]
    raise_q, raise_v = raising_of(raise_s)
    dquery = dquery_s[...]
    dvalue = dvalue_s[...]
    lane = lax.broadcasted_iota(jnp.int32, (HALF, 2 * RANK), 1)
    up_s[...] += jnp.where(lane < RANK, dot(dquery, low), dot(dvalue, low))
    inner_t = (dot(raise_q, dquery) + dot(raise_v, dvalue)).astype(BF16)
    down_s[...] += dot(inner_t, normed_s[owner])

    @pl.when(owner == 1)
    def _():
        down = down_s[...].T.reshape(SHARDS, BLOCK, 2 * RANK)
        first = down[:, :UPS].reshape(SHARDS * UPS, 2 * RANK)
        second = down[:, UPS:].reshape(SHARDS * UPS, 2 * RANK)
        keep_ref[...] = jnp.where(core == 0, first, second)
        send_ref[...] = jnp.where(core == 0, second, first).astype(BF16)
        up_ref[...] = up_s[...]


def backward(core, soft, saved, normed, masked, whole):
    anywhere = pl.BlockSpec(memory_space=pl.ANY)
    grid = pltpu.PrefetchScalarGridSpec(
        num_scalar_prefetch=1,
        grid=(2,),
        in_specs=[
            pl.BlockSpec(memory_space=SMEM),
            pl.BlockSpec((None, FOCI, PACKED, PACKED), lambda o, c: (o, 0, 0, 0)),
            pl.BlockSpec((None, 3 * HALF, PACKED), lambda o, c: (o, 0, 0)),
            pl.BlockSpec((None, PACKED, 2 * RANK), lambda o, c: (o, 0, 0)),
            pl.BlockSpec((None, HALF, PACKED), lambda o, c: (o, 0, 0)),
            pl.BlockSpec((None, 8, PACKED), lambda o, c: (o, 0, 0)),
        ]
        + [anywhere] * 5,
        out_specs=[
            pl.BlockSpec((SHARDS * UPS, 2 * RANK), lambda o, c: (0, 0)),
            pl.BlockSpec((SHARDS * UPS, 2 * RANK), lambda o, c: (0, 0)),
            pl.BlockSpec((HALF, 2 * RANK), lambda o, c: (0, 0)),
        ],
        scratch_shapes=[
            pltpu.VMEM((2, PACKED, WIDE), BF16),
            pltpu.VMEM((2, PACKED, WIDE), BF16),
            pltpu.VMEM((WIDE // 2, HIDDEN), BF16),
            pltpu.VMEM((WIDE // 2, 2 * RANK), BF16),
            pltpu.VMEM((HALF, PACKED), F32),
            pltpu.VMEM((HALF, PACKED), BF16),
            pltpu.VMEM((HALF, PACKED), BF16),
            pltpu.VMEM((2 * RANK, WIDE), F32),
            pltpu.VMEM((HALF, 2 * RANK), F32),
            pltpu.SemaphoreType.DMA((2,)),
            pltpu.SemaphoreType.DMA((2,)),
            pltpu.SemaphoreType.DMA,
            pltpu.SemaphoreType.DMA,
        ],
    )
    return pl.pallas_call(
        backward_kernel,
        grid_spec=grid,
        out_shape=(
            jax.ShapeDtypeStruct((SHARDS * UPS, 2 * RANK), F32),
            jax.ShapeDtypeStruct((SHARDS * UPS, 2 * RANK), BF16),
            jax.ShapeDtypeStruct((HALF, 2 * RANK), F32),
        ),
        compiler_params=pltpu.CompilerParams(
            vmem_limit_bytes=48 << 20, dimension_semantics=("arbitrary",)
        ),
        cost_estimate=pl.CostEstimate(flops=8 << 30, bytes_accessed=16 << 20, transcendentals=0),
        name="backward",
    )(core, soft, *saved, *normed, *masked, whole)


def combine_kernel(core_ref, keep_ref, come_ref, up_ref, parts_ref):
    down = keep_ref[...] + come_ref[...].astype(F32)
    up = up_ref[...]
    none = jnp.zeros_like(up)
    low_half = core_ref[0] == 0
    up = jnp.concatenate([jnp.where(low_half, up, none), jnp.where(low_half, none, up)], axis=0)
    shape = (SHARDS, UPS, 2 * RANK)
    parts = jnp.concatenate([down.reshape(shape), up.reshape(shape)], axis=1)
    parts_ref[...] = parts.reshape(parts_ref.shape).astype(BF16)


def combine(core, keep, come, up):
    return pl.pallas_call(
        combine_kernel,
        out_shape=jax.ShapeDtypeStruct((SHARDS * GRAD, 2 * RANK), BF16),
        in_specs=[pl.BlockSpec(memory_space=SMEM)] + [pl.BlockSpec(memory_space=VMEM)] * 3,
        out_specs=pl.BlockSpec(memory_space=VMEM),
        name="combine",
    )(core, keep, come, up)


def finish_kernel(owner_ref, live_ref, context_ref, x_ref, out_a_ref, out_b_ref, block_ref):
    place, step = spread(slot_places(owner_ref), (ROWS, 1), 0)
    target = place * LEN + step
    slots = lax.broadcasted_iota(jnp.int32, (ROWS, PACKED), 1)
    select = jnp.where(slots == target, 1.0, 0.0).astype(BF16)
    lives, _ = spread([live_ref[p] for p in range(PANELS)], (ROWS, 1), 0)
    halves = []
    for half in range(2):
        parts = []
        for o in range(OWNERS):
            source = o // 2 * 2 + half
            first = 0 if source == o else SLOTS * LEN
            parts.append(context_ref[source, first : first + SLOTS * LEN, :])
        halves.append(dot(select, jnp.concatenate(parts, axis=0)).astype(BF16))
    for side, ref in enumerate((out_a_ref, out_b_ref)):
        columns = slice(side * WIDE // 2, (side + 1) * WIDE // 2)
        attended = dot(halves[0], ref[:HALF, :]) + dot(halves[1], ref[HALF:, :])
        added = jnp.where(step < lives, attended, 0.0)
        block_ref[:, columns] = (x_ref[:, columns].astype(F32) + added).astype(BF16)


def finish(owners, lives, context, x, out_a, out_b):
    return pl.pallas_call(
        finish_kernel,
        out_shape=jax.ShapeDtypeStruct((ROWS, WIDE), BF16),
        in_specs=[pl.BlockSpec(memory_space=SMEM)] * 2 + [pl.BlockSpec(memory_space=VMEM)] * 4,
        out_specs=pl.BlockSpec(memory_space=VMEM),
        compiler_params=pltpu.CompilerParams(vmem_limit_bytes=40 << 20),
        cost_estimate=pl.CostEstimate(
            flops=2 * ROWS * 2 * HALF * (WIDE + PACKED), bytes_accessed=6 << 20, transcendentals=0
        ),
        name="finish",
    )(owners, lives, context, x, out_a, out_b)


def add_shards_kernel(part_ref, total_ref):
    total = part_ref[0].astype(F32)
    for t in range(1, SHARDS):
        total = total + part_ref[t].astype(F32)
    total = total.astype(BF16)
    for o in range(OWNERS):
        total_ref[o] = total


def add_shards(parts):
    return pl.pallas_call(
        add_shards_kernel,
        out_shape=jax.ShapeDtypeStruct((OWNERS, GRAD, 2 * RANK), BF16),
        in_specs=[pl.BlockSpec(memory_space=VMEM)],
        out_specs=pl.BlockSpec(memory_space=VMEM),
        name="add_shards",
    )(parts)


def add_owners_kernel(part_ref, down_ref, up_ref):
    downs = [jnp.zeros((UPS, 2 * RANK), F32)] * 2
    up = jnp.zeros((UPS, 2 * RANK), F32)
    for o in range(OWNERS):
        part = part_ref[o].astype(F32)
        downs[o % 2] = downs[o % 2] + part[:UPS, :]
        up = up + part[UPS:, :]
    down = jnp.concatenate(downs, axis=0)
    for n in range(2):
        down_ref[n] = down[:, n * RANK : (n + 1) * RANK]
        up_ref[n] = up[:, n * RANK : (n + 1) * RANK]


def add_owners(parts):
    return pl.pallas_call(
        add_owners_kernel,
        out_shape=(
            jax.ShapeDtypeStruct((2, BLOCK, RANK), F32),
            jax.ShapeDtypeStruct((2, UPS, RANK), F32),
        ),
        in_specs=[pl.BlockSpec(memory_space=VMEM)],
        out_specs=(pl.BlockSpec(memory_space=VMEM),) * 2,
        name="add_owners",
    )(parts)


def exchange(data, axis):
    return lax.all_to_all(data, axis, split_axis=0, concat_axis=0, tiled=True)


def swap_cores(data):
    pairs = [(s, s ^ 1) for s in range(OWNERS)]
    return lax.ppermute(data, "seq", pairs)


def packed_facts(owners, tags, lives):
    same = owners[:, None] == owners[None, :]
    order = jnp.arange(PANELS, dtype=jnp.int32)
    rank = jnp.sum((same & (order[:, None] > order[None, :])).astype(jnp.int32), axis=1)
    place = owners * SLOTS + rank
    hits = place[None, :] == jnp.arange(OWNERS * SLOTS, dtype=jnp.int32)[:, None]
    facts = [jnp.sum(jnp.where(hits, fact[None, :], 0), axis=1) for fact in (tags, lives)]
    sent = jnp.stack(facts, axis=-1).astype(BF16).reshape(OWNERS // 2, 2, SLOTS * 2)
    return jnp.stack([sent, sent[:, ::-1]], axis=2).reshape(OWNERS, 2, SLOTS, 2)


def row_facts(received):
    received = jnp.swapaxes(received.astype(F32), 0, 1).reshape(2, OWNERS * SLOTS, 1, 2)
    steps = jnp.arange(LEN, dtype=jnp.int32).astype(F32)[None, None, :]
    tag = jnp.broadcast_to(received[..., 0], (2, OWNERS * SLOTS, LEN))
    code = jnp.where(steps < received[..., 1], tag, -1.0)
    rows = jnp.broadcast_to(tag.reshape(2, 1, PACKED), (2, 8, PACKED))
    return rows, code.reshape(2, PACKED, 1)


def on_device(
    encoder_timesteps,
    tile_parent_sequence,
    tile_recording_label,
    tile_valid_timesteps,
    standardize_scaling,
    triple_projector,
    final_projector,
    lowered_maps,
    raising_maps,
    focus_softness,
    result_adjoint,
):
    core = lax.axis_index("seq") % 2
    starts = [n * 2 * HALF for n in range(3)]
    triple = [
        jnp.where(
            core == 0,
            triple_projector[:, first : first + HALF],
            triple_projector[:, first + HALF : first + 2 * HALF],
        )
        for first in starts
    ]
    lowered = jnp.concatenate([lowered_maps[0], lowered_maps[1]], axis=1)
    outward = jnp.concatenate([final_projector[:, : WIDE // 2], final_projector[:, WIDE // 2 :]], axis=0)
    raising = raising_maps.reshape(2 * RANK, UPS).T
    raising = jnp.concatenate([raising, jnp.zeros_like(raising)], axis=0)
    shard = jnp.concatenate([outward, *triple, lowered, raising], axis=1)
    whole = lax.all_gather(shard, "dp", axis=0, tiled=True)

    x = encoder_timesteps.reshape(ROWS, WIDE)
    facts = exchange(
        packed_facts(tile_parent_sequence, tile_recording_label, tile_valid_timesteps), "seq"
    )
    normed, masked = pack(
        tile_parent_sequence,
        tile_valid_timesteps,
        x,
        result_adjoint.reshape(ROWS, WIDE),
        standardize_scaling.reshape(1, WIDE),
    )
    normed, facts = lax.optimization_barrier((normed, facts))
    tag_rows, codes = row_facts(facts)
    normed = exchange(normed, "seq")
    normed, masked = lax.optimization_barrier((normed, masked))
    masked = exchange(masked, "seq")
    flat = (PACKED, WIDE)
    normed = (normed.reshape(flat), swap_cores(normed).reshape(flat))
    masked = (masked.reshape(flat), swap_cores(masked).reshape(flat))

    core = core.reshape(1)
    context, *saved = forward(core, focus_softness, tag_rows, codes, *normed, whole)
    whole, context = lax.optimization_barrier((whole, context))
    keep, send, up = backward(core, focus_softness, saved, normed, masked, whole)
    context = exchange(context.reshape(OWNERS, 2 * SLOTS * LEN, HALF), "seq")
    parts = combine(core, keep, swap_cores(send), up)
    outs = whole.reshape(SHARDS, BLOCK, -1)[:, :, :HIDDEN]
    out_a = outs[:, :UPS].reshape(HIDDEN, WIDE // 2)
    out_b = outs[:, UPS:].reshape(HIDDEN, WIDE // 2)
    parts, context = lax.optimization_barrier((parts, context))
    parts = exchange(parts.reshape(SHARDS, GRAD, 2 * RANK), "dp")
    block_out = finish(tile_parent_sequence, tile_valid_timesteps, context, x, out_a, out_b)
    shard_down, shard_up = add_owners(exchange(add_shards(parts), "seq"))
    return block_out.reshape(encoder_timesteps.shape), shard_down, jnp.swapaxes(shard_up, 1, 2)


def solution(mesh):
    in_specs = (
        P(("dp", "seq"), None, None),
        P(("dp", "seq")),
        P(("dp", "seq")),
        P(("dp", "seq")),
        P(),
        P("dp", None),
        P("dp", None),
        P(None, "dp", None),
        P(None, None, "dp"),
        P(),
        P(("dp", "seq"), None, None),
    )
    out_specs = (P(("dp", "seq"), None, None), P(None, "dp", None), P(None, None, "dp"))
    return jax.shard_map(
        on_device, mesh=mesh, in_specs=in_specs, out_specs=out_specs, check_vma=False
    )
```

time: 251 us -> 220 us (0.88)
  waiting for transfers between devices: 72.3 us -> 47.2 us
  blocking collectives: 77.9 us -> 66.7 us
  starting transfers between devices: 23.2 us -> 33 us
  Pallas kernels: 31.6 us -> 41.4 us
  local copies, waits for them, and re-layouts: 20.4 us -> 13 us
  other arithmetic: 10.2 us -> 3.41 us
    all_to_all x4, waiting for transfers between devices: 72.3 us -> 45.9 us  [exchange(): return lax.all_to_all(data, axis, split_axis=0, concat_axis=0, tiled=True)]
    all_to_all x2, blocking collectives: 77.9 us -> 66.7 us  [exchange(): return lax.all_to_all(data, axis, split_axis=0, concat_axis=0, tiled=True)]
    pallas_call x1 -> x3, Pallas kernels: 21.9 us -> 31.9 us  [the longest x1 17.4 us: forward(): pl.pallas_call(forward_kernel, grid_spec=grid, out_shape=(jax.ShapeDtypeS...]
    all_to_all x4, starting transfers between devices: 19.4 us -> 27.2 us  [exchange(): return lax.all_to_all(data, axis, split_axis=0, concat_axis=0, tiled=True)]
    another operation x5 -> x3, other arithmetic: 6.87 us -> 0.03 us  [the longest x1 0.01 us: packed_facts(): jnp.stack(facts, axis=-1).astype(BF16).reshape(OWNERS // 2, 2, SLOTS * 2)]
    slice x3 -> x2, local copies, waits for them, and re-layouts: 4.82 us -> 1.88 us  [the longest x1 1.87 us: on_device(): out_b = outs[:, UPS:].reshape(HIDDEN, WIDE // 2)]
    ppermute x2 -> x3, starting transfers between devices: 3.82 us -> 5.83 us  [swap_cores(): return lax.ppermute(data, 'seq', pairs)]
    unnamed x24 -> x27, local copies, waits for them, and re-layouts: 7.68 us -> 6.17 us
  transfers between devices with their start and end apart: 7 -> 8, of which waited for: 4 -> 5; matrix products, arithmetic and copies ran while one was open for 6% -> 3% of each run, Pallas kernels for 3% -> 17%
where the time goes in v2:
time: 220 us; the launch traced here: 219 us
  blocking collectives  66.7 us (30%)
  waiting for transfers between devices  47.2 us (21%)
  Pallas kernels  41.4 us (19%)
  starting transfers between devices  33 us (15%)
  between operations  14.4 us (7%)
  local copies, waits for them, and re-layouts  13 us (6%)
  other arithmetic  3.41 us (2%)
    all_to_all x2, blocking collectives, exchange(): return lax.all_to_all(data, axis, split_axis=0, concat_axis=0, tiled=True)  66.7 us
    all_to_all x4, waiting for transfers between devices, exchange(): return lax.all_to_all(data, axis, split_axis=0, concat_axis=0, tiled=True)  45.9 us
    all_to_all x4, starting transfers between devices, exchange(): return lax.all_to_all(data, axis, split_axis=0, concat_axis=0, tiled=True)  27.2 us
    pallas_call x1, Pallas kernels, forward(): pl.pallas_call(forward_kernel, grid_spec=grid, out_shape=(jax.ShapeDtypeS...  17.4 us
    pallas_call x1, Pallas kernels, backward(): pl.pallas_call(backward_kernel, grid_spec=grid, out_shape=(jax.ShapeDtype...  12.6 us
    unnamed x27, local copies, waits for them, and re-layouts  6.17 us
    ppermute x3, starting transfers between devices, swap_cores(): return lax.ppermute(data, 'seq', pairs)  5.83 us
  transfers between devices with their start and end apart: 8, of which 5 were waited for; matrix products, arithmetic and copies ran while one was open for 3% of the time, Pallas kernels for 17%

profile of v2, /device:TPU:1, one launch (start us, length us, event | category | flops | bytes accessed | tf_op | source)
XLA Modules:
  0.0 219.1 jit_solution(6567372773846269982)
XLA Ops:
  15.3 11.8 %all-to-all-start = ((bf16[16,2,2,2]{2,3,1,0:T(2,128)(2,1)}), bf16[16,2,2,2]{2,3,1,0:T(2,128)(2,1)S(1)}, u32[]{:S(2)}, u32[]{:S(2)}) async-start(bf16[16,2,2,2]{2,3,1,0:T(2,128)(2,1)} %copy.37), calls=%async_computation | async-start | bytes 32768 | tf_op jit(solution)/shard_map/all_to_all | solution.py:534
  27.2 3.2 %pack.1 = (bf16[16,32,1536]{2,1,0:T(8,128)(2,1)S(1)}, bf16[16,32,1536]{2,1,0:T(8,128)(2,1)}) custom-call(s32[16]{0:T(128)S(1)} %copy-done.5, s32[16]{0:T(128)S(1)} %copy-done.4, bf16[256,1536]{1,0:T(8,128)(2,1)S(1)} %bitcast.37, bf16[256,1536]{1,0:T(8,128)(2,1)S(1)} %bitcast.39, f32[1,1536]{1,0:T(1,128)S(1)} %reshape.162.gain_ref), custom_call_target="tpu_custom_call" | custom-call | flops 805306368 | bytes 4718592 | tf_op jit(solution)/shard_map/pack/pallas_call | solution.py:80
  30.4 4.1 %all-to-all-done = bf16[16,2,2,2]{2,3,1,0:T(2,128)(2,1)S(1)} async-done(((bf16[16,2,2,2]{2,3,1,0:T(2,128)(2,1)}), bf16[16,2,2,2]{2,3,1,0:T(2,128)(2,1)S(1)}, u32[]{:S(2)}, u32[]{:S(2)}) %all-to-all-start) | async-done | bytes 288 | tf_op jit(solution)/shard_map/all_to_all | solution.py:534
  34.5 42.7 %all_to_all.30 = bf16[16,32,1536]{2,1,0:T(8,128)(2,1)S(1)} all-to-all(bf16[16,32,1536]{2,1,0:T(8,128)(2,1)S(1)} %get-tuple-element.26), channel_id=1, replica_groups=mesh['dp'=32,'seq'=16] {'seq'}, dimensions={0} | all-to-all | bytes 3145728 | tf_op jit(solution)/shard_map/all_to_all | solution.py:534
  77.2 4.3 %all-to-all-start.2 = ((bf16[16,32,1536]{2,1,0:T(8,128)(2,1)}), bf16[16,32,1536]{2,1,0:T(8,128)(2,1)}, u32[]{:S(2)}, u32[]{:S(2)}) async-start(bf16[16,32,1536]{2,1,0:T(8,128)(2,1)} %get-tuple-element.34), calls=%async_computation.2 | async-start | bytes 3145728 | tf_op jit(solution)/shard_map/all_to_all | solution.py:534
  81.6 1.9 collective-permute-start
  83.6 35.0 %all-to-all-done.2 = bf16[16,32,1536]{2,1,0:T(8,128)(2,1)} async-done(((bf16[16,32,1536]{2,1,0:T(8,128)(2,1)}), bf16[16,32,1536]{2,1,0:T(8,128)(2,1)}, u32[]{:S(2)}, u32[]{:S(2)}) %all-to-all-start.2) | async-done | bytes 1572896 | tf_op jit(solution)/shard_map/all_to_all | solution.py:534
  118.6 1.9 collective-permute-start.1
  121.7 17.4 %forward.1 = (bf16[16,2,32,384]{3,2,1,0:T(8,128)(2,1)}, bf16[2,4,512,512]{3,2,1,0:T(8,128)(2,1)}, bf16[2,1152,512]{2,1,0:T(8,128)(2,1)}, bf16[2,512,128]{2,1,0:T...) custom-call(s32[1]{0:T(128)} %bitcast.core_ref, f32[8]{0:T(128)S(1)} %copy-done.7, ...), custom_call_target="tpu_custom_call" | custom-call | flops 6442450944 | bytes 16777216 | tf_op jit(solution)/shard_map/forward/pallas_call | solution.py:243
  139.2 1.1 copy-done.8
  140.3 4.5 %all-to-all-start.3 = ((bf16[16,64,384]{2,1,0:T(8,128)(2,1)}), bf16[16,64,384]{2,1,0:T(8,128)(2,1)S(1)}, u32[]{:S(2)}, u32[]{:S(2)}) async-start(bf16[16,64,384]{2,1,0:T(8,128)(2,1)} %bitcast.15), calls=%async_computation.3 | async-start | bytes 1572864 | tf_op jit(solution)/shard_map/all_to_all | solution.py:534
  144.8 1.4 copy-done.9
  146.2 12.6 %backward.1 = (f32[768,128]{1,0:T(8,128)S(1)}, bf16[768,128]{1,0:T(8,128)(2,1)S(1)}, f32[384,128]{1,0:T(8,128)S(1)}) custom-call(s32[1]{0:T(128)} %bitcast.core_ref, f32[8]{0:T(128)S(1)} %copy-done.7, bf16[2,4,512,512]{3,2,1,0:T(8,128)(2,1)} %get-tuple-element.29.weights_ref, bf16[2,1152,512]{2,1,0:T(8,128)(2,1)} %get-tuple-element.30.qkv_ref, ...), custom_call_target="tpu_custom_call" | custom-call | flops 8589934592 | bytes 16777216 | tf_op jit(solution)/shard_map/backward/pallas_call | solution.py:416
  160.2 2.0 collective-permute-start.2
  162.2 1.3 collective-permute-done.2.come_ref
  164.2 1.9 combine.1
  166.2 1.3 all-to-all-done.3.context_ref
  167.5 23.9 %all_to_all.31.part_ref = bf16[32,48,128]{2,1,0:T(8,128)(2,1)} all-to-all(bf16[32,48,128]{2,1,0:T(8,128)(2,1)} %bitcast.40), channel_id=1, replica_groups=mesh['dp'=32,'seq'=16] {'dp'}, dimensions={0} | all-to-all | bytes 786432 | tf_op jit(solution)/shard_map/all_to_all | solution.py:534
  191.4 1.8 add_shards.1
  193.1 6.5 %all-to-all-start.5 = ((bf16[16,48,128]{2,1,0:T(8,128)(2,1)}), bf16[16,48,128]{2,1,0:T(8,128)(2,1)S(1)}, u32[]{:S(2)}, u32[]{:S(2)}) async-start(bf16[16,48,128]{2,1,0:T(8,128)(2,1)} %add_shards.1), calls=%async_computation.5 | async-start | bytes 393216 | tf_op jit(solution)/shard_map/all_to_all | solution.py:534
  199.7 1.9 fusion.1
  201.5 2.9 %finish.1 = bf16[256,1536]{1,0:T(8,128)(2,1)} custom-call(s32[16]{0:T(128)S(1)} %copy-done.5, s32[16]{0:T(128)S(1)} %copy-done.4, bf16[16,64,384]{2,1,0:T(8,128)(2,1)S(1)} %all-to-all-done.3.context_ref, bf16[256,1536]{1,0:T(8,128)(2,1)S(1)} %bitcast.38, bf16[768,768]{1,0:T(8,128)(2,1)S(1)} %bitcast.34, bf16[768,768]{1,0:T(8,128)(2,1)S(1)} %bitcast.33), custom_call_target="tpu_custom_call" | custom-call | flops 805306368 | bytes 6291456 | tf_op jit(solution)/shard_map/finish/pallas_call | solution.py:475
  204.5 5.5 %all-to-all-done.5.part_ref = bf16[16,48,128]{2,1,0:T(8,128)(2,1)S(1)} async-done(((bf16[16,48,128]{2,1,0:T(8,128)(2,1)}), bf16[16,48,128]{2,1,0:T(8,128)(2,1)S(1)}, u32[]{:S(2)}, u32[]{:S(2)}) %all-to-all-start.5) | async-done | bytes 196640 | tf_op jit(solution)/shard_map/all_to_all | solution.py:534
  210.7 1.6 add_owners.1
  (68 shorter events, 12.0 us)
Async XLA Ops:
  7.2 20.0 %copy-start.5 = (s32[16]{0:T(128)S(1)}, s32[16]{0:T(128)}, u32[]{:S(2)}) copy-start(s32[16]{0:T(128)} %owner_ref.3) | copy-start | bytes 196
  7.2 20.0 %copy-start.4 = (s32[16]{0:T(128)S(1)}, s32[16]{0:T(128)}, u32[]{:S(2)}) copy-start(s32[16]{0:T(128)} %live_ref.3) | copy-start | bytes 196
  7.2 20.0 %copy-start.12 = (f32[1536]{0:T(1024)S(1)}, f32[1536]{0:T(1024)}, u32[]{:S(2)}) copy-start(f32[1536]{0:T(1024)} %param.15) | copy-start | bytes 18436
  7.2 20.0 %copy-start.6 = (bf16[16,16,1536]{2,1,0:T(8,128)(2,1)S(1)}, bf16[16,16,1536]{2,1,0:T(8,128)(2,1)}, u32[]{:S(2)}) copy-start(bf16[16,16,1536]{2,1,0:T(8,128)(2,1)} %param.21) | copy-start | bytes 2359300
  7.2 20.0 %copy-start = (bf16[16,16,1536]{2,1,0:T(8,128)(2,1)S(1)}, bf16[16,16,1536]{2,1,0:T(8,128)(2,1)}, u32[]{:S(2)}) copy-start(bf16[16,16,1536]{2,1,0:T(8,128)(2,1)} %param.11) | copy-start | bytes 2359300
  7.2 114.5 %all-gather.2.cloned.1.call-start = ((), (), s32[]{:S(2)}) async-start(), calls=%async_computation.6 | async-start | bytes 6893568 | tf_op jit(solution)/shard_map/all_gather | solution.py:590
  15.3 19.2 %all-to-all-start = ((bf16[16,2,2,2]{2,3,1,0:T(2,128)(2,1)}), bf16[16,2,2,2]{2,3,1,0:T(2,128)(2,1)S(1)}, u32[]{:S(2)}, u32[]{:S(2)}) async-start(bf16[16,2,2,2]{2,3,1,0:T(2,128)(2,1)} %copy.37), calls=%async_computation | async-start | bytes 32768 | tf_op jit(solution)/shard_map/all_to_all | solution.py:534
  77.2 41.4 %all-to-all-start.2 = ((bf16[16,32,1536]{2,1,0:T(8,128)(2,1)}), bf16[16,32,1536]{2,1,0:T(8,128)(2,1)}, u32[]{:S(2)}, u32[]{:S(2)}) async-start(bf16[16,32,1536]{2,1,0:T(8,128)(2,1)} %get-tuple-element.34), calls=%async_computation.2 | async-start | bytes 3145728 | tf_op jit(solution)/shard_map/all_to_all | solution.py:534
  81.6 40.2 %copy-start.7 = (f32[8]{0:T(128)S(1)}, f32[8]{0:T(128)}, u32[]{:S(2)}) copy-start(f32[8]{0:T(128)} %soft_ref.3) | copy-start | bytes 100
  81.6 40.1 %collective-permute-start = (bf16[16,32,1536]{2,1,0:T(8,128)(2,1)S(1)}, bf16[16,32,1536]{2,1,0:T(8,128)(2,1)}, u32[]{:S(2)}, u32[]{:S(2)}) collective-permute-start(bf16[16,32,1536]{2,1,0:T(8,128)(2,1)S(1)} %all_to_all.30), channel_id=1, source_target_pairs={{0,1},{1,0},{2,3},{3,2},{4,5},{5,4},{6,7},{7,6},{8,9},{9,8},{10,11... | collective-permute-start | bytes 4718600 | tf_op jit(solution)/shard_map/ppermute | solution.py:539
  118.6 26.2 %collective-permute-start.1 = (bf16[16,32,1536]{2,1,0:T(8,128)(2,1)}, bf16[16,32,1536]{2,1,0:T(8,128)(2,1)}, u32[]{:S(2)}, u32[]{:S(2)}) collective-permute-start(bf16[16,32,1536]{2,1,0:T(8,128)(2,1)} %all-to-all-done.2), channel_id=1, source_target_pairs={{0,1},{1,0},{2,3},{3,2},{4,5},{5,4},{6,7},{7,6},{8,9},{9,8},{10,11... | collective-permute-start | bytes 4718600 | tf_op jit(solution)/shard_map/ppermute | solution.py:539
  139.1 1.1 copy-start.8
  140.3 27.2 %all-to-all-start.3 = ((bf16[16,64,384]{2,1,0:T(8,128)(2,1)}), bf16[16,64,384]{2,1,0:T(8,128)(2,1)S(1)}, u32[]{:S(2)}, u32[]{:S(2)}) async-start(bf16[16,64,384]{2,1,0:T(8,128)(2,1)} %bitcast.15), calls=%async_computation.3 | async-start | bytes 1572864 | tf_op jit(solution)/shard_map/all_to_all | solution.py:534
  144.8 1.4 copy-start.9
  158.8 0.7 copy-start.2
  159.6 0.7 copy-start.3
  160.2 3.3 %collective-permute-start.2 = (bf16[768,128]{1,0:T(8,128)(2,1)S(1)}, bf16[768,128]{1,0:T(8,128)(2,1)S(1)}, u32[]{:S(2)}, u32[]{:S(2)}) collective-permute-start(bf16[768,128]{1,0:T(8,128)(2,1)S(1)} %get-tuple-element.38), channel_id=1, source_target_pairs={{0,1},{1,0},{2,3},{3,2},{4,5},{5,4},{6,7},{7,6},{8,9},{9,8},{10,11... | collective-permute-start | bytes 589832 | tf_op jit(solution)/shard_map/ppermute | solution.py:539
  163.6 0.7 copy-start.11
  193.1 16.8 %all-to-all-start.5 = ((bf16[16,48,128]{2,1,0:T(8,128)(2,1)}), bf16[16,48,128]{2,1,0:T(8,128)(2,1)S(1)}, u32[]{:S(2)}, u32[]{:S(2)}) async-start(bf16[16,48,128]{2,1,0:T(8,128)(2,1)} %add_shards.1), calls=%async_computation.5 | async-start | bytes 393216 | tf_op jit(solution)/shard_map/all_to_all | solution.py:534
  199.7 1.9 copy-start.1
  210.0 0.7 copy-start.10
Sparse Core Ops, SparseCore 0:
  11.8 100.6 all-gather.1

commit v3 on v2

--- a/solution.py
+++ b/solution.py
@@ -25,6 +25,8 @@
 UPS = 2 * HALF // SHARDS
 GRAD = 2 * UPS
 HIDDEN = 2 * HALF
+QUARTER = WIDE // 4
+FACTS = 128
 QKVL = 3 * HALF + 2 * RANK
 F32 = jnp.float32
 BF16 = jnp.bfloat16
@@ -60,7 +62,7 @@
     return values, index % LEN
 
 
-def pack_kernel(owner_ref, live_ref, x_ref, adjoint_ref, gain_ref, normed_ref, masked_ref):
+def pack_kernel(owner_ref, tag_ref, live_ref, x_ref, gain_ref, packed_ref):
     place, step = spread(slot_places(owner_ref), (1, ROWS), 1)
     target = place * LEN + step
     slots = lax.broadcasted_iota(jnp.int32, (PACKED, ROWS), 0)
@@ -69,25 +71,51 @@
     centred = values - jnp.mean(values, axis=-1, keepdims=True)
     scaled = centred * lax.rsqrt(jnp.mean(centred * centred, axis=-1, keepdims=True) + EPS_NORM)
     normed = (scaled * gain_ref[...]).astype(BF16)
-    normed_ref[...] = dot(select, normed).astype(BF16).reshape(normed_ref.shape)
+    packed_ref[:, :, :WIDE] = dot(select, normed).astype(BF16).reshape(OWNERS, SLOTS * LEN, WIDE)
+    tags, step = spread([tag_ref[p] for p in range(PANELS)], (ROWS, FACTS), 0)
+    lives, _ = spread([live_ref[p] for p in range(PANELS)], (ROWS, FACTS), 0)
+    lane = lax.broadcasted_iota(jnp.int32, (ROWS, FACTS), 1)
+    alive = jnp.where(step < lives, 1, 0)
+    facts = jnp.where(lane == 0, tags, jnp.where(lane == 1, alive, 0)).astype(F32).astype(BF16)
+    packed_ref[:, :, WIDE:] = dot(select, facts).astype(BF16).reshape(OWNERS, SLOTS * LEN, FACTS)
+
+
+def pack(owners, tags, lives, x, gain):
+    return pl.pallas_call(
+        pack_kernel,
+        out_shape=jax.ShapeDtypeStruct((OWNERS, SLOTS * LEN, WIDE + FACTS), BF16),
+        in_specs=[pl.BlockSpec(memory_space=SMEM)] * 3 + [pl.BlockSpec(memory_space=VMEM)] * 2,
+        out_specs=pl.BlockSpec(memory_space=VMEM),
+        compiler_params=pltpu.CompilerParams(vmem_limit_bytes=32 << 20),
+        cost_estimate=pl.CostEstimate(
+            flops=2 * PACKED * ROWS * WIDE, bytes_accessed=4 * PACKED * WIDE, transcendentals=0
+        ),
+        name="pack",
+    )(owners, tags, lives, x, gain)
+
+
+def pack_masked_kernel(owner_ref, live_ref, adjoint_ref, packed_ref):
+    place, step = spread(slot_places(owner_ref), (1, ROWS), 1)
+    target = place * LEN + step
+    slots = lax.broadcasted_iota(jnp.int32, (PACKED, ROWS), 0)
+    select = jnp.where(slots == target, 1.0, 0.0).astype(BF16)
     lives, step = spread([live_ref[p] for p in range(PANELS)], (ROWS, 1), 0)
     masked = jnp.where(step < lives, adjoint_ref[...].astype(F32), 0.0).astype(BF16)
-    masked_ref[...] = dot(select, masked).astype(BF16).reshape(masked_ref.shape)
-
-
-def pack(owners, lives, x, adjoint, gain):
-    packed = jax.ShapeDtypeStruct((OWNERS, SLOTS * LEN, WIDE), BF16)
-    return pl.pallas_call(
-        pack_kernel,
-        out_shape=(packed, packed),
-        in_specs=[pl.BlockSpec(memory_space=SMEM)] * 2 + [pl.BlockSpec(memory_space=VMEM)] * 3,
-        out_specs=(pl.BlockSpec(memory_space=VMEM),) * 2,
-        compiler_params=pltpu.CompilerParams(vmem_limit_bytes=40 << 20),
+    packed_ref[...] = dot(select, masked).astype(BF16).reshape(packed_ref.shape)
+
+
+def pack_masked(owners, lives, adjoint):
+    return pl.pallas_call(
+        pack_masked_kernel,
+        out_shape=jax.ShapeDtypeStruct((OWNERS, SLOTS * LEN, WIDE), BF16),
+        in_specs=[pl.BlockSpec(memory_space=SMEM)] * 2 + [pl.BlockSpec(memory_space=VMEM)],
+        out_specs=pl.BlockSpec(memory_space=VMEM),
+        compiler_params=pltpu.CompilerParams(vmem_limit_bytes=32 << 20),
         cost_estimate=pl.CostEstimate(
-            flops=4 * PACKED * ROWS * WIDE, bytes_accessed=6 * PACKED * WIDE, transcendentals=0
-        ),
-        name="pack",
-    )(owners, lives, x, adjoint, gain)
+            flops=2 * PACKED * ROWS * WIDE, bytes_accessed=4 * PACKED * WIDE, transcendentals=0
+        ),
+        name="pack_masked",
+    )(owners, lives, adjoint)
 
 
 def pad_rows(values, rows=128):
@@ -115,8 +143,6 @@
 def forward_kernel(
     core_ref,
     soft_ref,
-    tag_ref,
-    code_ref,
     mine_ref,
     other_ref,
     whole_ref,
@@ -139,7 +165,7 @@
     rows = owner_copies((mine_ref, other_ref), normed_s, row_sems)
     tiles = [
         pltpu.make_async_copy(
-            whole_ref.at[:, pl.ds(HIDDEN + n * 256, 256)],
+            whole_ref.at[:, pl.ds(n * 256, 256)],
             weight_s.at[:, pl.ds(n * 256, 256)],
             weight_sems.at[n],
         )
@@ -147,7 +173,7 @@
     ]
     half = pl.ds(pl.multiple_of(core * (WIDE // 2), WIDE // 2), WIDE // 2)
     raises = pltpu.make_async_copy(
-        whole_ref.at[half, pl.ds(HIDDEN + QKVL, 2 * RANK)], raise_s, raise_sem
+        whole_ref.at[half, pl.ds(QKVL, 2 * RANK)], raise_s, raise_sem
     )
 
     @pl.when(owner == 0)
@@ -170,7 +196,7 @@
             tile.wait()
 
         columns = slice(n * 256, (n + 1) * 256)
-        base_s[:, columns] = dot(normed_s[owner], weight_s[:, columns])
+        base_s[:, columns] = dot(normed_s[owner, :, :WIDE], weight_s[:, columns])
 
     @pl.when(owner == 0)
     def _():
@@ -188,7 +214,9 @@
 
     rows_j = lax.broadcasted_iota(jnp.int32, (PACKED, PACKED), 0)
     rows_i = lax.broadcasted_iota(jnp.int32, (PACKED, PACKED), 1)
-    allowed = (tag_ref[0:1, :] == code_ref[...]) | (rows_j == rows_i)
+    facts = normed_s[owner, :, WIDE:].astype(F32)
+    codes = jnp.where(facts[:, 1:2] > 0.5, facts[:, 0:1], -1.0)
+    allowed = (facts.T[0:1, :] == codes) | (rows_j == rows_i)
     ones_rows = jnp.where(lax.broadcasted_iota(jnp.int32, (32, PACKED), 0) < 2, 1.0, 0.0)
 
     for h in range(FOCI):
@@ -209,19 +237,15 @@
     context_ref[...] = mixed_ref[...].T.astype(BF16).reshape(context_ref.shape)
 
 
-def forward(core, soft, tags, codes, mine, other, whole):
+def forward(core, soft, mine, other, whole):
     anywhere = pl.BlockSpec(memory_space=pl.ANY)
     grid = pltpu.PrefetchScalarGridSpec(
         num_scalar_prefetch=1,
         grid=(2,),
         in_specs=[
             pl.BlockSpec(memory_space=SMEM),
-            pl.BlockSpec((None, 8, PACKED), lambda o, c: (o, 0, 0)),
-            pl.BlockSpec((None, PACKED, 1), lambda o, c: (o, 0, 0)),
-            anywhere,
-            anywhere,
-            anywhere,
-        ],
+        ]
+        + [anywhere] * 3,
         out_specs=[
             pl.BlockSpec((OWNERS, None, SLOTS * LEN, HALF), lambda o, c: (0, o, 0, 0)),
             pl.BlockSpec((None, FOCI, PACKED, PACKED), lambda o, c: (o, 0, 0, 0)),
@@ -231,7 +255,7 @@
             pl.BlockSpec((None, 8, PACKED), lambda o, c: (o, 0, 0)),
         ],
         scratch_shapes=[
-            pltpu.VMEM((2, PACKED, WIDE), BF16),
+            pltpu.VMEM((2, PACKED, WIDE + FACTS), BF16),
             pltpu.VMEM((WIDE, QKVL), BF16),
             pltpu.VMEM((WIDE // 2, 2 * RANK), BF16),
             pltpu.VMEM((PACKED, QKVL), F32),
@@ -258,7 +282,7 @@
             flops=6 << 30, bytes_accessed=16 << 20, transcendentals=2 * FOCI * PACKED * PACKED
         ),
         name="forward",
-    )(core, soft, tags, codes, mine, other, whole)
+    )(core, soft, mine, other, whole)
 
 
 def backward_kernel(
@@ -274,6 +298,7 @@
     masked_mine_ref,
     masked_other_ref,
     whole_ref,
+    out_other_ref,
     keep_ref,
     send_ref,
     up_ref,
@@ -288,43 +313,50 @@
     up_s,
     row_sems,
     masked_sems,
-    out_sem,
+    out_sems,
     raise_sem,
 ):
     owner = pl.program_id(0)
     core = core_ref[0]
-    rows = owner_copies((mine_ref, other_ref), normed_s, row_sems)
+    body = pl.ds(0, WIDE)
+    rows = owner_copies((mine_ref.at[:, body], other_ref.at[:, body]), normed_s, row_sems)
     masks = owner_copies((masked_mine_ref, masked_other_ref), masked_s, masked_sems)
     half = pl.ds(pl.multiple_of(core * (WIDE // 2), WIDE // 2), WIDE // 2)
-    outs = pltpu.make_async_copy(whole_ref.at[half, pl.ds(0, HIDDEN)], out_s, out_sem)
     raises = pltpu.make_async_copy(
-        whole_ref.at[half, pl.ds(HIDDEN + QKVL, 2 * RANK)], raise_s, raise_sem
+        whole_ref.at[half, pl.ds(QKVL, 2 * RANK)], raise_s, raise_sem
+    )
+    outs = owner_copies(
+        (whole_ref.at[half, pl.ds(QKVL + 2 * RANK, QUARTER)], out_other_ref.at[half, :]),
+        out_s,
+        out_sems,
     )
 
     @pl.when(owner == 0)
     def _():
-        outs.start()
         masks[0].start()
+        outs[0].start()
+        outs[1].start()
         rows[0].start()
         raises.start()
         masks[1].start()
         rows[1].start()
         down_s[...] = jnp.zeros_like(down_s)
         up_s[...] = jnp.zeros_like(up_s)
-        outs.wait()
         masks[0].wait()
+        outs[0].wait()
+        outs[1].wait()
 
     @pl.when(owner == 1)
     def _():
         masks[1].wait()
 
-    sides = []
-    for side in range(2):
-        columns = slice(side * WIDE // 2, (side + 1) * WIDE // 2)
-        both = dot_nt(out_s[...], masked_s[owner, :, columns])
-        both = both.reshape(SHARDS // 2, BLOCK, PACKED)
-        sides.append(both[:, side * UPS : (side + 1) * UPS])
-    cot_s[...] = (sides[0] + sides[1]).reshape(HALF, PACKED).astype(BF16).astype(F32)
+    total = jnp.zeros((SHARDS // 2, UPS, PACKED), F32)
+    for n, side in enumerate((core, 1 - core)):
+        for q in range(2):
+            first = pl.multiple_of(side * (WIDE // 2) + q * QUARTER, QUARTER)
+            both = dot_nt(out_s[n], masked_s[owner, :, pl.ds(first, QUARTER)])
+            total = total + both.reshape(SHARDS // 2, BLOCK, PACKED)[:, q * UPS : (q + 1) * UPS]
+    cot_s[...] = total.reshape(HALF, PACKED).astype(BF16).astype(F32)
 
     ones_rows = jnp.where(lax.broadcasted_iota(jnp.int32, (32, PACKED), 0) < 2, 1.0, 0.0)
     sub = lax.broadcasted_iota(jnp.int32, (32, PACKED), 0)
@@ -378,7 +410,7 @@
         up_ref[...] = up_s[...]
 
 
-def backward(core, soft, saved, normed, masked, whole):
+def backward(core, soft, saved, normed, masked, whole, out_other):
     anywhere = pl.BlockSpec(memory_space=pl.ANY)
     grid = pltpu.PrefetchScalarGridSpec(
         num_scalar_prefetch=1,
@@ -391,7 +423,7 @@
             pl.BlockSpec((None, HALF, PACKED), lambda o, c: (o, 0, 0)),
             pl.BlockSpec((None, 8, PACKED), lambda o, c: (o, 0, 0)),
         ]
-        + [anywhere] * 5,
+        + [anywhere] * 6,
         out_specs=[
             pl.BlockSpec((SHARDS * UPS, 2 * RANK), lambda o, c: (0, 0)),
             pl.BlockSpec((SHARDS * UPS, 2 * RANK), lambda o, c: (0, 0)),
@@ -400,7 +432,7 @@
         scratch_shapes=[
             pltpu.VMEM((2, PACKED, WIDE), BF16),
             pltpu.VMEM((2, PACKED, WIDE), BF16),
-            pltpu.VMEM((WIDE // 2, HIDDEN), BF16),
+            pltpu.VMEM((2, WIDE // 2, QUARTER), BF16),
             pltpu.VMEM((WIDE // 2, 2 * RANK), BF16),
             pltpu.VMEM((HALF, PACKED), F32),
             pltpu.VMEM((HALF, PACKED), BF16),
@@ -409,7 +441,7 @@
             pltpu.VMEM((HALF, 2 * RANK), F32),
             pltpu.SemaphoreType.DMA((2,)),
             pltpu.SemaphoreType.DMA((2,)),
-            pltpu.SemaphoreType.DMA,
+            pltpu.SemaphoreType.DMA((2,)),
             pltpu.SemaphoreType.DMA,
         ],
     )
@@ -426,7 +458,7 @@
         ),
         cost_estimate=pl.CostEstimate(flops=8 << 30, bytes_accessed=16 << 20, transcendentals=0),
         name="backward",
-    )(core, soft, *saved, *normed, *masked, whole)
+    )(core, soft, *saved, *normed, *masked, whole, out_other)
 
 
 def combine_kernel(core_ref, keep_ref, come_ref, up_ref, parts_ref):
@@ -446,11 +478,14 @@
         out_shape=jax.ShapeDtypeStruct((SHARDS * GRAD, 2 * RANK), BF16),
         in_specs=[pl.BlockSpec(memory_space=SMEM)] + [pl.BlockSpec(memory_space=VMEM)] * 3,
         out_specs=pl.BlockSpec(memory_space=VMEM),
+        compiler_params=pltpu.CompilerParams(vmem_limit_bytes=8 << 20),
         name="combine",
     )(core, keep, come, up)
 
 
-def finish_kernel(owner_ref, live_ref, context_ref, x_ref, out_a_ref, out_b_ref, block_ref):
+def finish_kernel(core_ref, owner_ref, live_ref, context_ref, x_ref, *refs):
+    *out_refs, block_ref = refs
+    core = core_ref[0]
     place, step = spread(slot_places(owner_ref), (ROWS, 1), 0)
     target = place * LEN + step
     slots = lax.broadcasted_iota(jnp.int32, (ROWS, PACKED), 1)
@@ -464,25 +499,27 @@
             first = 0 if source == o else SLOTS * LEN
             parts.append(context_ref[source, first : first + SLOTS * LEN, :])
         halves.append(dot(select, jnp.concatenate(parts, axis=0)).astype(BF16))
-    for side, ref in enumerate((out_a_ref, out_b_ref)):
-        columns = slice(side * WIDE // 2, (side + 1) * WIDE // 2)
+    for n, ref in enumerate(out_refs):
+        side = core if n < 2 else 1 - core
+        first = pl.multiple_of(side * (WIDE // 2) + n % 2 * QUARTER, QUARTER)
+        columns = pl.ds(first, QUARTER)
         attended = dot(halves[0], ref[:HALF, :]) + dot(halves[1], ref[HALF:, :])
         added = jnp.where(step < lives, attended, 0.0)
         block_ref[:, columns] = (x_ref[:, columns].astype(F32) + added).astype(BF16)
 
 
-def finish(owners, lives, context, x, out_a, out_b):
+def finish(core, owners, lives, context, x, outs):
     return pl.pallas_call(
         finish_kernel,
         out_shape=jax.ShapeDtypeStruct((ROWS, WIDE), BF16),
-        in_specs=[pl.BlockSpec(memory_space=SMEM)] * 2 + [pl.BlockSpec(memory_space=VMEM)] * 4,
+        in_specs=[pl.BlockSpec(memory_space=SMEM)] * 3 + [pl.BlockSpec(memory_space=VMEM)] * 6,
         out_specs=pl.BlockSpec(memory_space=VMEM),
         compiler_params=pltpu.CompilerParams(vmem_limit_bytes=40 << 20),
         cost_estimate=pl.CostEstimate(
             flops=2 * ROWS * 2 * HALF * (WIDE + PACKED), bytes_accessed=6 << 20, transcendentals=0
         ),
         name="finish",
-    )(owners, lives, context, x, out_a, out_b)
+    )(core, owners, lives, context, x, *outs)
 
 
 def add_shards_kernel(part_ref, total_ref):
@@ -500,6 +537,7 @@
         out_shape=jax.ShapeDtypeStruct((OWNERS, GRAD, 2 * RANK), BF16),
         in_specs=[pl.BlockSpec(memory_space=VMEM)],
         out_specs=pl.BlockSpec(memory_space=VMEM),
+        compiler_params=pltpu.CompilerParams(vmem_limit_bytes=8 << 20),
         name="add_shards",
     )(parts)
 
@@ -526,6 +564,7 @@
         ),
         in_specs=[pl.BlockSpec(memory_space=VMEM)],
         out_specs=(pl.BlockSpec(memory_space=VMEM),) * 2,
+        compiler_params=pltpu.CompilerParams(vmem_limit_bytes=8 << 20),
         name="add_owners",
     )(parts)
 
@@ -537,26 +576,6 @@
 def swap_cores(data):
     pairs = [(s, s ^ 1) for s in range(OWNERS)]
     return lax.ppermute(data, "seq", pairs)
-
-
-def packed_facts(owners, tags, lives):
-    same = owners[:, None] == owners[None, :]
-    order = jnp.arange(PANELS, dtype=jnp.int32)
-    rank = jnp.sum((same & (order[:, None] > order[None, :])).astype(jnp.int32), axis=1)
-    place = owners * SLOTS + rank
-    hits = place[None, :] == jnp.arange(OWNERS * SLOTS, dtype=jnp.int32)[:, None]
-    facts = [jnp.sum(jnp.where(hits, fact[None, :], 0), axis=1) for fact in (tags, lives)]
-    sent = jnp.stack(facts, axis=-1).astype(BF16).reshape(OWNERS // 2, 2, SLOTS * 2)
-    return jnp.stack([sent, sent[:, ::-1]], axis=2).reshape(OWNERS, 2, SLOTS, 2)
-
-
-def row_facts(received):
-    received = jnp.swapaxes(received.astype(F32), 0, 1).reshape(2, OWNERS * SLOTS, 1, 2)
-    steps = jnp.arange(LEN, dtype=jnp.int32).astype(F32)[None, None, :]
-    tag = jnp.broadcast_to(received[..., 0], (2, OWNERS * SLOTS, LEN))
-    code = jnp.where(steps < received[..., 1], tag, -1.0)
-    rows = jnp.broadcast_to(tag.reshape(2, 1, PACKED), (2, 8, PACKED))
-    return rows, code.reshape(2, PACKED, 1)
 
 
 def on_device(
@@ -573,54 +592,55 @@
     result_adjoint,
 ):
     core = lax.axis_index("seq") % 2
+    def own(left, right):
+        return jnp.where(core == 0, left, right)
+
     starts = [n * 2 * HALF for n in range(3)]
     triple = [
-        jnp.where(
-            core == 0,
+        own(
             triple_projector[:, first : first + HALF],
             triple_projector[:, first + HALF : first + 2 * HALF],
         )
         for first in starts
     ]
-    lowered = jnp.concatenate([lowered_maps[0], lowered_maps[1]], axis=1)
-    outward = jnp.concatenate([final_projector[:, : WIDE // 2], final_projector[:, WIDE // 2 :]], axis=0)
     raising = raising_maps.reshape(2 * RANK, UPS).T
     raising = jnp.concatenate([raising, jnp.zeros_like(raising)], axis=0)
-    shard = jnp.concatenate([outward, *triple, lowered, raising], axis=1)
+    quarters = [final_projector[:, n * QUARTER : (n + 1) * QUARTER] for n in range(4)]
+    outward = jnp.concatenate([own(quarters[0], quarters[2]), own(quarters[1], quarters[3])], axis=0)
+    shard = jnp.concatenate([*triple, lowered_maps[0], lowered_maps[1], raising, outward], axis=1)
     whole = lax.all_gather(shard, "dp", axis=0, tiled=True)
 
     x = encoder_timesteps.reshape(ROWS, WIDE)
-    facts = exchange(
-        packed_facts(tile_parent_sequence, tile_recording_label, tile_valid_timesteps), "seq"
-    )
-    normed, masked = pack(
+    packed = pack(
         tile_parent_sequence,
+        tile_recording_label,
         tile_valid_timesteps,
         x,
-        result_adjoint.reshape(ROWS, WIDE),
         standardize_scaling.reshape(1, WIDE),
     )
-    normed, facts = lax.optimization_barrier((normed, facts))
-    tag_rows, codes = row_facts(facts)
-    normed = exchange(normed, "seq")
-    normed, masked = lax.optimization_barrier((normed, masked))
+    packed, adjoint = lax.optimization_barrier((packed, result_adjoint.reshape(ROWS, WIDE)))
+    masked = pack_masked(tile_parent_sequence, tile_valid_timesteps, adjoint)
+    packed = exchange(packed, "seq")
+    packed, masked = lax.optimization_barrier((packed, masked))
     masked = exchange(masked, "seq")
-    flat = (PACKED, WIDE)
-    normed = (normed.reshape(flat), swap_cores(normed).reshape(flat))
-    masked = (masked.reshape(flat), swap_cores(masked).reshape(flat))
+    normed = [part.reshape(PACKED, WIDE + FACTS) for part in (packed, swap_cores(packed))]
+    masked = [part.reshape(PACKED, WIDE) for part in (masked, swap_cores(masked))]
 
     core = core.reshape(1)
-    context, *saved = forward(core, focus_softness, tag_rows, codes, *normed, whole)
-    whole, context = lax.optimization_barrier((whole, context))
-    keep, send, up = backward(core, focus_softness, saved, normed, masked, whole)
+    out_own = whole[:, QKVL + 2 * RANK :]
+    out_other = swap_cores(out_own)
+    context, *saved = forward(core, focus_softness, *normed, whole)
+    out_own, out_later, context = lax.optimization_barrier((out_own, out_other, context))
+    keep, send, up = backward(core, focus_softness, saved, normed, masked, whole, out_other)
     context = exchange(context.reshape(OWNERS, 2 * SLOTS * LEN, HALF), "seq")
     parts = combine(core, keep, swap_cores(send), up)
-    outs = whole.reshape(SHARDS, BLOCK, -1)[:, :, :HIDDEN]
-    out_a = outs[:, :UPS].reshape(HIDDEN, WIDE // 2)
-    out_b = outs[:, UPS:].reshape(HIDDEN, WIDE // 2)
+    outs = []
+    for part in (out_own, out_later):
+        part = part.reshape(SHARDS, BLOCK, QUARTER)
+        outs += [part[:, :UPS].reshape(HIDDEN, QUARTER), part[:, UPS:].reshape(HIDDEN, QUARTER)]
     parts, context = lax.optimization_barrier((parts, context))
     parts = exchange(parts.reshape(SHARDS, GRAD, 2 * RANK), "dp")
-    block_out = finish(tile_parent_sequence, tile_valid_timesteps, context, x, out_a, out_b)
+    block_out = finish(core, tile_parent_sequence, tile_valid_timesteps, context, x, outs)
     shard_down, shard_up = add_owners(exchange(add_shards(parts), "seq"))
     return block_out.reshape(encoder_timesteps.shape), shard_down, jnp.swapaxes(shard_up, 1, 2)
 

time: 220 us -> 208 us (0.945)
  blocking collectives: 66.7 us -> 18.8 us
  waiting for transfers between devices: 47.2 us -> 78.3 us
  starting transfers between devices: 33 us -> 39.7 us
    all_to_all x2 -> x1, blocking collectives: 66.7 us -> 18.8 us  [exchange(): return lax.all_to_all(data, axis, split_axis=0, concat_axis=0, tiled=True)]
    all_gather x1, waiting for transfers between devices: 0.02 us -> 29.9 us  [on_device(): whole = lax.all_gather(shard, 'dp', axis=0, tiled=True)]
    ppermute x3 -> x4, starting transfers between devices: 5.83 us -> 10.6 us  [swap_cores(): return lax.ppermute(data, 'seq', pairs)]
    slice x3, local copies, waits for them, and re-layouts: 2.67 us -> 5.15 us  [the longest x2 2.74 us: on_device(): part[:, UPS:].reshape(HIDDEN, QUARTER)]
    pallas_call x1 -> x2, Pallas kernels: 3.21 us -> 5.33 us  [the longest x1 2.89 us: pack(): pl.pallas_call(pack_kernel, out_shape=jax.ShapeDtypeStruct((OWNERS, SLOTS...]
    unnamed x27 -> x23, local copies, waits for them, and re-layouts: 6.17 us -> 5.32 us
  transfers between devices with their start and end apart: 8 -> 9, of which waited for: 5 -> 5; matrix products, arithmetic and copies ran while one was open for 3% -> 3% of each run, Pallas kernels for 17% -> 19%
where the time goes in v3:
time: 208 us; the launch traced here: 207 us
  waiting for transfers between devices  78.3 us (38%)
  Pallas kernels  41.5 us (20%)
  starting transfers between devices  39.7 us (19%)
  blocking collectives  18.8 us (9%)
  between operations  14.2 us (7%)
  local copies, waits for them, and re-layouts  12.8 us (6%)
    all_to_all x4, waiting for transfers between devices, exchange(): return lax.all_to_all(data, axis, split_axis=0, concat_axis=0, tiled=True)  47.1 us
    all_gather x1, waiting for transfers between devices, on_device(): whole = lax.all_gather(shard, 'dp', axis=0, tiled=True)  29.9 us
    all_to_all x4, starting transfers between devices, exchange(): return lax.all_to_all(data, axis, split_axis=0, concat_axis=0, tiled=True)  29 us
    all_to_all x1, blocking collectives, exchange(): return lax.all_to_all(data, axis, split_axis=0, concat_axis=0, tiled=True)  18.8 us
    pallas_call x1, Pallas kernels, forward(): pl.pallas_call(forward_kernel, grid_spec=grid, out_shape=(jax.ShapeDtypeS...  17.7 us
    pallas_call x1, Pallas kernels, backward(): pl.pallas_call(backward_kernel, grid_spec=grid, out_shape=(jax.ShapeDtype...  13.9 us
    ppermute x4, starting transfers between devices, swap_cores(): return lax.ppermute(data, 'seq', pairs)  10.6 us
    unnamed x23, local copies, waits for them, and re-layouts  5.32 us
  transfers between devices with their start and end apart: 9, of which 5 were waited for; matrix products, arithmetic and copies ran while one was open for 3% of the time, Pallas kernels for 19%

profile of v3, /device:TPU:1, one launch (start us, length us, event | category | flops | bytes accessed | tf_op | source)
XLA Modules:
  0.0 206.9 jit_solution(15914090910289550755)
XLA Ops:
  14.0 2.9 %pack.1 = bf16[16,32,1664]{2,1,0:T(8,128)(2,1)} custom-call(s32[16]{0:T(128)S(1)} %copy-done.3, s32[16]{0:T(128)S(1)} %copy-done.7, s32[16]{0:T(128)S(1)} %copy-done.5, bf16[256,1536]{1,0:T(8,128)(2,1)S(1)} %bitcast.24, f32[1,1536]{1,0:T(1,128)S(1)} %reshape.62.gain_ref), custom_call_target="tpu_custom_call" | custom-call | flops 402653184 | bytes 3145728 | tf_op jit(solution)/shard_map/pack/pallas_call | solution.py:84
  16.9 12.0 %all-to-all-start = ((bf16[16,32,1664]{2,1,0:T(8,128)(2,1)}), bf16[16,32,1664]{2,1,0:T(8,128)(2,1)S(1)}, u32[]{:S(2)}, u32[]{:S(2)}) async-start(bf16[16,32,1664]{2,1,0:T(8,128)(2,1)} %pack.1), calls=%async_computation | async-start | bytes 3407872 | tf_op jit(solution)/shard_map/all_to_all | solution.py:573
  28.9 2.4 %pack_masked.1 = bf16[16,32,1536]{2,1,0:T(8,128)(2,1)} custom-call(s32[16]{0:T(128)S(1)} %copy-done.4, s32[16]{0:T(128)S(1)} %copy-done.6, bf16[256,1536]{1,0:T(8,128)(2,1)S(1)} %bitcast.33), custom_call_target="tpu_custom_call" | custom-call | flops 402653184 | bytes 3145728 | tf_op jit(solution)/shard_map/pack_masked/pallas_call | solution.py:108
  31.3 38.6 %all-to-all-done = bf16[16,32,1664]{2,1,0:T(8,128)(2,1)S(1)} async-done(((bf16[16,32,1664]{2,1,0:T(8,128)(2,1)}), bf16[16,32,1664]{2,1,0:T(8,128)(2,1)S(1)}, u32[]{:S(2)}, u32[]{:S(2)}) %all-to-all-start) | async-done | bytes 1703968 | tf_op jit(solution)/shard_map/all_to_all | solution.py:573
  69.9 4.4 %all-to-all-start.1 = ((bf16[16,32,1536]{2,1,0:T(8,128)(2,1)}), bf16[16,32,1536]{2,1,0:T(8,128)(2,1)}, u32[]{:S(2)}, u32[]{:S(2)}) async-start(bf16[16,32,1536]{2,1,0:T(8,128)(2,1)} %pack_masked.1), calls=%async_computation.1 | async-start | bytes 3145728 | tf_op jit(solution)/shard_map/all_to_all | solution.py:573
  74.3 2.1 collective-permute-start
  76.4 29.9 %all-gather.2.cloned.1.call-done.whole_ref = bf16[1536,1792]{1,0:T(8,128)(2,1)} async-done(((bf16[48,1792]{1,0:T(8,128)(2,1)}), bf16[1536,1792]{1,0:T(8,128)(2,1)}) %all-gather.2.cloned.1.call-update) | async-done | bytes 5505040 | tf_op jit(solution)/shard_map/all_gather | solution.py:611
  106.3 2.4 %slice.68 = bf16[1536,384]{1,0:T(8,128)(2,1)} slice(bf16[1536,1792]{1,0:T(8,128)(2,1)} %all-gather.2.cloned.1.call-done.whole_ref), slice={[0:1536], [1408:1792]} | slice | bytes 2359296 | tf_op jit(solution)/shard_map/slice | solution.py:630
  108.7 4.6 %collective-permute-start.2 = (bf16[1536,384]{1,0:T(8,128)(2,1)}, bf16[1536,384]{1,0:T(8,128)(2,1)}, u32[]{:S(2)}, u32[]{:S(2)}) collective-permute-start(bf16[1536,384]{1,0:T(8,128)(2,1)} %slice.68), channel_id=1, source_target_pairs={{0,1},{1,0},{2,3},{3,2},{4,5},{5,4},{6,7},{7,6},{8,9},{9,8},{10,11... | collective-permute-start | bytes 3538952 | tf_op jit(solution)/shard_map/ppermute | solution.py:578
  113.4 1.9 collective-permute-start.1
  115.3 17.7 %forward.1 = (bf16[16,2,32,384]{3,2,1,0:T(8,128)(2,1)}, bf16[2,4,512,512]{3,2,1,0:T(8,128)(2,1)}, bf16[2,1152,512]{2,1,0:T(8,128)(2,1)}, bf16[2,512,128]{2,1,0:T...) custom-call(s32[1]{0:T(128)} %bitcast.core_ref, f32[8]{0:T(128)S(1)} %copy-done.8, ...), custom_call_target="tpu_custom_call" | custom-call | flops 6442450944 | bytes 16777216 | tf_op jit(solution)/shard_map/forward/pallas_call | solution.py:267
  133.1 1.2 copy-done.9
  134.2 7.9 %all-to-all-start.2 = ((bf16[16,64,384]{2,1,0:T(8,128)(2,1)}), bf16[16,64,384]{2,1,0:T(8,128)(2,1)S(1)}, u32[]{:S(2)}, u32[]{:S(2)}) async-start(bf16[16,64,384]{2,1,0:T(8,128)(2,1)} %bitcast.10), calls=%async_computation.2 | async-start | bytes 1572864 | tf_op jit(solution)/shard_map/all_to_all | solution.py:573
  142.1 1.4 copy-done.10
  143.5 13.9 %backward.1 = (f32[768,128]{1,0:T(8,128)S(1)}, bf16[768,128]{1,0:T(8,128)(2,1)S(1)}, f32[384,128]{1,0:T(8,128)S(1)}) custom-call(s32[1]{0:T(128)} %bitcast.core_ref, f32[8]{0:T(128)S(1)} %copy-done.8, bf16[2,4,512,512]{3,2,1,0:T(8,128)(2,1)} %get-tuple-element.26.weights_ref, bf16[2,1152,512]{2,1,0:T(8,128)(2,1)} %get-tuple-element.27.qkv_ref, ...), custom_call_target="tpu_custom_call" | custom-call | flops 8589934592 | bytes 16777216 | tf_op jit(solution)/shard_map/backward/pallas_call | solution.py:448
  157.4 2.0 collective-permute-start.3
  159.5 1.3 collective-permute-done.3.come_ref
  160.8 4.0 %all-to-all-done.2.context_ref = bf16[16,64,384]{2,1,0:T(8,128)(2,1)S(1)} async-done(((bf16[16,64,384]{2,1,0:T(8,128)(2,1)}), bf16[16,64,384]{2,1,0:T(8,128)(2,1)S(1)}, u32[]{:S(2)}, u32[]{:S(2)}) %all-to-all-start.2) | async-done | bytes 786464 | tf_op jit(solution)/shard_map/all_to_all | solution.py:573
  164.8 18.8 %all_to_all.25.part_ref = bf16[32,48,128]{2,1,0:T(8,128)(2,1)S(1)} all-to-all(bf16[32,48,128]{2,1,0:T(8,128)(2,1)S(1)} %bitcast.32), channel_id=1, replica_groups=mesh['dp'=32,'seq'=16] {'dp'}, dimensions={0} | all-to-all | bytes 786432 | tf_op jit(solution)/shard_map/all_to_all | solution.py:573
  184.3 4.7 %all-to-all-start.4 = ((bf16[16,48,128]{2,1,0:T(8,128)(2,1)}), bf16[16,48,128]{2,1,0:T(8,128)(2,1)S(1)}, u32[]{:S(2)}, u32[]{:S(2)}) async-start(bf16[16,48,128]{2,1,0:T(8,128)(2,1)} %add_shards.1), calls=%async_computation.4 | async-start | bytes 393216 | tf_op jit(solution)/shard_map/all_to_all | solution.py:573
  189.0 1.4 fusion.1
  190.4 1.4 fusion
  191.7 3.1 %finish.1 = bf16[256,1536]{1,0:T(8,128)(2,1)} custom-call(s32[1]{0:T(128)} %bitcast.core_ref, s32[16]{0:T(128)S(1)} %copy-done.4, s32[16]{0:T(128)S(1)} %copy-done.6, bf16[16,64,384]{2,1,0:T(8,128)(2,1)S(1)} %all-to-all-done.2.context_ref, bf16[256,1536]{1,0:T(8,128)(2,1)S(1)} %bitcast.25, bf16[768,384]{1,0:T(8,128)(2,1)S(1)} %bitcast.27, ...), custom_call_target="tpu_custom_call" | custom-call | flops 805306368 | bytes 6291456 | tf_op jit(solution)/shard_map/finish/pallas_call | solution.py:512
  194.8 4.5 %all-to-all-done.4.part_ref = bf16[16,48,128]{2,1,0:T(8,128)(2,1)S(1)} async-done(((bf16[16,48,128]{2,1,0:T(8,128)(2,1)}), bf16[16,48,128]{2,1,0:T(8,128)(2,1)S(1)}, u32[]{:S(2)}, u32[]{:S(2)}) %all-to-all-start.4) | async-done | bytes 196640 | tf_op jit(solution)/shard_map/all_to_all | solution.py:573
  (37 shorter events, 8.3 us)
Async XLA Ops:
  7.2 4.8 %copy-start = (bf16[16,16,1536]{2,1,0:T(8,128)(2,1)S(1)}, bf16[16,16,1536]{2,1,0:T(8,128)(2,1)}, u32[]{:S(2)}) copy-start(bf16[16,16,1536]{2,1,0:T(8,128)(2,1)} %param.11) | copy-start | bytes 2359300
  7.2 99.1 %all-gather.2.cloned.1.call-start = ((), (), s32[]{:S(2)}) async-start(), calls=%async_computation.5 | async-start | bytes 5677056 | tf_op jit(solution)/shard_map/all_gather | solution.py:611
  12.0 0.7 copy-start.3
  12.7 0.7 copy-start.5
  13.3 0.7 copy-start.7
  16.9 12.0 %copy-start.2 = (bf16[16,16,1536]{2,1,0:T(8,128)(2,1)S(1)}, bf16[16,16,1536]{2,1,0:T(8,128)(2,1)}, u32[]{:S(2)}) copy-start(bf16[16,16,1536]{2,1,0:T(8,128)(2,1)} %param.21) | copy-start | bytes 2359300
  16.9 12.0 %copy-start.4 = (s32[16]{0:T(128)S(1)}, s32[16]{0:T(128)}, u32[]{:S(2)}) copy-start(s32[16]{0:T(128)} %owner_ref.5) | copy-start | bytes 196
  16.9 12.0 %copy-start.6 = (s32[16]{0:T(128)S(1)}, s32[16]{0:T(128)}, u32[]{:S(2)}) copy-start(s32[16]{0:T(128)} %live_ref.5) | copy-start | bytes 196
  16.9 53.0 %all-to-all-start = ((bf16[16,32,1664]{2,1,0:T(8,128)(2,1)}), bf16[16,32,1664]{2,1,0:T(8,128)(2,1)S(1)}, u32[]{:S(2)}, u32[]{:S(2)}) async-start(bf16[16,32,1664]{2,1,0:T(8,128)(2,1)} %pack.1), calls=%async_computation | async-start | bytes 3407872 | tf_op jit(solution)/shard_map/all_to_all | solution.py:573
  69.9 45.4 %copy-start.1 = (bf16[16,32,1664]{2,1,0:T(8,128)(2,1)}, bf16[16,32,1664]{2,1,0:T(8,128)(2,1)S(1)}, u32[]{:S(2)}) copy-start(bf16[16,32,1664]{2,1,0:T(8,128)(2,1)S(1)} %all-to-all-done) | copy-start | bytes 5111812
  69.9 43.5 %all-to-all-start.1 = ((bf16[16,32,1536]{2,1,0:T(8,128)(2,1)}), bf16[16,32,1536]{2,1,0:T(8,128)(2,1)}, u32[]{:S(2)}, u32[]{:S(2)}) async-start(bf16[16,32,1536]{2,1,0:T(8,128)(2,1)} %pack_masked.1), calls=%async_computation.1 | async-start | bytes 3145728 | tf_op jit(solution)/shard_map/all_to_all | solution.py:573
  74.3 41.0 %copy-start.8 = (f32[8]{0:T(128)S(1)}, f32[8]{0:T(128)}, u32[]{:S(2)}) copy-start(f32[8]{0:T(128)} %soft_ref.3) | copy-start | bytes 100
  74.3 41.0 %collective-permute-start = (bf16[16,32,1664]{2,1,0:T(8,128)(2,1)S(1)}, bf16[16,32,1664]{2,1,0:T(8,128)(2,1)}, u32[]{:S(2)}, u32[]{:S(2)}) collective-permute-start(bf16[16,32,1664]{2,1,0:T(8,128)(2,1)S(1)} %all-to-all-done), channel_id=1, source_target_pairs={{0,1},{1,0},{2,3},{3,2},{4,5},{5,4},{6,7},{7,6},{8,9},{9,8},{10,11... | collective-permute-start | bytes 5111816 | tf_op jit(solution)/shard_map/ppermute | solution.py:578
  108.7 25.5 %collective-permute-start.2 = (bf16[1536,384]{1,0:T(8,128)(2,1)}, bf16[1536,384]{1,0:T(8,128)(2,1)}, u32[]{:S(2)}, u32[]{:S(2)}) collective-permute-start(bf16[1536,384]{1,0:T(8,128)(2,1)} %slice.68), channel_id=1, source_target_pairs={{0,1},{1,0},{2,3},{3,2},{4,5},{5,4},{6,7},{7,6},{8,9},{9,8},{10,11... | collective-permute-start | bytes 3538952 | tf_op jit(solution)/shard_map/ppermute | solution.py:578
  113.4 28.8 %collective-permute-start.1 = (bf16[16,32,1536]{2,1,0:T(8,128)(2,1)}, bf16[16,32,1536]{2,1,0:T(8,128)(2,1)}, u32[]{:S(2)}, u32[]{:S(2)}) collective-permute-start(bf16[16,32,1536]{2,1,0:T(8,128)(2,1)} %all-to-all-done.1), channel_id=1, source_target_pairs={{0,1},{1,0},{2,3},{3,2},{4,5},{5,4},{6,7},{7,6},{8,9},{9,8},{10,11... | collective-permute-start | bytes 4718600 | tf_op jit(solution)/shard_map/ppermute | solution.py:578
  133.1 1.2 copy-start.9
  134.2 30.5 %all-to-all-start.2 = ((bf16[16,64,384]{2,1,0:T(8,128)(2,1)}), bf16[16,64,384]{2,1,0:T(8,128)(2,1)S(1)}, u32[]{:S(2)}, u32[]{:S(2)}) async-start(bf16[16,64,384]{2,1,0:T(8,128)(2,1)} %bitcast.10), calls=%async_computation.2 | async-start | bytes 1572864 | tf_op jit(solution)/shard_map/all_to_all | solution.py:573
  142.1 1.4 copy-start.10
  157.4 3.3 %collective-permute-start.3 = (bf16[768,128]{1,0:T(8,128)(2,1)S(1)}, bf16[768,128]{1,0:T(8,128)(2,1)S(1)}, u32[]{:S(2)}, u32[]{:S(2)}) collective-permute-start(bf16[768,128]{1,0:T(8,128)(2,1)S(1)} %get-tuple-element.33), channel_id=1, source_target_pairs={{0,1},{1,0},{2,3},{3,2},{4,5},{5,4},{6,7},{7,6},{8,9},{9,8},{10,11... | collective-permute-start | bytes 589832 | tf_op jit(solution)/shard_map/ppermute | solution.py:578
  184.3 15.1 %all-to-all-start.4 = ((bf16[16,48,128]{2,1,0:T(8,128)(2,1)}), bf16[16,48,128]{2,1,0:T(8,128)(2,1)S(1)}, u32[]{:S(2)}, u32[]{:S(2)}) async-start(bf16[16,48,128]{2,1,0:T(8,128)(2,1)} %add_shards.1), calls=%async_computation.4 | async-start | bytes 393216 | tf_op jit(solution)/shard_map/all_to_all | solution.py:573
Sparse Core Ops, SparseCore 0:
  11.7 94.5 all-gather.1

commit v4 on v3

--- a/solution.py
+++ b/solution.py
@@ -25,8 +25,11 @@
 UPS = 2 * HALF // SHARDS
 GRAD = 2 * UPS
 HIDDEN = 2 * HALF
-QUARTER = WIDE // 4
 FACTS = 128
+X_SIZE = 4
+Y_SIZE = 8
+X_TURNS = (0, -1, 1, 2)
+Y_TURNS = (0, -1, 1, -2, 2, -3, 3)
 QKVL = 3 * HALF + 2 * RANK
 F32 = jnp.float32
 BF16 = jnp.bfloat16
@@ -94,28 +97,93 @@
     )(owners, tags, lives, x, gain)
 
 
-def pack_masked_kernel(owner_ref, live_ref, adjoint_ref, packed_ref):
+def cotangent_kernel(
+    core_ref,
+    owner_ref,
+    live_ref,
+    adjoint_ref,
+    block_0_ref,
+    block_1_ref,
+    block_2_ref,
+    block_3_ref,
+    block_4_ref,
+    block_5_ref,
+    block_6_ref,
+    far_a_ref,
+    far_b_ref,
+    packed_ref,
+    out_a_ref,
+    out_b_ref,
+    whole_s,
+    piece_sems,
+):
+    place_x, place_y = core_ref[1], core_ref[2]
+    blocks = (block_0_ref, block_1_ref, block_2_ref, block_3_ref, block_4_ref, block_5_ref, block_6_ref)
+    sources = [
+        (blocks[j], i * BLOCK, dx, dy)
+        for j, dy in enumerate(Y_TURNS)
+        for i, dx in enumerate(X_TURNS)
+    ]
+    sources += [(far_a_ref, i * BLOCK, X_TURNS[i], Y_SIZE // 2) for i in range(2)]
+    sources += [(far_b_ref, i * BLOCK, X_TURNS[2 + i], Y_SIZE // 2) for i in range(2)]
+    pieces = []
+    for n, (source, first, dx, dy) in enumerate(sources):
+        shard = lax.rem(place_x + dx + X_SIZE, X_SIZE) * Y_SIZE + lax.rem(
+            place_y + dy + Y_SIZE, Y_SIZE
+        )
+        target = pl.ds(pl.multiple_of(shard * BLOCK, BLOCK), BLOCK)
+        pieces.append(
+            pltpu.make_async_copy(
+                source.at[pl.ds(first, BLOCK), :],
+                whole_s.at[target, :],
+                piece_sems.at[n],
+            )
+        )
+    for piece in pieces:
+        piece.start()
     place, step = spread(slot_places(owner_ref), (1, ROWS), 1)
     target = place * LEN + step
     slots = lax.broadcasted_iota(jnp.int32, (PACKED, ROWS), 0)
     select = jnp.where(slots == target, 1.0, 0.0).astype(BF16)
     lives, step = spread([live_ref[p] for p in range(PANELS)], (ROWS, 1), 0)
     masked = jnp.where(step < lives, adjoint_ref[...].astype(F32), 0.0).astype(BF16)
-    packed_ref[...] = dot(select, masked).astype(BF16).reshape(packed_ref.shape)
-
-
-def pack_masked(owners, lives, adjoint):
+    for piece in pieces:
+        piece.wait()
+    tall = whole_s[...].astype(F32).reshape(SHARDS, BLOCK, WIDE // 2)
+    out_a = tall[:, :UPS].reshape(HIDDEN, WIDE // 2).astype(BF16)
+    out_b = tall[:, UPS:].reshape(HIDDEN, WIDE // 2).astype(BF16)
+    out_a_ref[...] = out_a
+    out_b_ref[...] = out_b
+    cot = dot_nt(masked[:, : WIDE // 2], out_a) + dot_nt(masked[:, WIDE // 2 :], out_b)
+    cot = dot(select, cot.astype(BF16)).astype(BF16)
+    span = SLOTS * LEN
+    for o in range(OWNERS):
+        columns = slice(o % 2 * HALF, (o % 2 + 1) * HALF)
+        for place_in, owner in enumerate((o, o ^ 1)):
+            packed_ref[o, place_in * span : (place_in + 1) * span, :] = cot[
+                owner * span : (owner + 1) * span, columns
+            ]
+
+
+def cotangent(places, owners, lives, adjoint, pieces):
+    half = jax.ShapeDtypeStruct((HIDDEN, WIDE // 2), BF16)
     return pl.pallas_call(
-        pack_masked_kernel,
-        out_shape=jax.ShapeDtypeStruct((OWNERS, SLOTS * LEN, WIDE), BF16),
-        in_specs=[pl.BlockSpec(memory_space=SMEM)] * 2 + [pl.BlockSpec(memory_space=VMEM)],
-        out_specs=pl.BlockSpec(memory_space=VMEM),
+        cotangent_kernel,
+        out_shape=(jax.ShapeDtypeStruct((OWNERS, 2 * SLOTS * LEN, HALF), BF16), half, half),
+        in_specs=[pl.BlockSpec(memory_space=SMEM)] * 3
+        + [pl.BlockSpec(memory_space=VMEM)]
+        + [pl.BlockSpec(memory_space=pl.ANY)] * len(pieces),
+        out_specs=(pl.BlockSpec(memory_space=VMEM),) * 3,
+        scratch_shapes=[
+            pltpu.VMEM((WIDE, WIDE // 2), BF16),
+            pltpu.SemaphoreType.DMA((SHARDS,)),
+        ],
         compiler_params=pltpu.CompilerParams(vmem_limit_bytes=32 << 20),
         cost_estimate=pl.CostEstimate(
-            flops=2 * PACKED * ROWS * WIDE, bytes_accessed=4 * PACKED * WIDE, transcendentals=0
-        ),
-        name="pack_masked",
-    )(owners, lives, adjoint)
+            flops=2 * ROWS * HIDDEN * (WIDE + PACKED), bytes_accessed=8 << 20, transcendentals=0
+        ),
+        name="cotangent",
+    )(places, owners, lives, adjoint, *pieces)
 
 
 def pad_rows(values, rows=128):
@@ -293,71 +361,40 @@
     low_ref,
     mixed_ref,
     inverse_ref,
+    cot_ref,
     mine_ref,
     other_ref,
-    masked_mine_ref,
-    masked_other_ref,
     whole_ref,
-    out_other_ref,
     keep_ref,
     send_ref,
     up_ref,
     normed_s,
-    masked_s,
-    out_s,
     raise_s,
-    cot_s,
     dquery_s,
     dvalue_s,
     down_s,
     up_s,
     row_sems,
-    masked_sems,
-    out_sems,
     raise_sem,
 ):
     owner = pl.program_id(0)
     core = core_ref[0]
     body = pl.ds(0, WIDE)
     rows = owner_copies((mine_ref.at[:, body], other_ref.at[:, body]), normed_s, row_sems)
-    masks = owner_copies((masked_mine_ref, masked_other_ref), masked_s, masked_sems)
     half = pl.ds(pl.multiple_of(core * (WIDE // 2), WIDE // 2), WIDE // 2)
     raises = pltpu.make_async_copy(
         whole_ref.at[half, pl.ds(QKVL, 2 * RANK)], raise_s, raise_sem
     )
-    outs = owner_copies(
-        (whole_ref.at[half, pl.ds(QKVL + 2 * RANK, QUARTER)], out_other_ref.at[half, :]),
-        out_s,
-        out_sems,
-    )
 
     @pl.when(owner == 0)
     def _():
-        masks[0].start()
-        outs[0].start()
-        outs[1].start()
         rows[0].start()
         raises.start()
-        masks[1].start()
         rows[1].start()
         down_s[...] = jnp.zeros_like(down_s)
         up_s[...] = jnp.zeros_like(up_s)
-        masks[0].wait()
-        outs[0].wait()
-        outs[1].wait()
-
-    @pl.when(owner == 1)
-    def _():
-        masks[1].wait()
-
-    total = jnp.zeros((SHARDS // 2, UPS, PACKED), F32)
-    for n, side in enumerate((core, 1 - core)):
-        for q in range(2):
-            first = pl.multiple_of(side * (WIDE // 2) + q * QUARTER, QUARTER)
-            both = dot_nt(out_s[n], masked_s[owner, :, pl.ds(first, QUARTER)])
-            total = total + both.reshape(SHARDS // 2, BLOCK, PACKED)[:, q * UPS : (q + 1) * UPS]
-    cot_s[...] = total.reshape(HALF, PACKED).astype(BF16).astype(F32)
-
+
+    cot = cot_ref[...].reshape(PACKED, HALF).astype(F32).T
     ones_rows = jnp.where(lax.broadcasted_iota(jnp.int32, (32, PACKED), 0) < 2, 1.0, 0.0)
     sub = lax.broadcasted_iota(jnp.int32, (32, PACKED), 0)
 
@@ -369,7 +406,7 @@
         value = qkv_ref[2 * HALF + h * HEAD : 2 * HALF + (h + 1) * HEAD, :].astype(F32)
         v = jnp.concatenate([value, ones_rows], axis=0)
         unnormed = weights_ref[h]
-        dc = (cot_s[head, :] * inverse_ref[h : h + 1, :]).astype(BF16)
+        dc = (cot[head, :] * inverse_ref[h : h + 1, :]).astype(BF16)
         shift = jnp.sum(dc.astype(F32) * mixed_ref[head, :], axis=0, keepdims=True)
         shift_top = shift.astype(BF16).astype(F32)
         extra = jnp.where(sub == 0, -shift_top, jnp.where(sub == 1, shift_top - shift, 0.0))
@@ -410,7 +447,7 @@
         up_ref[...] = up_s[...]
 
 
-def backward(core, soft, saved, normed, masked, whole, out_other):
+def backward(core, soft, saved, cot, normed, whole):
     anywhere = pl.BlockSpec(memory_space=pl.ANY)
     grid = pltpu.PrefetchScalarGridSpec(
         num_scalar_prefetch=1,
@@ -422,8 +459,9 @@
             pl.BlockSpec((None, PACKED, 2 * RANK), lambda o, c: (o, 0, 0)),
             pl.BlockSpec((None, HALF, PACKED), lambda o, c: (o, 0, 0)),
             pl.BlockSpec((None, 8, PACKED), lambda o, c: (o, 0, 0)),
+            pl.BlockSpec((OWNERS, SLOTS * LEN, HALF), lambda o, c: (0, o, 0)),
         ]
-        + [anywhere] * 6,
+        + [anywhere] * 3,
         out_specs=[
             pl.BlockSpec((SHARDS * UPS, 2 * RANK), lambda o, c: (0, 0)),
             pl.BlockSpec((SHARDS * UPS, 2 * RANK), lambda o, c: (0, 0)),
@@ -431,16 +469,11 @@
         ],
         scratch_shapes=[
             pltpu.VMEM((2, PACKED, WIDE), BF16),
-            pltpu.VMEM((2, PACKED, WIDE), BF16),
-            pltpu.VMEM((2, WIDE // 2, QUARTER), BF16),
             pltpu.VMEM((WIDE // 2, 2 * RANK), BF16),
-            pltpu.VMEM((HALF, PACKED), F32),
             pltpu.VMEM((HALF, PACKED), BF16),
             pltpu.VMEM((HALF, PACKED), BF16),
             pltpu.VMEM((2 * RANK, WIDE), F32),
             pltpu.VMEM((HALF, 2 * RANK), F32),
-            pltpu.SemaphoreType.DMA((2,)),
-            pltpu.SemaphoreType.DMA((2,)),
             pltpu.SemaphoreType.DMA((2,)),
             pltpu.SemaphoreType.DMA,
         ],
@@ -458,7 +491,7 @@
         ),
         cost_estimate=pl.CostEstimate(flops=8 << 30, bytes_accessed=16 << 20, transcendentals=0),
         name="backward",
-    )(core, soft, *saved, *normed, *masked, whole, out_other)
+    )(core, soft, *saved, cot, *normed, whole)
 
 
 def combine_kernel(core_ref, keep_ref, come_ref, up_ref, parts_ref):
@@ -483,9 +516,7 @@
     )(core, keep, come, up)
 
 
-def finish_kernel(core_ref, owner_ref, live_ref, context_ref, x_ref, *refs):
-    *out_refs, block_ref = refs
-    core = core_ref[0]
+def finish_kernel(owner_ref, live_ref, context_ref, x_ref, out_a_ref, out_b_ref, block_ref):
     place, step = spread(slot_places(owner_ref), (ROWS, 1), 0)
     target = place * LEN + step
     slots = lax.broadcasted_iota(jnp.int32, (ROWS, PACKED), 1)
@@ -499,27 +530,25 @@
             first = 0 if source == o else SLOTS * LEN
             parts.append(context_ref[source, first : first + SLOTS * LEN, :])
         halves.append(dot(select, jnp.concatenate(parts, axis=0)).astype(BF16))
-    for n, ref in enumerate(out_refs):
-        side = core if n < 2 else 1 - core
-        first = pl.multiple_of(side * (WIDE // 2) + n % 2 * QUARTER, QUARTER)
-        columns = pl.ds(first, QUARTER)
+    for side, ref in enumerate((out_a_ref, out_b_ref)):
+        columns = slice(side * WIDE // 2, (side + 1) * WIDE // 2)
         attended = dot(halves[0], ref[:HALF, :]) + dot(halves[1], ref[HALF:, :])
         added = jnp.where(step < lives, attended, 0.0)
         block_ref[:, columns] = (x_ref[:, columns].astype(F32) + added).astype(BF16)
 
 
-def finish(core, owners, lives, context, x, outs):
+def finish(owners, lives, context, x, out_a, out_b):
     return pl.pallas_call(
         finish_kernel,
         out_shape=jax.ShapeDtypeStruct((ROWS, WIDE), BF16),
-        in_specs=[pl.BlockSpec(memory_space=SMEM)] * 3 + [pl.BlockSpec(memory_space=VMEM)] * 6,
+        in_specs=[pl.BlockSpec(memory_space=SMEM)] * 2 + [pl.BlockSpec(memory_space=VMEM)] * 4,
         out_specs=pl.BlockSpec(memory_space=VMEM),
         compiler_params=pltpu.CompilerParams(vmem_limit_bytes=40 << 20),
         cost_estimate=pl.CostEstimate(
             flops=2 * ROWS * 2 * HALF * (WIDE + PACKED), bytes_accessed=6 << 20, transcendentals=0
         ),
         name="finish",
-    )(core, owners, lives, context, x, *outs)
+    )(owners, lives, context, x, out_a, out_b)
 
 
 def add_shards_kernel(part_ref, total_ref):
@@ -576,6 +605,31 @@
 def swap_cores(data):
     pairs = [(s, s ^ 1) for s in range(OWNERS)]
     return lax.ppermute(data, "seq", pairs)
+
+
+def shift(data, turn_x, turn_y):
+    pairs = []
+    for x in range(X_SIZE):
+        for y in range(Y_SIZE):
+            to_x, to_y = (x + turn_x) % X_SIZE, (y + turn_y) % Y_SIZE
+            pairs.append((x * Y_SIZE + y, to_x * Y_SIZE + to_y))
+    return lax.ppermute(data, "dp", pairs)
+
+
+def ring_start(shard):
+    return jnp.concatenate([shard] + [shift(shard, -dx, 0) for dx in X_TURNS[1:]], axis=0)
+
+
+def ring_steps(ups, downs, steps):
+    ups, downs = list(ups), list(downs)
+    for _ in range(steps):
+        ups.append(shift(ups[-1], 0, 1))
+        downs.append(shift(downs[-1], 0, -1))
+    return ups, downs
+
+
+def ring_end(ups, downs):
+    return shift(ups[-1][: 2 * BLOCK], 0, 1), shift(downs[-1][2 * BLOCK :], 0, -1)
 
 
 def on_device(
@@ -605,10 +659,9 @@
     ]
     raising = raising_maps.reshape(2 * RANK, UPS).T
     raising = jnp.concatenate([raising, jnp.zeros_like(raising)], axis=0)
-    quarters = [final_projector[:, n * QUARTER : (n + 1) * QUARTER] for n in range(4)]
-    outward = jnp.concatenate([own(quarters[0], quarters[2]), own(quarters[1], quarters[3])], axis=0)
-    shard = jnp.concatenate([*triple, lowered_maps[0], lowered_maps[1], raising, outward], axis=1)
-    whole = lax.all_gather(shard, "dp", axis=0, tiled=True)
+    narrow = jnp.concatenate([*triple, lowered_maps[0], lowered_maps[1], raising], axis=1)
+    whole = lax.all_gather(narrow, "dp", axis=0, tiled=True)
+    outward = jnp.concatenate([final_projector[:, : WIDE // 2], final_projector[:, WIDE // 2 :]], axis=0)
 
     x = encoder_timesteps.reshape(ROWS, WIDE)
     packed = pack(
@@ -618,29 +671,32 @@
         x,
         standardize_scaling.reshape(1, WIDE),
     )
-    packed, adjoint = lax.optimization_barrier((packed, result_adjoint.reshape(ROWS, WIDE)))
-    masked = pack_masked(tile_parent_sequence, tile_valid_timesteps, adjoint)
+    packed, outward = lax.optimization_barrier((packed, outward))
     packed = exchange(packed, "seq")
-    packed, masked = lax.optimization_barrier((packed, masked))
-    masked = exchange(masked, "seq")
+    block = ring_start(outward)
+    ups, downs = ring_steps([block], [block], 3)
+    far_a, far_b = ring_end(ups, downs)
+    packed, far_a, far_b = lax.optimization_barrier((packed, far_a, far_b))
+    pieces = (block, ups[1], downs[1], ups[2], downs[2], ups[3], downs[3], far_a, far_b)
+    dp = lax.axis_index("dp")
+    places = jnp.stack([core, dp // Y_SIZE, dp % Y_SIZE]).astype(jnp.int32)
+    cot, out_a, out_b = cotangent(
+        places,
+        tile_parent_sequence,
+        tile_valid_timesteps,
+        result_adjoint.reshape(ROWS, WIDE),
+        pieces,
+    )
+    cot = exchange(cot, "seq")
     normed = [part.reshape(PACKED, WIDE + FACTS) for part in (packed, swap_cores(packed))]
-    masked = [part.reshape(PACKED, WIDE) for part in (masked, swap_cores(masked))]
-
-    core = core.reshape(1)
-    out_own = whole[:, QKVL + 2 * RANK :]
-    out_other = swap_cores(out_own)
-    context, *saved = forward(core, focus_softness, *normed, whole)
-    out_own, out_later, context = lax.optimization_barrier((out_own, out_other, context))
-    keep, send, up = backward(core, focus_softness, saved, normed, masked, whole, out_other)
+    context, *saved = forward(places, focus_softness, *normed, whole)
+    cot, context = lax.optimization_barrier((cot, context))
+    keep, send, up = backward(places, focus_softness, saved, cot, normed, whole)
     context = exchange(context.reshape(OWNERS, 2 * SLOTS * LEN, HALF), "seq")
-    parts = combine(core, keep, swap_cores(send), up)
-    outs = []
-    for part in (out_own, out_later):
-        part = part.reshape(SHARDS, BLOCK, QUARTER)
-        outs += [part[:, :UPS].reshape(HIDDEN, QUARTER), part[:, UPS:].reshape(HIDDEN, QUARTER)]
+    parts = combine(places, keep, swap_cores(send), up)
     parts, context = lax.optimization_barrier((parts, context))
     parts = exchange(parts.reshape(SHARDS, GRAD, 2 * RANK), "dp")
-    block_out = finish(core, tile_parent_sequence, tile_valid_timesteps, context, x, outs)
+    block_out = finish(tile_parent_sequence, tile_valid_timesteps, context, x, out_a, out_b)
     shard_down, shard_up = add_owners(exchange(add_shards(parts), "seq"))
     return block_out.reshape(encoder_timesteps.shape), shard_down, jnp.swapaxes(shard_up, 1, 2)
 

time: 208 us -> 218 us (1.048)
  starting transfers between devices: 39.7 us -> 75.2 us
  waiting for transfers between devices: 78.3 us -> 44.6 us
  local copies, waits for them, and re-layouts: 12.8 us -> 21.2 us
    ppermute x0 -> x11, starting transfers between devices: none -> 38.8 us  [shift(): return lax.ppermute(data, 'dp', pairs)]
    all_to_all x4, waiting for transfers between devices: 47.1 us -> 16 us  [exchange(): return lax.all_to_all(data, axis, split_axis=0, concat_axis=0, tiled=True)]
    all_gather x1, waiting for transfers between devices: 29.9 us -> 0.02 us  [on_device(): whole = lax.all_gather(narrow, 'dp', axis=0, tiled=True)]
    ppermute x0 -> x11, waiting for transfers between devices: none -> 27.3 us  [shift(): return lax.ppermute(data, 'dp', pairs)]
    unnamed x23 -> x60, local copies, waits for them, and re-layouts: 5.32 us -> 18.9 us
    slice x3, local copies, waits for them, and re-layouts: 5.15 us -> 0.03 us  [the longest x1 0.01 us: ring_end(): downs[-1][2 * BLOCK:]]
    pallas_call x1, Pallas kernels: 13.9 us -> 8.8 us  [backward(): pl.pallas_call(backward_kernel, grid_spec=grid, out_shape=(jax.ShapeDtype...]
    pallas_call x1, Pallas kernels: 2.45 us -> 7.01 us  [cotangent(): pl.pallas_call(cotangent_kernel, out_shape=(jax.ShapeDtypeStruct((OWNERS,...]
  transfers between devices with their start and end apart: 9 -> 18, of which waited for: 5 -> 10; matrix products, arithmetic and copies ran while one was open for 3% -> 0% of each run, Pallas kernels for 19% -> 19%
where the time goes in v4:
time: 218 us; the launch traced here: 217 us
  starting transfers between devices  75.2 us (34%)
  waiting for transfers between devices  44.6 us (20%)
  Pallas kernels  42 us (19%)
  local copies, waits for them, and re-layouts  21.2 us (10%)
  blocking collectives  18.1 us (8%)
  between operations  14.4 us (7%)
    ppermute x11, starting transfers between devices, shift(): return lax.ppermute(data, 'dp', pairs)  38.8 us
    ppermute x11, waiting for transfers between devices, shift(): return lax.ppermute(data, 'dp', pairs)  27.3 us
    all_to_all x4, starting transfers between devices, exchange(): return lax.all_to_all(data, axis, split_axis=0, concat_axis=0, tiled=True)  27.2 us
    unnamed x60, local copies, waits for them, and re-layouts  18.9 us
    pallas_call x1, Pallas kernels, forward(): pl.pallas_call(forward_kernel, grid_spec=grid, out_shape=(jax.ShapeDtypeS...  18.3 us
    all_to_all x1, blocking collectives, exchange(): return lax.all_to_all(data, axis, split_axis=0, concat_axis=0, tiled=True)  18.1 us
    all_to_all x4, waiting for transfers between devices, exchange(): return lax.all_to_all(data, axis, split_axis=0, concat_axis=0, tiled=True)  16 us
    ppermute x2, starting transfers between devices, swap_cores(): return lax.ppermute(data, 'seq', pairs)  9.23 us
  transfers between devices with their start and end apart: 18, of which 10 were waited for; matrix products, arithmetic and copies ran while one was open for 0% of the time, Pallas kernels for 19%

profile of v4, /device:TPU:1, one launch (start us, length us, event | category | flops | bytes accessed | tf_op | source)
XLA Modules:
  0.0 216.6 jit_solution(7570606369650552136)
XLA Ops:
  14.3 2.9 %pack.1 = bf16[16,32,1664]{2,1,0:T(8,128)(2,1)} custom-call(s32[16]{0:T(128)S(1)} %copy-done.17, s32[16]{0:T(128)S(1)} %copy-done.21, s32[16]{0:T(128)S(1)} %copy-done.19, bf16[256,1536]{1,0:T(8,128)(2,1)S(1)} %bitcast.18, f32[1,1536]{1,0:T(1,128)S(1)} %reshape.34.gain_ref), custom_call_target="tpu_custom_call" | custom-call | flops 402653184 | bytes 3145728 | tf_op jit(solution)/shard_map/pack/pallas_call | solution.py:87
  17.2 12.0 %all-to-all-start = ((bf16[16,32,1664]{2,1,0:T(8,128)(2,1)}), bf16[16,32,1664]{2,1,0:T(8,128)(2,1)S(1)}, u32[]{:S(2)}, u32[]{:S(2)}) async-start(bf16[16,32,1664]{2,1,0:T(8,128)(2,1)} %pack.1), calls=%async_computation | async-start | bytes 3407872 | tf_op jit(solution)/shard_map/all_to_all | solution.py:602
  29.2 4.7 %collective-permute-start.2 = (bf16[48,768]{1,0:T(8,128)(2,1)S(1)}, bf16[48,768]{1,0:T(8,128)(2,1)S(1)}, u32[]{:S(2)}, u32[]{:S(2)}) collective-permute-start(bf16[48,768]{1,0:T(8,128)(2,1)S(1)} %pad_maximum_fusion), channel_id=1, source_target_pairs={{0,256},{16,272},{32,288},{48,304},{64,320},{80,336},{96,352},{112... | collective-permute-start | bytes 221192 | tf_op jit(solution)/shard_map/ppermute | solution.py:616
  33.9 2.8 %collective-permute-start.1 = (bf16[48,768]{1,0:T(8,128)(2,1)S(1)}, bf16[48,768]{1,0:T(8,128)(2,1)S(1)}, u32[]{:S(2)}, u32[]{:S(2)}) collective-permute-start(bf16[48,768]{1,0:T(8,128)(2,1)S(1)} %pad_maximum_fusion), channel_id=1, source_target_pairs={{0,384},{16,400},{32,416},{48,432},{64,448},{80,464},{96,480},{112... | collective-permute-start | bytes 221192 | tf_op jit(solution)/shard_map/ppermute | solution.py:616
  39.2 4.1 %collective-permute-done = bf16[48,768]{1,0:T(8,128)(2,1)S(1)} collective-permute-done((bf16[48,768]{1,0:T(8,128)(2,1)S(1)}, bf16[48,768]{1,0:T(8,128)(2,1)S(1)}, u32[]{:S(2)}, u32[]{:S(2)}) %collective-permute-start) | collective-permute-done | bytes 73760 | tf_op jit(solution)/shard_map/ppermute | solution.py:616
  43.3 5.1 %collective-permute-start.7 = (bf16[192,768]{1,0:T(8,128)(2,1)S(1)}, bf16[192,768]{1,0:T(8,128)(2,1)S(1)}, u32[]{:S(2)}, u32[]{:S(2)}) collective-permute-start(bf16[192,768]{1,0:T(8,128)(2,1)S(1)} %constant_dynamic-update-slice_fusion.block_0_ref), channel_id=1, source_target_pairs={{0,112},{16,0},{32,16},{48,32},{64,48},{80,64},{96,80},{112,96},{1... | collective-permute-start | bytes 884744 | tf_op jit(solution)/shard_map/ppermute | solution.py:616
  50.4 4.8 %collective-permute-done.7.block_2_ref = bf16[192,768]{1,0:T(8,128)(2,1)S(1)} collective-permute-done((bf16[192,768]{1,0:T(8,128)(2,1)S(1)}, bf16[192,768]{1,0:T(8,128)(2,1)S(1)}, u32[]{:S(2)}, u32[]{:S(2)}) %collective-permute-start.7) | collective-permute-done | bytes 294944 | tf_op jit(solution)/shard_map/ppermute | solution.py:616
  55.1 5.3 %collective-permute-start.8 = (bf16[192,768]{1,0:T(8,128)(2,1)S(1)}, bf16[192,768]{1,0:T(8,128)(2,1)S(1)}, u32[]{:S(2)}, u32[]{:S(2)}) collective-permute-start(bf16[192,768]{1,0:T(8,128)(2,1)S(1)} %collective-permute-done.7.block_2_ref), channel_id=1, source_target_pairs={{0,112},{16,0},{32,16},{48,32},{64,48},{80,64},{96,80},{112,96},{1... | collective-permute-start | bytes 884744 | tf_op jit(solution)/shard_map/ppermute | solution.py:616
  64.7 5.3 %collective-permute-start.9 = (bf16[192,768]{1,0:T(8,128)(2,1)S(1)}, bf16[192,768]{1,0:T(8,128)(2,1)S(1)}, u32[]{:S(2)}, u32[]{:S(2)}) collective-permute-start(bf16[192,768]{1,0:T(8,128)(2,1)S(1)} %collective-permute-done.8.block_4_ref), channel_id=1, source_target_pairs={{0,112},{16,0},{32,16},{48,32},{64,48},{80,64},{96,80},{112,96},{1... | collective-permute-start | bytes 884744 | tf_op jit(solution)/shard_map/ppermute | solution.py:616
  72.7 3.4 %collective-permute-done.9.block_6_ref = bf16[192,768]{1,0:T(8,128)(2,1)S(1)} collective-permute-done((bf16[192,768]{1,0:T(8,128)(2,1)S(1)}, bf16[192,768]{1,0:T(8,128)(2,1)S(1)}, u32[]{:S(2)}, u32[]{:S(2)}) %collective-permute-start.9) | collective-permute-done | bytes 294944 | tf_op jit(solution)/shard_map/ppermute | solution.py:616
  76.1 5.4 %collective-permute-start.10 = (bf16[96,768]{1,0:T(8,128)(2,1)S(1)}, bf16[96,768]{1,0:T(8,128)(2,1)S(1)}, u32[]{:S(2)}, u32[]{:S(2)}) collective-permute-start(bf16[96,768]{1,0:T(8,128)(2,1)S(1)} %slice.49), channel_id=1, source_target_pairs={{0,112},{16,0},{32,16},{48,32},{64,48},{80,64},{96,80},{112,96},{1... | collective-permute-start | bytes 442376 | tf_op jit(solution)/shard_map/ppermute | solution.py:616
  81.5 6.1 %collective-permute-done.5.block_5_ref = bf16[192,768]{1,0:T(8,128)(2,1)S(1)} collective-permute-done((bf16[192,768]{1,0:T(8,128)(2,1)S(1)}, bf16[192,768]{1,0:T(8,128)(2,1)S(1)}, u32[]{:S(2)}, u32[]{:S(2)}) %collective-permute-start.5) | collective-permute-done | bytes 294944 | tf_op jit(solution)/shard_map/ppermute | solution.py:616
  89.6 8.0 %collective-permute-done.6.far_a_ref = bf16[96,768]{1,0:T(8,128)(2,1)S(1)} collective-permute-done((bf16[96,768]{1,0:T(8,128)(2,1)S(1)}, bf16[96,768]{1,0:T(8,128)(2,1)S(1)}, u32[]{:S(2)}, u32[]{:S(2)}) %collective-permute-start.6) | collective-permute-done | bytes 147488 | tf_op jit(solution)/shard_map/ppermute | solution.py:616
  98.2 7.1 %collective-permute-start.11 = (bf16[16,32,1664]{2,1,0:T(8,128)(2,1)S(1)}, bf16[16,32,1664]{2,1,0:T(8,128)(2,1)}, u32[]{:S(2)}, u32[]{:S(2)}) collective-permute-start(bf16[16,32,1664]{2,1,0:T(8,128)(2,1)S(1)} %all-to-all-done), channel_id=1, source_target_pairs={{0,1},{1,0},{2,3},{3,2},{4,5},{5,4},{6,7},{7,6},{8,9},{9,8},{10,11... | collective-permute-start | bytes 5111816 | tf_op jit(solution)/shard_map/ppermute | solution.py:607
  110.2 7.0 %cotangent.1 = (bf16[16,64,384]{2,1,0:T(8,128)(2,1)}, bf16[768,768]{1,0:T(8,128)(2,1)S(1)}, bf16[768,768]{1,0:T(8,128)(2,1)S(1)}) custom-call(s32[3]{0:T(128)S(1)} %pad_add_fusion.core_ref, s32[16]{0:T(128)S(1)} %copy-done.18, s32[16]{0:T(128)S(1)} %copy-done.20, bf16[256,1536]{1,0:T(8,128)(2,1)S(1)} %bitcast.23, ...), custom_call_target="tpu_custom_call" | custom-call | flops 805306368 | bytes 8388608 | tf_op jit(solution)/shard_map/cotangent/pallas_call | solution.py:170
  119.3 5.8 %all-to-all-start.1 = ((bf16[16,64,384]{2,1,0:T(8,128)(2,1)}), bf16[16,64,384]{2,1,0:T(8,128)(2,1)S(1)}, u32[]{:S(2)}, u32[]{:S(2)}) async-start(bf16[16,64,384]{2,1,0:T(8,128)(2,1)} %get-tuple-element.36), calls=%async_computation.1 | async-start | bytes 1572864 | tf_op jit(solution)/shard_map/all_to_all | solution.py:602
  125.2 18.3 %forward.1 = (bf16[16,2,32,384]{3,2,1,0:T(8,128)(2,1)}, bf16[2,4,512,512]{3,2,1,0:T(8,128)(2,1)}, bf16[2,1152,512]{2,1,0:T(8,128)(2,1)}, bf16[2,512,128]{2,1,0:T...) custom-call(s32[3]{0:T(128)S(1)} %pad_add_fusion.core_ref, f32[8]{0:T(128)S(1)} %copy-done.22, ...), custom_call_target="tpu_custom_call" | custom-call | flops 6442450944 | bytes 16777216 | tf_op jit(solution)/shard_map/forward/pallas_call | solution.py:335
  147.8 4.8 %all-to-all-start.2 = ((bf16[16,64,384]{2,1,0:T(8,128)(2,1)}), bf16[16,64,384]{2,1,0:T(8,128)(2,1)S(1)}, u32[]{:S(2)}, u32[]{:S(2)}) async-start(bf16[16,64,384]{2,1,0:T(8,128)(2,1)} %bitcast.10), calls=%async_computation.2 | async-start | bytes 1572864 | tf_op jit(solution)/shard_map/all_to_all | solution.py:602
  154.9 8.8 %backward.1 = (f32[768,128]{1,0:T(8,128)S(1)}, bf16[768,128]{1,0:T(8,128)(2,1)S(1)}, f32[384,128]{1,0:T(8,128)S(1)}) custom-call(s32[3]{0:T(128)S(1)} %pad_add_fusion.core_ref, f32[8]{0:T(128)S(1)} %copy-done.22, bf16[2,4,512,512]{3,2,1,0:T(8,128)(2,1)} %get-tuple-element.29.weights_ref, bf16[2,1152,512]{2,1,0:T(8,128)(2,1)} %get-tuple-element.30.qkv_ref, ...), custom_call_target="tpu_custom_call" | custom-call | flops 8589934592 | bytes 16777216 | tf_op jit(solution)/shard_map/backward/pallas_call | solution.py:481
  167.8 7.4 %all-to-all-done.2.context_ref = bf16[16,64,384]{2,1,0:T(8,128)(2,1)S(1)} async-done(((bf16[16,64,384]{2,1,0:T(8,128)(2,1)}), bf16[16,64,384]{2,1,0:T(8,128)(2,1)S(1)}, u32[]{:S(2)}, u32[]{:S(2)}) %all-to-all-start.2) | async-done | bytes 786464 | tf_op jit(solution)/shard_map/all_to_all | solution.py:602
  175.2 18.1 %all_to_all.25.part_ref = bf16[32,48,128]{2,1,0:T(8,128)(2,1)S(1)} all-to-all(bf16[32,48,128]{2,1,0:T(8,128)(2,1)S(1)} %bitcast.22), channel_id=1, replica_groups=mesh['dp'=32,'seq'=16] {'dp'}, dimensions={0} | all-to-all | bytes 786432 | tf_op jit(solution)/shard_map/all_to_all | solution.py:602
  194.1 4.6 %all-to-all-start.4 = ((bf16[16,48,128]{2,1,0:T(8,128)(2,1)}), bf16[16,48,128]{2,1,0:T(8,128)(2,1)S(1)}, u32[]{:S(2)}, u32[]{:S(2)}) async-start(bf16[16,48,128]{2,1,0:T(8,128)(2,1)} %add_shards.1), calls=%async_computation.4 | async-start | bytes 393216 | tf_op jit(solution)/shard_map/all_to_all | solution.py:602
  200.0 2.9 %finish.1 = bf16[256,1536]{1,0:T(8,128)(2,1)} custom-call(s32[16]{0:T(128)S(1)} %copy-done.18, s32[16]{0:T(128)S(1)} %copy-done.20, bf16[16,64,384]{2,1,0:T(8,128)(2,1)S(1)} %all-to-all-done.2.context_ref, bf16[256,1536]{1,0:T(8,128)(2,1)S(1)} %bitcast.19, bf16[768,768]{1,0:T(8,128)(2,1)S(1)} %copy-done.3, bf16[768,768]{1,0:T(8,128)(2,1)S(1)} %copy-done.5), custom_call_target="tpu_custom_call" | custom-call | flops 805306368 | bytes 6291456 | tf_op jit(solution)/shard_map/finish/pallas_call | solution.py:541
  202.9 6.1 %all-to-all-done.4.part_ref = bf16[16,48,128]{2,1,0:T(8,128)(2,1)S(1)} async-done(((bf16[16,48,128]{2,1,0:T(8,128)(2,1)}), bf16[16,48,128]{2,1,0:T(8,128)(2,1)S(1)}, u32[]{:S(2)}, u32[]{:S(2)}) %all-to-all-start.4) | async-done | bytes 196640 | tf_op jit(solution)/shard_map/all_to_all | solution.py:602
  (94 shorter events, 41.3 us)
Async XLA Ops:
  7.2 118.0 %all-gather.2.cloned.1.call-start = ((), (), s32[]{:S(2)}) async-start(), calls=%async_computation.5 | async-start | bytes 4460544 | tf_op jit(solution)/shard_map/all_gather | solution.py:663
  17.2 88.2 %copy-start.6 = (bf16[16,16,1536]{2,1,0:T(8,128)(2,1)S(1)}, bf16[16,16,1536]{2,1,0:T(8,128)(2,1)}, u32[]{:S(2)}) copy-start(bf16[16,16,1536]{2,1,0:T(8,128)(2,1)} %param.21) | copy-start | bytes 2359300
  17.2 88.2 %copy-start.18 = (s32[16]{0:T(128)S(1)}, s32[16]{0:T(128)}, u32[]{:S(2)}) copy-start(s32[16]{0:T(128)} %owner_ref.5) | copy-start | bytes 196
  17.2 88.2 %copy-start.20 = (s32[16]{0:T(128)S(1)}, s32[16]{0:T(128)}, u32[]{:S(2)}) copy-start(s32[16]{0:T(128)} %live_ref.5) | copy-start | bytes 196
  17.2 81.0 %all-to-all-start = ((bf16[16,32,1664]{2,1,0:T(8,128)(2,1)}), bf16[16,32,1664]{2,1,0:T(8,128)(2,1)S(1)}, u32[]{:S(2)}, u32[]{:S(2)}) async-start(bf16[16,32,1664]{2,1,0:T(8,128)(2,1)} %pack.1), calls=%async_computation | async-start | bytes 3407872 | tf_op jit(solution)/shard_map/all_to_all | solution.py:602
  29.2 14.1 %collective-permute-start.2 = (bf16[48,768]{1,0:T(8,128)(2,1)S(1)}, bf16[48,768]{1,0:T(8,128)(2,1)S(1)}, u32[]{:S(2)}, u32[]{:S(2)}) collective-permute-start(bf16[48,768]{1,0:T(8,128)(2,1)S(1)} %pad_maximum_fusion), channel_id=1, source_target_pairs={{0,256},{16,272},{32,288},{48,304},{64,320},{80,336},{96,352},{112... | collective-permute-start | bytes 221192 | tf_op jit(solution)/shard_map/ppermute | solution.py:616
  33.9 9.4 %collective-permute-start.1 = (bf16[48,768]{1,0:T(8,128)(2,1)S(1)}, bf16[48,768]{1,0:T(8,128)(2,1)S(1)}, u32[]{:S(2)}, u32[]{:S(2)}) collective-permute-start(bf16[48,768]{1,0:T(8,128)(2,1)S(1)} %pad_maximum_fusion), channel_id=1, source_target_pairs={{0,384},{16,400},{32,416},{48,432},{64,448},{80,464},{96,480},{112... | collective-permute-start | bytes 221192 | tf_op jit(solution)/shard_map/ppermute | solution.py:616
  36.7 6.6 %collective-permute-start = (bf16[48,768]{1,0:T(8,128)(2,1)S(1)}, bf16[48,768]{1,0:T(8,128)(2,1)S(1)}, u32[]{:S(2)}, u32[]{:S(2)}) collective-permute-start(bf16[48,768]{1,0:T(8,128)(2,1)S(1)} %pad_maximum_fusion), channel_id=1, source_target_pairs={{0,128},{16,144},{32,160},{48,176},{64,192},{80,208},{96,224},{112... | collective-permute-start | bytes 221192 | tf_op jit(solution)/shard_map/ppermute | solution.py:616
  43.3 11.8 %collective-permute-start.7 = (bf16[192,768]{1,0:T(8,128)(2,1)S(1)}, bf16[192,768]{1,0:T(8,128)(2,1)S(1)}, u32[]{:S(2)}, u32[]{:S(2)}) collective-permute-start(bf16[192,768]{1,0:T(8,128)(2,1)S(1)} %constant_dynamic-update-slice_fusion.block_0_ref), channel_id=1, source_target_pairs={{0,112},{16,0},{32,16},{48,32},{64,48},{80,64},{96,80},{112,96},{1... | collective-permute-start | bytes 884744 | tf_op jit(solution)/shard_map/ppermute | solution.py:616
  48.4 12.8 %collective-permute-start.3 = (bf16[192,768]{1,0:T(8,128)(2,1)S(1)}, bf16[192,768]{1,0:T(8,128)(2,1)S(1)}, u32[]{:S(2)}, u32[]{:S(2)}) collective-permute-start(bf16[192,768]{1,0:T(8,128)(2,1)S(1)} %constant_dynamic-update-slice_fusion.block_0_ref), channel_id=1, source_target_pairs={{0,16},{16,32},{32,48},{48,64},{64,80},{80,96},{96,112},{112,0},{1... | collective-permute-start | bytes 884744 | tf_op jit(solution)/shard_map/ppermute | solution.py:616
  55.1 9.6 %collective-permute-start.8 = (bf16[192,768]{1,0:T(8,128)(2,1)S(1)}, bf16[192,768]{1,0:T(8,128)(2,1)S(1)}, u32[]{:S(2)}, u32[]{:S(2)}) collective-permute-start(bf16[192,768]{1,0:T(8,128)(2,1)S(1)} %collective-permute-done.7.block_2_ref), channel_id=1, source_target_pairs={{0,112},{16,0},{32,16},{48,32},{64,48},{80,64},{96,80},{112,96},{1... | collective-permute-start | bytes 884744 | tf_op jit(solution)/shard_map/ppermute | solution.py:616
  61.2 9.5 %collective-permute-start.4 = (bf16[192,768]{1,0:T(8,128)(2,1)S(1)}, bf16[192,768]{1,0:T(8,128)(2,1)S(1)}, u32[]{:S(2)}, u32[]{:S(2)}) collective-permute-start(bf16[192,768]{1,0:T(8,128)(2,1)S(1)} %collective-permute-done.3.block_1_ref), channel_id=1, source_target_pairs={{0,16},{16,32},{32,48},{48,64},{64,80},{80,96},{96,112},{112,0},{1... | collective-permute-start | bytes 884744 | tf_op jit(solution)/shard_map/ppermute | solution.py:616
  64.7 11.4 %collective-permute-start.9 = (bf16[192,768]{1,0:T(8,128)(2,1)S(1)}, bf16[192,768]{1,0:T(8,128)(2,1)S(1)}, u32[]{:S(2)}, u32[]{:S(2)}) collective-permute-start(bf16[192,768]{1,0:T(8,128)(2,1)S(1)} %collective-permute-done.8.block_4_ref), channel_id=1, source_target_pairs={{0,112},{16,0},{32,16},{48,32},{64,48},{80,64},{96,80},{112,96},{1... | collective-permute-start | bytes 884744 | tf_op jit(solution)/shard_map/ppermute | solution.py:616
  70.7 18.8 %copy-start.13 = (bf16[192,768]{1,0:T(8,128)(2,1)}, bf16[192,768]{1,0:T(8,128)(2,1)S(1)}, u32[]{:S(2)}) copy-start(bf16[192,768]{1,0:T(8,128)(2,1)S(1)} %collective-permute-done.4.block_3_ref) | copy-start | bytes 884740
  70.7 16.9 %collective-permute-start.5 = (bf16[192,768]{1,0:T(8,128)(2,1)S(1)}, bf16[192,768]{1,0:T(8,128)(2,1)S(1)}, u32[]{:S(2)}, u32[]{:S(2)}) collective-permute-start(bf16[192,768]{1,0:T(8,128)(2,1)S(1)} %collective-permute-done.4.block_3_ref), channel_id=1, source_target_pairs={{0,16},{16,32},{32,48},{48,64},{64,80},{80,96},{96,112},{112,0},{1... | collective-permute-start | bytes 884744 | tf_op jit(solution)/shard_map/ppermute | solution.py:616
  76.1 13.5 %collective-permute-start.10 = (bf16[96,768]{1,0:T(8,128)(2,1)S(1)}, bf16[96,768]{1,0:T(8,128)(2,1)S(1)}, u32[]{:S(2)}, u32[]{:S(2)}) collective-permute-start(bf16[96,768]{1,0:T(8,128)(2,1)S(1)} %slice.49), channel_id=1, source_target_pairs={{0,112},{16,0},{32,16},{48,32},{64,48},{80,64},{96,80},{112,96},{1... | collective-permute-start | bytes 442376 | tf_op jit(solution)/shard_map/ppermute | solution.py:616
  87.6 9.9 %collective-permute-start.6 = (bf16[96,768]{1,0:T(8,128)(2,1)S(1)}, bf16[96,768]{1,0:T(8,128)(2,1)S(1)}, u32[]{:S(2)}, u32[]{:S(2)}) collective-permute-start(bf16[96,768]{1,0:T(8,128)(2,1)S(1)} %slice.48), channel_id=1, source_target_pairs={{0,16},{16,32},{32,48},{48,64},{64,80},{80,96},{96,112},{112,0},{1... | collective-permute-start | bytes 442376 | tf_op jit(solution)/shard_map/ppermute | solution.py:616
  98.2 26.9 %collective-permute-start.11 = (bf16[16,32,1664]{2,1,0:T(8,128)(2,1)S(1)}, bf16[16,32,1664]{2,1,0:T(8,128)(2,1)}, u32[]{:S(2)}, u32[]{:S(2)}) collective-permute-start(bf16[16,32,1664]{2,1,0:T(8,128)(2,1)S(1)} %all-to-all-done), channel_id=1, source_target_pairs={{0,1},{1,0},{2,3},{3,2},{4,5},{5,4},{6,7},{7,6},{8,9},{9,8},{10,11... | collective-permute-start | bytes 5111816 | tf_op jit(solution)/shard_map/ppermute | solution.py:607
  119.3 28.5 %all-to-all-start.1 = ((bf16[16,64,384]{2,1,0:T(8,128)(2,1)}), bf16[16,64,384]{2,1,0:T(8,128)(2,1)S(1)}, u32[]{:S(2)}, u32[]{:S(2)}) async-start(bf16[16,64,384]{2,1,0:T(8,128)(2,1)} %get-tuple-element.36), calls=%async_computation.1 | async-start | bytes 1572864 | tf_op jit(solution)/shard_map/all_to_all | solution.py:602
  147.8 27.4 %all-to-all-start.2 = ((bf16[16,64,384]{2,1,0:T(8,128)(2,1)}), bf16[16,64,384]{2,1,0:T(8,128)(2,1)S(1)}, u32[]{:S(2)}, u32[]{:S(2)}) async-start(bf16[16,64,384]{2,1,0:T(8,128)(2,1)} %bitcast.10), calls=%async_computation.2 | async-start | bytes 1572864 | tf_op jit(solution)/shard_map/all_to_all | solution.py:602
  163.7 35.0 %copy-start.1 = (bf16[16,16,1536]{2,1,0:T(8,128)(2,1)S(1)}, bf16[16,16,1536]{2,1,0:T(8,128)(2,1)}, u32[]{:S(2)}) copy-start(bf16[16,16,1536]{2,1,0:T(8,128)(2,1)} %param.11) | copy-start | bytes 2359300
  163.7 35.0 %copy-start.3 = (bf16[768,768]{1,0:T(8,128)(2,1)S(1)}, bf16[768,768]{1,0:T(8,128)(2,1)}, u32[]{:S(2)}) copy-start(bf16[768,768]{1,0:T(8,128)(2,1)} %copy-done.2) | copy-start | bytes 3538948
  163.7 3.5 %collective-permute-start.12 = (bf16[768,128]{1,0:T(8,128)(2,1)S(1)}, bf16[768,128]{1,0:T(8,128)(2,1)S(1)}, u32[]{:S(2)}, u32[]{:S(2)}) collective-permute-start(bf16[768,128]{1,0:T(8,128)(2,1)S(1)} %get-tuple-element.40), channel_id=1, source_target_pairs={{0,1},{1,0},{2,3},{3,2},{4,5},{5,4},{6,7},{7,6},{8,9},{9,8},{10,11... | collective-permute-start | bytes 589832 | tf_op jit(solution)/shard_map/ppermute | solution.py:607
  194.1 14.9 %all-to-all-start.4 = ((bf16[16,48,128]{2,1,0:T(8,128)(2,1)}), bf16[16,48,128]{2,1,0:T(8,128)(2,1)S(1)}, u32[]{:S(2)}, u32[]{:S(2)}) async-start(bf16[16,48,128]{2,1,0:T(8,128)(2,1)} %add_shards.1), calls=%async_computation.4 | async-start | bytes 393216 | tf_op jit(solution)/shard_map/all_to_all | solution.py:602
  (22 other events, 43.1 us)
Sparse Core Ops, SparseCore 0:
  11.2 94.4 all-gather.1

commit v5 on v3

--- a/solution.py
+++ b/solution.py
@@ -94,6 +94,33 @@
     )(owners, tags, lives, x, gain)
 
 
+def shard_kernel(core_ref, triple_ref, lowered_ref, raising_ref, final_ref, shard_ref):
+    core = core_ref[0]
+    for n in range(3):
+        first = pl.multiple_of(n * HIDDEN + core * HALF, HALF)
+        shard_ref[:, n * HALF : (n + 1) * HALF] = triple_ref[:, pl.ds(first, HALF)]
+    lowered = [lowered_ref[n].astype(F32) for n in range(2)]
+    shard_ref[:, 3 * HALF : QKVL] = jnp.concatenate(lowered, axis=1).astype(BF16)
+    raising = jnp.concatenate([raising_ref[n].astype(F32) for n in range(2)], axis=1)
+    shard_ref[:, QKVL : QKVL + 2 * RANK] = pad_rows(raising, BLOCK).astype(BF16)
+    quarters = []
+    for q in range(2):
+        first = pl.multiple_of(core * (WIDE // 2) + q * QUARTER, QUARTER)
+        quarters.append(final_ref[:, pl.ds(first, QUARTER)].astype(F32))
+    shard_ref[:, QKVL + 2 * RANK :] = jnp.concatenate(quarters, axis=0).astype(BF16)
+
+
+def make_shard(core, triple, lowered, raising, final):
+    return pl.pallas_call(
+        shard_kernel,
+        out_shape=jax.ShapeDtypeStruct((BLOCK, QKVL + 2 * RANK + QUARTER), BF16),
+        in_specs=[pl.BlockSpec(memory_space=SMEM)] + [pl.BlockSpec(memory_space=VMEM)] * 4,
+        out_specs=pl.BlockSpec(memory_space=VMEM),
+        compiler_params=pltpu.CompilerParams(vmem_limit_bytes=60 << 20),
+        name="make_shard",
+    )(core, triple, lowered, raising, final)
+
+
 def pack_masked_kernel(owner_ref, live_ref, adjoint_ref, packed_ref):
     place, step = spread(slot_places(owner_ref), (1, ROWS), 1)
     target = place * LEN + step
@@ -147,6 +174,7 @@
     other_ref,
     whole_ref,
     context_ref,
+    out_ref,
     weights_ref,
     qkv_ref,
     low_ref,
@@ -159,10 +187,14 @@
     row_sems,
     weight_sems,
     raise_sem,
+    out_sem,
 ):
     owner = pl.program_id(0)
     core = core_ref[0]
     rows = owner_copies((mine_ref, other_ref), normed_s, row_sems)
+    outs = pltpu.make_async_copy(
+        whole_ref.at[:, pl.ds(QKVL + 2 * RANK, QUARTER)], out_ref, out_sem
+    )
     tiles = [
         pltpu.make_async_copy(
             whole_ref.at[:, pl.ds(n * 256, 256)],
@@ -183,11 +215,13 @@
             tile.start()
         raises.start()
         rows[1].start()
+        outs.start()
         rows[0].wait()
 
     @pl.when(owner == 1)
     def _():
         rows[1].wait()
+        outs.wait()
 
     for n, tile in enumerate(tiles):
 
@@ -248,6 +282,7 @@
         + [anywhere] * 3,
         out_specs=[
             pl.BlockSpec((OWNERS, None, SLOTS * LEN, HALF), lambda o, c: (0, o, 0, 0)),
+            anywhere,
             pl.BlockSpec((None, FOCI, PACKED, PACKED), lambda o, c: (o, 0, 0, 0)),
             pl.BlockSpec((None, 3 * HALF, PACKED), lambda o, c: (o, 0, 0)),
             pl.BlockSpec((None, PACKED, 2 * RANK), lambda o, c: (o, 0, 0)),
@@ -262,6 +297,7 @@
             pltpu.SemaphoreType.DMA((2,)),
             pltpu.SemaphoreType.DMA((QKVL // 256,)),
             pltpu.SemaphoreType.DMA,
+            pltpu.SemaphoreType.DMA,
         ],
     )
     return pl.pallas_call(
@@ -269,6 +305,7 @@
         grid_spec=grid,
         out_shape=(
             jax.ShapeDtypeStruct((OWNERS, 2, SLOTS * LEN, HALF), BF16),
+            jax.ShapeDtypeStruct((WIDE, QUARTER), BF16),
             jax.ShapeDtypeStruct((2, FOCI, PACKED, PACKED), BF16),
             jax.ShapeDtypeStruct((2, 3 * HALF, PACKED), BF16),
             jax.ShapeDtypeStruct((2, PACKED, 2 * RANK), BF16),
@@ -276,7 +313,7 @@
             jax.ShapeDtypeStruct((2, 8, PACKED), F32),
         ),
         compiler_params=pltpu.CompilerParams(
-            vmem_limit_bytes=48 << 20, dimension_semantics=("arbitrary",)
+            vmem_limit_bytes=36 << 20, dimension_semantics=("arbitrary",)
         ),
         cost_estimate=pl.CostEstimate(
             flops=6 << 30, bytes_accessed=16 << 20, transcendentals=2 * FOCI * PACKED * PACKED
@@ -298,6 +335,7 @@
     masked_mine_ref,
     masked_other_ref,
     whole_ref,
+    out_own_ref,
     out_other_ref,
     keep_ref,
     send_ref,
@@ -305,6 +343,7 @@
     normed_s,
     masked_s,
     out_s,
+    tight_s,
     raise_s,
     cot_s,
     dquery_s,
@@ -326,7 +365,7 @@
         whole_ref.at[half, pl.ds(QKVL, 2 * RANK)], raise_s, raise_sem
     )
     outs = owner_copies(
-        (whole_ref.at[half, pl.ds(QKVL + 2 * RANK, QUARTER)], out_other_ref.at[half, :]),
+        (out_own_ref.at[half, :], out_other_ref.at[half, :]),
         out_s,
         out_sems,
     )
@@ -343,20 +382,22 @@
         down_s[...] = jnp.zeros_like(down_s)
         up_s[...] = jnp.zeros_like(up_s)
         masks[0].wait()
-        outs[0].wait()
-        outs[1].wait()
+        for n, out in enumerate(outs):
+            out.wait()
+            tall = out_s[n].astype(F32).reshape(SHARDS // 2, BLOCK, QUARTER)
+            for q in range(2):
+                tight = tall[:, q * UPS : (q + 1) * UPS].reshape(HALF, QUARTER)
+                tight_s[n, :, q * QUARTER : (q + 1) * QUARTER] = tight.astype(BF16)
 
     @pl.when(owner == 1)
     def _():
         masks[1].wait()
 
-    total = jnp.zeros((SHARDS // 2, UPS, PACKED), F32)
+    total = jnp.zeros((HALF, PACKED), F32)
     for n, side in enumerate((core, 1 - core)):
-        for q in range(2):
-            first = pl.multiple_of(side * (WIDE // 2) + q * QUARTER, QUARTER)
-            both = dot_nt(out_s[n], masked_s[owner, :, pl.ds(first, QUARTER)])
-            total = total + both.reshape(SHARDS // 2, BLOCK, PACKED)[:, q * UPS : (q + 1) * UPS]
-    cot_s[...] = total.reshape(HALF, PACKED).astype(BF16).astype(F32)
+        columns = pl.ds(pl.multiple_of(side * (WIDE // 2), WIDE // 2), WIDE // 2)
+        total = total + dot_nt(tight_s[n], masked_s[owner, :, columns])
+    cot_s[...] = total.astype(BF16).astype(F32)
 
     ones_rows = jnp.where(lax.broadcasted_iota(jnp.int32, (32, PACKED), 0) < 2, 1.0, 0.0)
     sub = lax.broadcasted_iota(jnp.int32, (32, PACKED), 0)
@@ -410,7 +451,7 @@
         up_ref[...] = up_s[...]
 
 
-def backward(core, soft, saved, normed, masked, whole, out_other):
+def backward(core, soft, saved, normed, masked, whole, out_own, out_other):
     anywhere = pl.BlockSpec(memory_space=pl.ANY)
     grid = pltpu.PrefetchScalarGridSpec(
         num_scalar_prefetch=1,
@@ -423,7 +464,7 @@
             pl.BlockSpec((None, HALF, PACKED), lambda o, c: (o, 0, 0)),
             pl.BlockSpec((None, 8, PACKED), lambda o, c: (o, 0, 0)),
         ]
-        + [anywhere] * 6,
+        + [anywhere] * 7,
         out_specs=[
             pl.BlockSpec((SHARDS * UPS, 2 * RANK), lambda o, c: (0, 0)),
             pl.BlockSpec((SHARDS * UPS, 2 * RANK), lambda o, c: (0, 0)),
@@ -433,6 +474,7 @@
             pltpu.VMEM((2, PACKED, WIDE), BF16),
             pltpu.VMEM((2, PACKED, WIDE), BF16),
             pltpu.VMEM((2, WIDE // 2, QUARTER), BF16),
+            pltpu.VMEM((2, HALF, WIDE // 2), BF16),
             pltpu.VMEM((WIDE // 2, 2 * RANK), BF16),
             pltpu.VMEM((HALF, PACKED), F32),
             pltpu.VMEM((HALF, PACKED), BF16),
@@ -454,11 +496,11 @@
             jax.ShapeDtypeStruct((HALF, 2 * RANK), F32),
         ),
         compiler_params=pltpu.CompilerParams(
-            vmem_limit_bytes=48 << 20, dimension_semantics=("arbitrary",)
+            vmem_limit_bytes=36 << 20, dimension_semantics=("arbitrary",)
         ),
         cost_estimate=pl.CostEstimate(flops=8 << 30, bytes_accessed=16 << 20, transcendentals=0),
         name="backward",
-    )(core, soft, *saved, *normed, *masked, whole, out_other)
+    )(core, soft, *saved, *normed, *masked, whole, out_own, out_other)
 
 
 def combine_kernel(core_ref, keep_ref, come_ref, up_ref, parts_ref):
@@ -591,23 +633,10 @@
     focus_softness,
     result_adjoint,
 ):
-    core = lax.axis_index("seq") % 2
-    def own(left, right):
-        return jnp.where(core == 0, left, right)
-
-    starts = [n * 2 * HALF for n in range(3)]
-    triple = [
-        own(
-            triple_projector[:, first : first + HALF],
-            triple_projector[:, first + HALF : first + 2 * HALF],
-        )
-        for first in starts
-    ]
-    raising = raising_maps.reshape(2 * RANK, UPS).T
-    raising = jnp.concatenate([raising, jnp.zeros_like(raising)], axis=0)
-    quarters = [final_projector[:, n * QUARTER : (n + 1) * QUARTER] for n in range(4)]
-    outward = jnp.concatenate([own(quarters[0], quarters[2]), own(quarters[1], quarters[3])], axis=0)
-    shard = jnp.concatenate([*triple, lowered_maps[0], lowered_maps[1], raising, outward], axis=1)
+    core = (lax.axis_index("seq") % 2).astype(jnp.int32).reshape(1)
+    shard = make_shard(
+        core, triple_projector, lowered_maps, jnp.swapaxes(raising_maps, 1, 2), final_projector
+    )
     whole = lax.all_gather(shard, "dp", axis=0, tiled=True)
 
     x = encoder_timesteps.reshape(ROWS, WIDE)
@@ -624,18 +653,15 @@
     packed, masked = lax.optimization_barrier((packed, masked))
     masked = exchange(masked, "seq")
     normed = [part.reshape(PACKED, WIDE + FACTS) for part in (packed, swap_cores(packed))]
+    context, out_own, *saved = forward(core, focus_softness, *normed, whole)
+    masked, context = lax.optimization_barrier((masked, context))
     masked = [part.reshape(PACKED, WIDE) for part in (masked, swap_cores(masked))]
-
-    core = core.reshape(1)
-    out_own = whole[:, QKVL + 2 * RANK :]
     out_other = swap_cores(out_own)
-    context, *saved = forward(core, focus_softness, *normed, whole)
-    out_own, out_later, context = lax.optimization_barrier((out_own, out_other, context))
-    keep, send, up = backward(core, focus_softness, saved, normed, masked, whole, out_other)
+    keep, send, up = backward(core, focus_softness, saved, normed, masked, whole, out_own, out_other)
     context = exchange(context.reshape(OWNERS, 2 * SLOTS * LEN, HALF), "seq")
     parts = combine(core, keep, swap_cores(send), up)
     outs = []
-    for part in (out_own, out_later):
+    for part in (out_own, out_other):
         part = part.reshape(SHARDS, BLOCK, QUARTER)
         outs += [part[:, :UPS].reshape(HIDDEN, QUARTER), part[:, UPS:].reshape(HIDDEN, QUARTER)]
     parts, context = lax.optimization_barrier((parts, context))

time: 208 us -> 213 us (1.024)
  local copies, waits for them, and re-layouts: 12.8 us -> 21.7 us
  Pallas kernels: 41.5 us -> 37.9 us
    unnamed x23 -> x42, local copies, waits for them, and re-layouts: 5.32 us -> 19.4 us
    pallas_call x1, Pallas kernels: 13.9 us -> 9.76 us  [backward(): pl.pallas_call(backward_kernel, grid_spec=grid, out_shape=(jax.ShapeDtype...]
    ppermute x4, waiting for transfers between devices: 1.31 us -> 4.75 us  [swap_cores(): return lax.ppermute(data, 'seq', pairs)]
    all_gather x1, waiting for transfers between devices: 29.9 us -> 26.5 us  [on_device(): whole = lax.all_gather(shard, 'dp', axis=0, tiled=True)]
    slice x1 -> x0, local copies, waits for them, and re-layouts: 2.41 us -> none  [on_device(): out_own = whole[:, QKVL + 2 * RANK:]]
  transfers between devices with their start and end apart: 9 -> 9, of which waited for: 5 -> 6; matrix products, arithmetic and copies ran while one was open for 3% -> 1% of each run, Pallas kernels for 19% -> 16%
where the time goes in v5:
time: 213 us; the launch traced here: 212 us
  waiting for transfers between devices  77 us (36%)
  starting transfers between devices  41.7 us (20%)
  Pallas kernels  37.9 us (18%)
  local copies, waits for them, and re-layouts  21.7 us (10%)
  blocking collectives  19 us (9%)
  between operations  14.2 us (7%)
    all_to_all x4, waiting for transfers between devices, exchange(): return lax.all_to_all(data, axis, split_axis=0, concat_axis=0, tiled=True)  45.7 us
    all_to_all x4, starting transfers between devices, exchange(): return lax.all_to_all(data, axis, split_axis=0, concat_axis=0, tiled=True)  30.9 us
    all_gather x1, waiting for transfers between devices, on_device(): whole = lax.all_gather(shard, 'dp', axis=0, tiled=True)  26.5 us
    unnamed x42, local copies, waits for them, and re-layouts  19.4 us
    all_to_all x1, blocking collectives, exchange(): return lax.all_to_all(data, axis, split_axis=0, concat_axis=0, tiled=True)  19 us
    pallas_call x1, Pallas kernels, forward(): pl.pallas_call(forward_kernel, grid_spec=grid, out_shape=(jax.ShapeDtypeS...  16.6 us
    ppermute x4, starting transfers between devices, swap_cores(): return lax.ppermute(data, 'seq', pairs)  10.7 us
    pallas_call x1, Pallas kernels, backward(): pl.pallas_call(backward_kernel, grid_spec=grid, out_shape=(jax.ShapeDtype...  9.76 us
  transfers between devices with their start and end apart: 9, of which 6 were waited for; matrix products, arithmetic and copies ran while one was open for 1% of the time, Pallas kernels for 16%

profile of v5, /device:TPU:1, one launch (start us, length us, event | category | flops | bytes accessed | tf_op | source)
XLA Modules:
  0.0 211.5 jit_solution(14024640350827601940)
XLA Ops:
  7.2 1.8 make_shard.1
  12.8 2.9 %pack.1 = bf16[16,32,1664]{2,1,0:T(8,128)(2,1)} custom-call(s32[16]{0:T(128)S(1)} %copy-done.6, s32[16]{0:T(128)S(1)} %copy-done.10, s32[16]{0:T(128)S(1)} %copy-done.8, bf16[256,1536]{1,0:T(8,128)(2,1)S(1)} %bitcast.18, f32[1,1536]{1,0:T(1,128)S(1)} %reshape.59.gain_ref), custom_call_target="tpu_custom_call" | custom-call | flops 402653184 | bytes 3145728 | tf_op jit(solution)/shard_map/pack/pallas_call | solution.py:84
  15.7 12.0 %all-to-all-start = ((bf16[16,32,1664]{2,1,0:T(8,128)(2,1)}), bf16[16,32,1664]{2,1,0:T(8,128)(2,1)S(1)}, u32[]{:S(2)}, u32[]{:S(2)}) async-start(bf16[16,32,1664]{2,1,0:T(8,128)(2,1)} %pack.1), calls=%async_computation | async-start | bytes 3407872 | tf_op jit(solution)/shard_map/all_to_all | solution.py:615
  27.7 2.4 %pack_masked.1 = bf16[16,32,1536]{2,1,0:T(8,128)(2,1)} custom-call(s32[16]{0:T(128)S(1)} %copy-done.7, s32[16]{0:T(128)S(1)} %copy-done.9, bf16[256,1536]{1,0:T(8,128)(2,1)S(1)} %bitcast.28), custom_call_target="tpu_custom_call" | custom-call | flops 402653184 | bytes 3145728 | tf_op jit(solution)/shard_map/pack_masked/pallas_call | solution.py:135
  30.1 38.7 %all-to-all-done = bf16[16,32,1664]{2,1,0:T(8,128)(2,1)S(1)} async-done(((bf16[16,32,1664]{2,1,0:T(8,128)(2,1)}), bf16[16,32,1664]{2,1,0:T(8,128)(2,1)S(1)}, u32[]{:S(2)}, u32[]{:S(2)}) %all-to-all-start) | async-done | bytes 1703968 | tf_op jit(solution)/shard_map/all_to_all | solution.py:615
  68.7 4.4 %all-to-all-start.1 = ((bf16[16,32,1536]{2,1,0:T(8,128)(2,1)}), bf16[16,32,1536]{2,1,0:T(8,128)(2,1)}, u32[]{:S(2)}, u32[]{:S(2)}) async-start(bf16[16,32,1536]{2,1,0:T(8,128)(2,1)} %pack_masked.1), calls=%async_computation.1 | async-start | bytes 3145728 | tf_op jit(solution)/shard_map/all_to_all | solution.py:615
  73.2 2.1 collective-permute-start
  75.2 3.4 %collective-permute-done = bf16[16,32,1664]{2,1,0:T(8,128)(2,1)S(1)} collective-permute-done((bf16[16,32,1664]{2,1,0:T(8,128)(2,1)S(1)}, bf16[16,32,1664]{2,1,0:T(8,128)(2,1)S(1)}, u32[]{:S(2)}, u32[]{:S(2)}) %collective-permute-start) | collective-permute-done | bytes 1703968 | tf_op jit(solution)/shard_map/ppermute | solution.py:620
  79.9 26.5 %all-gather.2.cloned.1.call-done.whole_ref = bf16[1536,1792]{1,0:T(8,128)(2,1)} async-done(((bf16[48,1792]{1,0:T(8,128)(2,1)}), bf16[1536,1792]{1,0:T(8,128)(2,1)}) %all-gather.2.cloned.1.call-update) | async-done | bytes 5505040 | tf_op jit(solution)/shard_map/all_gather | solution.py:640
  106.4 1.5 copy-done.12
  107.9 16.6 %forward.1 = (bf16[16,2,32,384]{3,2,1,0:T(8,128)(2,1)}, bf16[1536,384]{1,0:T(8,128)(2,1)S(1)}, bf16[2,4,512,512]{3,2,1,0:T(8,128)(2,1)S(1)}, bf16[2,1152,512]{2,...) custom-call(s32[1]{0:T(128)} %bitcast.core_ref, ...), custom_call_target="tpu_custom_call" | custom-call | flops 6442450944 | bytes 16777216 | tf_op jit(solution)/shard_map/forward/pallas_call | solution.py:303
  125.5 2.0 copy-done.15
  130.1 4.6 %collective-permute-start.1 = (bf16[16,32,1536]{2,1,0:T(8,128)(2,1)}, bf16[16,32,1536]{2,1,0:T(8,128)(2,1)}, u32[]{:S(2)}, u32[]{:S(2)}) collective-permute-start(bf16[16,32,1536]{2,1,0:T(8,128)(2,1)} %all-to-all-done.1), channel_id=1, source_target_pairs={{0,1},{1,0},{2,3},{3,2},{4,5},{5,4},{6,7},{7,6},{8,9},{9,8},{10,11... | collective-permute-start | bytes 4718600 | tf_op jit(solution)/shard_map/ppermute | solution.py:620
  134.7 1.9 collective-permute-start.2
  136.7 7.9 %all-to-all-start.2 = ((bf16[16,64,384]{2,1,0:T(8,128)(2,1)}), bf16[16,64,384]{2,1,0:T(8,128)(2,1)S(1)}, u32[]{:S(2)}, u32[]{:S(2)}) async-start(bf16[16,64,384]{2,1,0:T(8,128)(2,1)} %bitcast.8), calls=%async_computation.2 | async-start | bytes 1572864 | tf_op jit(solution)/shard_map/all_to_all | solution.py:615
  145.9 1.5 copy-done.13
  147.3 2.2 %copy-done.16 = bf16[2,4,512,512]{3,2,1,0:T(8,128)(2,1)S(1)} copy-done((bf16[2,4,512,512]{3,2,1,0:T(8,128)(2,1)S(1)}, bf16[2,4,512,512]{3,2,1,0:T(8,128)(2,1)}, u32[]{:S(2)}) %copy-start.16) | copy-done | bytes 4194328
  149.5 1.7 copy-done.18
  152.6 9.8 %backward.1 = (f32[768,128]{1,0:T(8,128)S(1)}, bf16[768,128]{1,0:T(8,128)(2,1)S(1)}, f32[384,128]{1,0:T(8,128)S(1)}) custom-call(s32[1]{0:T(128)} %bitcast.core_ref, f32[8]{0:T(128)S(1)} %copy-done.14, bf16[2,4,512,512]{3,2,1,0:T(8,128)(2,1)S(1)} %copy-done.16, bf16[2,1152,512]{2,1,0:T(8,128)(2,1)S(1)} %copy-done.18, ...), custom_call_target="tpu_custom_call" | custom-call | flops 8589934592 | bytes 16777216 | tf_op jit(solution)/shard_map/backward/pallas_call | solution.py:490
  162.3 2.1 %collective-permute-start.3 = (bf16[768,128]{1,0:T(8,128)(2,1)S(1)}, bf16[768,128]{1,0:T(8,128)(2,1)S(1)}, u32[]{:S(2)}, u32[]{:S(2)}) collective-permute-start(bf16[768,128]{1,0:T(8,128)(2,1)S(1)} %get-tuple-element.36), channel_id=1, source_target_pairs={{0,1},{1,0},{2,3},{3,2},{4,5},{5,4},{6,7},{7,6},{8,9},{9,8},{10,11... | collective-permute-start | bytes 589832 | tf_op jit(solution)/shard_map/ppermute | solution.py:620
  167.2 19.0 %all_to_all.25.part_ref = bf16[32,48,128]{2,1,0:T(8,128)(2,1)S(1)} all-to-all(bf16[32,48,128]{2,1,0:T(8,128)(2,1)S(1)} %bitcast.26), channel_id=1, replica_groups=mesh['dp'=32,'seq'=16] {'dp'}, dimensions={0} | all-to-all | bytes 786432 | tf_op jit(solution)/shard_map/all_to_all | solution.py:615
  187.0 6.6 %all-to-all-start.4 = ((bf16[16,48,128]{2,1,0:T(8,128)(2,1)}), bf16[16,48,128]{2,1,0:T(8,128)(2,1)S(1)}, u32[]{:S(2)}, u32[]{:S(2)}) async-start(bf16[16,48,128]{2,1,0:T(8,128)(2,1)} %add_shards.1), calls=%async_computation.4 | async-start | bytes 393216 | tf_op jit(solution)/shard_map/all_to_all | solution.py:615
  195.3 3.1 %finish.1 = bf16[256,1536]{1,0:T(8,128)(2,1)} custom-call(s32[1]{0:T(128)} %bitcast.core_ref, s32[16]{0:T(128)S(1)} %copy-done.7, s32[16]{0:T(128)S(1)} %copy-done.9, bf16[16,64,384]{2,1,0:T(8,128)(2,1)S(1)} %all-to-all-done.2.context_ref, bf16[256,1536]{1,0:T(8,128)(2,1)S(1)} %bitcast.19, bf16[768,384]{1,0:T(8,128)(2,1)S(1)} %bitcast.21, ...), custom_call_target="tpu_custom_call" | custom-call | flops 805306368 | bytes 6291456 | tf_op jit(solution)/shard_map/finish/pallas_call | solution.py:554
  198.3 5.6 %all-to-all-done.4.part_ref = bf16[16,48,128]{2,1,0:T(8,128)(2,1)S(1)} async-done(((bf16[16,48,128]{2,1,0:T(8,128)(2,1)}), bf16[16,48,128]{2,1,0:T(8,128)(2,1)S(1)}, u32[]{:S(2)}, u32[]{:S(2)}) %all-to-all-start.4) | async-done | bytes 196640 | tf_op jit(solution)/shard_map/all_to_all | solution.py:615
  (50 shorter events, 17.2 us)
Async XLA Ops:
  7.2 99.2 %all-gather.2.cloned.1.call-start = ((), (), s32[]{:S(2)}) async-start(), calls=%async_computation.5 | async-start | bytes 5677056 | tf_op jit(solution)/shard_map/all_gather | solution.py:640
  15.7 12.0 %copy-start.5 = (bf16[16,16,1536]{2,1,0:T(8,128)(2,1)S(1)}, bf16[16,16,1536]{2,1,0:T(8,128)(2,1)}, u32[]{:S(2)}) copy-start(bf16[16,16,1536]{2,1,0:T(8,128)(2,1)} %param.21) | copy-start | bytes 2359300
  15.7 12.0 %copy-start.7 = (s32[16]{0:T(128)S(1)}, s32[16]{0:T(128)}, u32[]{:S(2)}) copy-start(s32[16]{0:T(128)} %owner_ref.5) | copy-start | bytes 196
  15.7 12.0 %copy-start.9 = (s32[16]{0:T(128)S(1)}, s32[16]{0:T(128)}, u32[]{:S(2)}) copy-start(s32[16]{0:T(128)} %live_ref.5) | copy-start | bytes 196
  15.7 53.0 %all-to-all-start = ((bf16[16,32,1664]{2,1,0:T(8,128)(2,1)}), bf16[16,32,1664]{2,1,0:T(8,128)(2,1)S(1)}, u32[]{:S(2)}, u32[]{:S(2)}) async-start(bf16[16,32,1664]{2,1,0:T(8,128)(2,1)} %pack.1), calls=%async_computation | async-start | bytes 3407872 | tf_op jit(solution)/shard_map/all_to_all | solution.py:615
  30.1 76.4 %copy-start.14 = (f32[8]{0:T(128)S(1)}, f32[8]{0:T(128)}, u32[]{:S(2)}) copy-start(f32[8]{0:T(128)} %soft_ref.3) | copy-start | bytes 100
  68.7 61.4 %all-to-all-start.1 = ((bf16[16,32,1536]{2,1,0:T(8,128)(2,1)}), bf16[16,32,1536]{2,1,0:T(8,128)(2,1)}, u32[]{:S(2)}, u32[]{:S(2)}) async-start(bf16[16,32,1536]{2,1,0:T(8,128)(2,1)} %pack_masked.1), calls=%async_computation.1 | async-start | bytes 3145728 | tf_op jit(solution)/shard_map/all_to_all | solution.py:615
  73.2 5.5 %collective-permute-start = (bf16[16,32,1664]{2,1,0:T(8,128)(2,1)S(1)}, bf16[16,32,1664]{2,1,0:T(8,128)(2,1)S(1)}, u32[]{:S(2)}, u32[]{:S(2)}) collective-permute-start(bf16[16,32,1664]{2,1,0:T(8,128)(2,1)S(1)} %all-to-all-done), channel_id=1, source_target_pairs={{0,1},{1,0},{2,3},{3,2},{4,5},{5,4},{6,7},{7,6},{8,9},{9,8},{10,11... | collective-permute-start | bytes 5111816 | tf_op jit(solution)/shard_map/ppermute | solution.py:620
  78.6 1.2 copy-start.11
  106.4 1.5 copy-start.12
  125.5 2.0 copy-start.15
  127.5 1.4 copy-start.17
  130.1 14.5 %collective-permute-start.1 = (bf16[16,32,1536]{2,1,0:T(8,128)(2,1)}, bf16[16,32,1536]{2,1,0:T(8,128)(2,1)}, u32[]{:S(2)}, u32[]{:S(2)}) collective-permute-start(bf16[16,32,1536]{2,1,0:T(8,128)(2,1)} %all-to-all-done.1), channel_id=1, source_target_pairs={{0,1},{1,0},{2,3},{3,2},{4,5},{5,4},{6,7},{7,6},{8,9},{9,8},{10,11... | collective-permute-start | bytes 4718600 | tf_op jit(solution)/shard_map/ppermute | solution.py:620
  134.7 9.8 %collective-permute-start.2 = (bf16[1536,384]{1,0:T(8,128)(2,1)}, bf16[1536,384]{1,0:T(8,128)(2,1)}, u32[]{:S(2)}, u32[]{:S(2)}) collective-permute-start(bf16[1536,384]{1,0:T(8,128)(2,1)} %copy-done.2), channel_id=1, source_target_pairs={{0,1},{1,0},{2,3},{3,2},{4,5},{5,4},{6,7},{7,6},{8,9},{9,8},{10,11... | collective-permute-start | bytes 3538952 | tf_op jit(solution)/shard_map/ppermute | solution.py:620
  136.7 30.6 %all-to-all-start.2 = ((bf16[16,64,384]{2,1,0:T(8,128)(2,1)}), bf16[16,64,384]{2,1,0:T(8,128)(2,1)S(1)}, u32[]{:S(2)}, u32[]{:S(2)}) async-start(bf16[16,64,384]{2,1,0:T(8,128)(2,1)} %bitcast.8), calls=%async_computation.2 | async-start | bytes 1572864 | tf_op jit(solution)/shard_map/all_to_all | solution.py:615
  144.6 1.3 copy-start.3
  145.9 1.5 copy-start.13
  147.3 2.2 %copy-start.16 = (bf16[2,4,512,512]{3,2,1,0:T(8,128)(2,1)S(1)}, bf16[2,4,512,512]{3,2,1,0:T(8,128)(2,1)}, u32[]{:S(2)}) copy-start(bf16[2,4,512,512]{3,2,1,0:T(8,128)(2,1)} %copy-done.15) | copy-start | bytes 12582916
  149.5 1.7 copy-start.18
  151.2 1.4 copy-start.20
  162.3 31.3 %copy-start.4 = (bf16[1536,384]{1,0:T(8,128)(2,1)S(1)}, bf16[1536,384]{1,0:T(8,128)(2,1)}, u32[]{:S(2)}) copy-start(bf16[1536,384]{1,0:T(8,128)(2,1)} %copy-done.2) | copy-start | bytes 3538948
  162.3 3.5 %collective-permute-start.3 = (bf16[768,128]{1,0:T(8,128)(2,1)S(1)}, bf16[768,128]{1,0:T(8,128)(2,1)S(1)}, u32[]{:S(2)}, u32[]{:S(2)}) collective-permute-start(bf16[768,128]{1,0:T(8,128)(2,1)S(1)} %get-tuple-element.36), channel_id=1, source_target_pairs={{0,1},{1,0},{2,3},{3,2},{4,5},{5,4},{6,7},{7,6},{8,9},{9,8},{10,11... | collective-permute-start | bytes 589832 | tf_op jit(solution)/shard_map/ppermute | solution.py:620
  187.0 17.0 %all-to-all-start.4 = ((bf16[16,48,128]{2,1,0:T(8,128)(2,1)}), bf16[16,48,128]{2,1,0:T(8,128)(2,1)S(1)}, u32[]{:S(2)}, u32[]{:S(2)}) async-start(bf16[16,48,128]{2,1,0:T(8,128)(2,1)} %add_shards.1), calls=%async_computation.4 | async-start | bytes 393216 | tf_op jit(solution)/shard_map/all_to_all | solution.py:615
  193.8 1.5 copy-start.1
  (6 other events, 5.3 us)
Sparse Core Ops, SparseCore 0:
  11.7 94.6 all-gather.1
